TPU v7x, 128 devices: a whole 4x4x4 slice. The times are simulated.
128 devices in a mesh: samp: 2 (over y_lo), vox: 8 (over y_hi, z), chan: 8 (over x, core).
Axes of the slice: x: 4, y: 4 (y_hi: 2, y_lo: 2; y = y_hi * 2 + y_lo), z: 4, core: 2. Of those that a mesh axis runs over, the one named last changes fastest.
Arguments:
- activations: bfloat16 [2, 32, 16, 32, 256], P('samp', 'vox', 'chan'), may hold values from -6 to 6
- out_grad: bfloat16 [2, 32, 16, 32, 512], P('samp', 'vox', None, None, 'chan'), may hold values from -6 to 6
- weight: bfloat16 [27, 256, 512], replicated, may hold values from -0.0546875 to 0.0546875
Outputs:
- data_grad: float32 [2, 32, 16, 32, 256], P('samp', 'vox', None, None, 'chan')
- weight_grad: float32 [27, 256, 512], P(None, 'chan')
All inputs are finite; a program needn't handle non-finite values.
Results may differ from a plain program's by a relative error of at most 0.0003.
Values may be sent and summed in bfloat16 or wider, within the bound.
No kernel may reach another device: no remote copies, remote signals or barrier semaphores. Data moves between devices by JAX's collectives and lax.ppermute only.
A program may use at most 192 MiB of HBM per device.

v0:
```python
import jax
import jax.numpy as jnp
from jax import lax
from jax.sharding import PartitionSpec as P

OFFSETS = [(a, b, c) for a in (-1, 0, 1) for b in (-1, 0, 1) for c in (-1, 0, 1)]


def with_halo(cells, sides, width):
    for axis, dim in sides:
        count = lax.axis_size(axis)
        ends = count - 1
        head = lax.slice_in_dim(cells, 0, width, axis=dim)
        tail = lax.slice_in_dim(cells, cells.shape[dim] - width, cells.shape[dim], axis=dim)
        cells = jnp.concatenate(
            [
                lax.ppermute(tail, axis, [(i, (i + 1) % count) for i in range(ends)]),
                cells,
                lax.ppermute(head, axis, [((i + 1) % count, i) for i in range(ends)]),
            ],
            axis=dim,
        )
    return cells


def pad_sides(block):
    return jnp.pad(block, ((0, 0), (0, 0), (1, 1), (1, 1), (0, 0)))


def window(padded, a, b, c, slab_depth, grid_rows, grid_cols):
    return padded[
        :, 1 + a : 1 + a + slab_depth, 1 + b : 1 + b + grid_rows, 1 + c : 1 + c + grid_cols
    ]


def on_device(activations, out_grad, weight):
    own_cells = (
        activations.shape[0] * activations.shape[1] * activations.shape[2] * activations.shape[3]
    )
    factor = (own_cells * lax.axis_size("samp") * lax.axis_size("vox") * lax.axis_size("chan")) ** (
        -0.5
    )
    grid_x = lax.all_to_all(activations, "chan", split_axis=4, concat_axis=2, tiled=True)
    rim_x = with_halo(grid_x, (("vox", 1),), 1)
    rim_g = with_halo(out_grad, (("vox", 1),), 1)
    samples, slab_depth, grid_rows, grid_cols, cin_panel = grid_x.shape
    cell_count = samples * slab_depth * grid_rows * grid_cols
    dims = (slab_depth, grid_rows, grid_cols)
    column = lax.axis_index("chan")
    w_local = lax.dynamic_slice_in_dim(weight, column * cin_panel, cin_panel, 1)
    padded_x = pad_sides(rim_x)
    panel = lax.all_gather(rim_g, "chan", axis=4, tiled=True)
    dx_part = jnp.zeros((cell_count, cin_panel), jnp.float32)
    piece_width = panel.shape[4]
    padded_g = pad_sides(panel)
    inner_g = panel[:, 1 : 1 + slab_depth].reshape(cell_count, piece_width)
    blocks = []
    for k, (accumulate_a, accumulate_b, accumulate_c) in enumerate(OFFSETS):
        shifted = window(padded_x, accumulate_a, accumulate_b, accumulate_c, *dims).reshape(
            cell_count, cin_panel
        )
        blocks.append(
            lax.dot_general(
                shifted, inner_g, (((0,), (0,)), ((), ())), preferred_element_type=jnp.float32
            )
        )
        moved_g = window(padded_g, -accumulate_a, -accumulate_b, -accumulate_c, *dims).reshape(
            cell_count, piece_width
        )
        dx_part = dx_part + lax.dot_general(
            moved_g, w_local[k], (((1,), (1,)), ((), ())), preferred_element_type=jnp.float32
        )
    dw_part = jnp.stack(blocks)
    dw_part, dx_part = (dw_part, dx_part)
    weight_grad = lax.psum(dw_part, ("samp", "vox")) * factor
    data_grad = dx_part.reshape(grid_x.shape)
    return (data_grad, weight_grad)


def solution(mesh):
    placed = (P("samp", "vox", "chan", None, None), P("samp", "vox", None, None, "chan"), P())
    return jax.shard_map(
        on_device,
        mesh=mesh,
        in_specs=placed,
        out_specs=(P("samp", "vox", None, None, "chan"), P(None, "chan", None)),
        check_vma=False,
    )
```

profile of v0, /device:TPU:0, one launch (start us, length us, event | category | flops | bytes accessed | tf_op | source)
XLA Modules:
  0.0 272.2 jit_solution(9750849623722784430)
XLA Ops:
  7.2 2.6 copy.24
  11.2 4.7 %collective-permute-start = (bf16[1,1,16,32,64]{3,2,1,0,4:T(8,128)(2,1)S(1)}, bf16[1,1,16,32,64]{3,2,1,0,4:T(8,128)(2,1)S(1)}, u32[]{:S(2)}, u32[]{:S(2)}) collective-permute-start(bf16[1,1,16,32,64]{3,2,1,0,4:T(8,128)(2,1)S(1)} %get-tuple-element.37), channel_id=1, source_target_pairs={{0,8},{8,16},{16,24},{24,32},{32,40},{40,48},{48,56},{1,9},{9,17},... | collective-permute-start | bytes 196616 | tf_op jit(solution)/shard_map/ppermute | solution.py:17
  15.9 4.2 %collective-permute-done.1 = bf16[1,1,16,32,64]{3,2,1,0,4:T(8,128)(2,1)S(1)} collective-permute-done((bf16[1,1,16,32,64]{3,2,1,0,4:T(8,128)(2,1)S(1)}, bf16[1,1,16,32,64]{3,2,1,0,4:T(8,128)(2,1)S(1)}, u32[]{:S(2)}, u32[]{:S(2)}) %collective-permute-start.1) | collective-permute-done | bytes 65568 | tf_op jit(solution)/shard_map/ppermute | solution.py:19
  23.8 10.2 %all_to_all.18 = bf16[8,2,4096]{2,1,0:T(2,128)(2,1)S(1)} all-to-all(bf16[8,2,4096]{2,1,0:T(2,128)(2,1)S(1)} %reshape.310), channel_id=1, replica_groups=mesh['samp'=2,'vox'=8,'chan'=8] {'chan'}, dimensions={0} | all-to-all | bytes 262144 | tf_op jit(solution)/shard_map/all_to_all | solution.py:43
  35.7 5.0 %collective-permute-start.2 = (bf16[1,1,16,32,32]{3,4,2,1,0:T(8,128)(2,1)S(1)}, bf16[1,1,16,32,32]{3,4,2,1,0:T(8,128)(2,1)S(1)}, u32[]{:S(2)}, u32[]{:S(2)}) collective-permute-start(bf16[1,1,16,32,32]{3,4,2,1,0:T(8,128)(2,1)S(1)} %get-tuple-element.39), channel_id=1, source_target_pairs={{0,8},{8,16},{16,24},{24,32},{32,40},{40,48},{48,56},{1,9},{9,17},... | collective-permute-start | bytes 98312 | tf_op jit(solution)/shard_map/ppermute | solution.py:17
  44.7 53.0 %all-gather.2.cloned.1.call-done = bf16[1,6,16,32,512]{3,2,1,0,4:T(8,128)(2,1)} async-done(((bf16[1,6,16,32,64]{3,2,1,0,4:T(8,128)(2,1)}), bf16[1,6,16,32,512]{3,2,1,0,4:T(8,128)(2,1)}) %all-gather.2.cloned.1.call-update) | async-done | bytes 3145744 | tf_op jit(solution)/shard_map/all_gather | solution.py:52
  97.7 12.2 %copy.27 = bf16[1,6,16,32,512]{4,3,2,1,0:T(8,128)(2,1)S(1)} copy(bf16[1,6,16,32,512]{3,2,1,0,4:T(8,128)(2,1)} %all-gather.2.cloned.1.call-done) | data formatting | bytes 6291456 | tf_op jit(solution)/shard_map/all_gather | solution.py:52
  109.9 6.8 %pad_slice_fusion.1 = (bf16[1,4,16,32,512]{4,3,2,1,0:T(8,128)(2,1)}, bf16[1,4,16,32,512]{4,3,2,1,0:T(8,128)(2,1)}, bf16[1,4,16,32,512]{4,3,2,1,0:T(8,128)(2,1)},...) fusion(bf16[1,6,16,32,512]{4,3,2,1,0:T(8,128)(2,1)S(1)} %copy.27), kind=kLoop, calls=%fused_computation.1 | loop fusion | bytes 26214400 | tf_op jit(solution)/shard_map/slice | solution.py:31
  116.7 14.7 %pad_slice_fusion = (bf16[1,4,16,32,512]{4,3,2,1,0:T(8,128)(2,1)}, bf16[1,4,16,32,512]{4,3,2,1,0:T(8,128)(2,1)}, bf16[1,4,16,32,512]{4,3,2,1,0:T(8,128)(2,1)}, b...) fusion(bf16[1,6,16,32,512]{4,3,2,1,0:T(8,128)(2,1)S(1)} %copy.27), kind=kLoop, calls=%fused_computation | loop fusion | bytes 42991616 | tf_op jit(solution)/shard_map/slice | solution.py:31
  170.6 1.8 fusion.216
  172.4 2.5 fusion.228
  176.5 1.6 convolution_add_fusion.24
  178.2 1.6 convolution_add_fusion.23
  179.8 1.6 convolution_add_fusion.22
  181.5 1.6 convolution_add_fusion.21
  183.1 1.6 convolution_add_fusion.20
  184.8 1.6 convolution_add_fusion.19
  186.4 1.6 convolution_add_fusion.18
  188.1 1.6 convolution_add_fusion.17
  189.7 1.6 convolution_add_fusion.16
  191.4 1.6 convolution_add_fusion.15
  193.0 1.6 convolution_add_fusion.14
  194.7 1.6 convolution_add_fusion.13
  196.3 1.6 convolution_add_fusion.12
  198.0 1.6 convolution_add_fusion.11
  199.6 1.6 convolution_add_fusion.10
  201.3 1.6 convolution_add_fusion.9
  202.9 1.6 convolution_add_fusion.8
  204.6 1.6 convolution_add_fusion.7
  206.2 1.6 convolution_add_fusion.6
  218.8 43.6 %all-reduce.4.cloned.1.call-done = f32[27,32,512]{2,1,0:T(8,128)} async-done(((f32[27,32,512]{2,1,0:T(8,128)}), f32[27,32,512]{2,1,0:T(8,128)}) %all-reduce.4.cloned.1.call-update) | async-done | bytes 1769488 | tf_op jit(solution)/shard_map/psum | solution.py:75
  262.4 3.0 %broadcast_multiply_fusion = f32[27,32,512]{2,1,0:T(8,128)} fusion(f32[27,32,512]{2,1,0:T(8,128)} %all-reduce.4.cloned.1.call-done), kind=kLoop, calls=%fused_computation.171 | loop fusion | flops 442368 | bytes 3538944 | tf_op jit(solution)/shard_map/mul | solution.py:75
  (111 shorter events, 62.6 us)
Async XLA Ops:
  7.2 90.5 %all-gather.2.cloned.1.call-start = ((), (), s32[]{:S(2)}) async-start(), calls=%async_computation.1 | async-start | bytes 14155776 | tf_op jit(solution)/shard_map/all_gather | solution.py:52
  9.9 10.2 %collective-permute-start.1 = (bf16[1,1,16,32,64]{3,2,1,0,4:T(8,128)(2,1)S(1)}, bf16[1,1,16,32,64]{3,2,1,0,4:T(8,128)(2,1)S(1)}, u32[]{:S(2)}, u32[]{:S(2)}) collective-permute-start(bf16[1,1,16,32,64]{3,2,1,0,4:T(8,128)(2,1)S(1)} %get-tuple-element.38), channel_id=1, source_target_pairs={{8,0},{16,8},{24,16},{32,24},{40,32},{48,40},{56,48},{9,1},{17,9},... | collective-permute-start | bytes 196616 | tf_op jit(solution)/shard_map/ppermute | solution.py:19
  11.2 11.8 %copy-start.29 = (bf16[1,4,2,32,256]{4,3,2,1,0:T(8,128)(2,1)S(1)}, bf16[1,4,2,32,256]{4,3,2,1,0:T(8,128)(2,1)}, u32[]{:S(2)}) copy-start(bf16[1,4,2,32,256]{4,3,2,1,0:T(8,128)(2,1)} %param.3) | copy-start | bytes 393220
  11.2 10.2 %collective-permute-start = (bf16[1,1,16,32,64]{3,2,1,0,4:T(8,128)(2,1)S(1)}, bf16[1,1,16,32,64]{3,2,1,0,4:T(8,128)(2,1)S(1)}, u32[]{:S(2)}, u32[]{:S(2)}) collective-permute-start(bf16[1,1,16,32,64]{3,2,1,0,4:T(8,128)(2,1)S(1)} %get-tuple-element.37), channel_id=1, source_target_pairs={{0,8},{8,16},{16,24},{24,32},{32,40},{40,48},{48,56},{1,9},{9,17},... | collective-permute-start | bytes 196616 | tf_op jit(solution)/shard_map/ppermute | solution.py:17
  22.9 239.5 %all-reduce.4.cloned.1.call-start = ((), (), s32[]{:S(2)}) async-start(), calls=%async_computation.2 | async-start | bytes 3538944 | tf_op jit(solution)/shard_map/psum | solution.py:75
  34.4 10.3 %copy-start.26 = (bf16[1,4,2,32,8,32]{3,5,2,4,1,0:T(8,128)(2,1)}, bf16[1,4,2,32,8,32]{3,5,2,4,1,0:T(8,128)(2,1)S(1)}, u32[]{:S(2)}) copy-start(bf16[1,4,2,32,8,32]{3,5,2,4,1,0:T(8,128)(2,1)S(1)} %copy.32) | copy-start | bytes 393220
  34.4 7.7 %collective-permute-start.3 = (bf16[1,1,16,32,32]{3,4,2,1,0:T(8,128)(2,1)S(1)}, bf16[1,1,16,32,32]{3,4,2,1,0:T(8,128)(2,1)S(1)}, u32[]{:S(2)}, u32[]{:S(2)}) collective-permute-start(bf16[1,1,16,32,32]{3,4,2,1,0:T(8,128)(2,1)S(1)} %get-tuple-element.40), channel_id=1, source_target_pairs={{8,0},{16,8},{24,16},{32,24},{40,32},{48,40},{56,48},{9,1},{17,9},... | collective-permute-start | bytes 98312 | tf_op jit(solution)/shard_map/ppermute | solution.py:19
  35.7 7.6 %collective-permute-start.2 = (bf16[1,1,16,32,32]{3,4,2,1,0:T(8,128)(2,1)S(1)}, bf16[1,1,16,32,32]{3,4,2,1,0:T(8,128)(2,1)S(1)}, u32[]{:S(2)}, u32[]{:S(2)}) collective-permute-start(bf16[1,1,16,32,32]{3,4,2,1,0:T(8,128)(2,1)S(1)} %get-tuple-element.39), channel_id=1, source_target_pairs={{0,8},{8,16},{16,24},{24,32},{32,40},{40,48},{48,56},{1,9},{9,17},... | collective-permute-start | bytes 98312 | tf_op jit(solution)/shard_map/ppermute | solution.py:17
  116.7 14.7 %copy-start.28 = (bf16[1,6,18,34,32]{3,4,2,1,0:T(8,128)(2,1)S(1)}, bf16[1,6,18,34,32]{3,4,2,1,0:T(8,128)(2,1)}, u32[]{:S(2)}) copy-start(bf16[1,6,18,34,32]{3,4,2,1,0:T(8,128)(2,1)} %select_maximum_fusion) | copy-start | bytes 705028
  172.4 4.1 %copy-start.24 = (bf16[1,4,16,32,512]{4,3,2,1,0:T(8,128)(2,1)S(1)}, bf16[1,4,16,32,512]{4,3,2,1,0:T(8,128)(2,1)}, u32[]{:S(2)}) copy-start(bf16[1,4,16,32,512]{4,3,2,1,0:T(8,128)(2,1)} %get-tuple-element.12) | copy-start | bytes 6291460
  176.5 3.3 %copy-start.6 = (bf16[1,4,16,32,512]{4,3,2,1,0:T(8,128)(2,1)S(1)}, bf16[1,4,16,32,512]{4,3,2,1,0:T(8,128)(2,1)}, u32[]{:S(2)}) copy-start(bf16[1,4,16,32,512]{4,3,2,1,0:T(8,128)(2,1)} %get-tuple-element.35) | copy-start | bytes 6291460
  178.2 3.3 %copy-start.22 = (bf16[1,4,16,32,512]{4,3,2,1,0:T(8,128)(2,1)S(1)}, bf16[1,4,16,32,512]{4,3,2,1,0:T(8,128)(2,1)}, u32[]{:S(2)}) copy-start(bf16[1,4,16,32,512]{4,3,2,1,0:T(8,128)(2,1)} %get-tuple-element.14) | copy-start | bytes 6291460
  179.8 3.3 %copy-start.21 = (bf16[1,4,16,32,512]{4,3,2,1,0:T(8,128)(2,1)S(1)}, bf16[1,4,16,32,512]{4,3,2,1,0:T(8,128)(2,1)}, u32[]{:S(2)}) copy-start(bf16[1,4,16,32,512]{4,3,2,1,0:T(8,128)(2,1)} %get-tuple-element.15) | copy-start | bytes 6291460
  181.5 3.3 %copy-start.20 = (bf16[1,4,16,32,512]{4,3,2,1,0:T(8,128)(2,1)S(1)}, bf16[1,4,16,32,512]{4,3,2,1,0:T(8,128)(2,1)}, u32[]{:S(2)}) copy-start(bf16[1,4,16,32,512]{4,3,2,1,0:T(8,128)(2,1)} %get-tuple-element.16) | copy-start | bytes 6291460
  183.1 3.3 %copy-start.19 = (bf16[1,4,16,32,512]{4,3,2,1,0:T(8,128)(2,1)S(1)}, bf16[1,4,16,32,512]{4,3,2,1,0:T(8,128)(2,1)}, u32[]{:S(2)}) copy-start(bf16[1,4,16,32,512]{4,3,2,1,0:T(8,128)(2,1)} %get-tuple-element.17) | copy-start | bytes 6291460
  184.8 3.3 %copy-start.18 = (bf16[1,4,16,32,512]{4,3,2,1,0:T(8,128)(2,1)S(1)}, bf16[1,4,16,32,512]{4,3,2,1,0:T(8,128)(2,1)}, u32[]{:S(2)}) copy-start(bf16[1,4,16,32,512]{4,3,2,1,0:T(8,128)(2,1)} %get-tuple-element.18) | copy-start | bytes 6291460
  186.4 3.3 %copy-start.17 = (bf16[1,4,16,32,512]{4,3,2,1,0:T(8,128)(2,1)S(1)}, bf16[1,4,16,32,512]{4,3,2,1,0:T(8,128)(2,1)}, u32[]{:S(2)}) copy-start(bf16[1,4,16,32,512]{4,3,2,1,0:T(8,128)(2,1)} %get-tuple-element.19) | copy-start | bytes 6291460
  188.1 3.3 %copy-start.16 = (bf16[1,4,16,32,512]{4,3,2,1,0:T(8,128)(2,1)S(1)}, bf16[1,4,16,32,512]{4,3,2,1,0:T(8,128)(2,1)}, u32[]{:S(2)}) copy-start(bf16[1,4,16,32,512]{4,3,2,1,0:T(8,128)(2,1)} %get-tuple-element.20) | copy-start | bytes 6291460
  189.7 3.3 %copy-start.15 = (bf16[1,4,16,32,512]{4,3,2,1,0:T(8,128)(2,1)S(1)}, bf16[1,4,16,32,512]{4,3,2,1,0:T(8,128)(2,1)}, u32[]{:S(2)}) copy-start(bf16[1,4,16,32,512]{4,3,2,1,0:T(8,128)(2,1)} %get-tuple-element.21) | copy-start | bytes 6291460
  191.4 3.3 %copy-start.5 = (bf16[1,4,16,32,512]{4,3,2,1,0:T(8,128)(2,1)S(1)}, bf16[1,4,16,32,512]{4,3,2,1,0:T(8,128)(2,1)}, u32[]{:S(2)}) copy-start(bf16[1,4,16,32,512]{4,3,2,1,0:T(8,128)(2,1)} %get-tuple-element.34) | copy-start | bytes 6291460
  193.0 3.3 %copy-start.14 = (bf16[1,4,16,32,512]{4,3,2,1,0:T(8,128)(2,1)S(1)}, bf16[1,4,16,32,512]{4,3,2,1,0:T(8,128)(2,1)}, u32[]{:S(2)}) copy-start(bf16[1,4,16,32,512]{4,3,2,1,0:T(8,128)(2,1)} %get-tuple-element.22) | copy-start | bytes 6291460
  194.7 3.3 %copy-start.13 = (bf16[1,4,16,32,512]{4,3,2,1,0:T(8,128)(2,1)S(1)}, bf16[1,4,16,32,512]{4,3,2,1,0:T(8,128)(2,1)}, u32[]{:S(2)}) copy-start(bf16[1,4,16,32,512]{4,3,2,1,0:T(8,128)(2,1)} %get-tuple-element.23) | copy-start | bytes 6291460
  196.3 3.3 %copy-start.12 = (bf16[1,4,16,32,512]{4,3,2,1,0:T(8,128)(2,1)S(1)}, bf16[1,4,16,32,512]{4,3,2,1,0:T(8,128)(2,1)}, u32[]{:S(2)}) copy-start(bf16[1,4,16,32,512]{4,3,2,1,0:T(8,128)(2,1)} %get-tuple-element.24) | copy-start | bytes 6291460
  198.0 3.3 %copy-start.11 = (bf16[1,4,16,32,512]{4,3,2,1,0:T(8,128)(2,1)S(1)}, bf16[1,4,16,32,512]{4,3,2,1,0:T(8,128)(2,1)}, u32[]{:S(2)}) copy-start(bf16[1,4,16,32,512]{4,3,2,1,0:T(8,128)(2,1)} %get-tuple-element.25) | copy-start | bytes 6291460
  199.6 3.3 %copy-start.10 = (bf16[1,4,16,32,512]{4,3,2,1,0:T(8,128)(2,1)S(1)}, bf16[1,4,16,32,512]{4,3,2,1,0:T(8,128)(2,1)}, u32[]{:S(2)}) copy-start(bf16[1,4,16,32,512]{4,3,2,1,0:T(8,128)(2,1)} %get-tuple-element.26) | copy-start | bytes 6291460
  201.3 3.3 %copy-start.9 = (bf16[1,4,16,32,512]{4,3,2,1,0:T(8,128)(2,1)S(1)}, bf16[1,4,16,32,512]{4,3,2,1,0:T(8,128)(2,1)}, u32[]{:S(2)}) copy-start(bf16[1,4,16,32,512]{4,3,2,1,0:T(8,128)(2,1)} %get-tuple-element.27) | copy-start | bytes 6291460
  202.9 3.3 %copy-start.8 = (bf16[1,4,16,32,512]{4,3,2,1,0:T(8,128)(2,1)S(1)}, bf16[1,4,16,32,512]{4,3,2,1,0:T(8,128)(2,1)}, u32[]{:S(2)}) copy-start(bf16[1,4,16,32,512]{4,3,2,1,0:T(8,128)(2,1)} %get-tuple-element.28) | copy-start | bytes 6291460
  204.6 3.3 %copy-start.4 = (bf16[1,4,16,32,512]{4,3,2,1,0:T(8,128)(2,1)S(1)}, bf16[1,4,16,32,512]{4,3,2,1,0:T(8,128)(2,1)}, u32[]{:S(2)}) copy-start(bf16[1,4,16,32,512]{4,3,2,1,0:T(8,128)(2,1)} %get-tuple-element.30) | copy-start | bytes 6291460
  206.2 3.3 %copy-start.3 = (bf16[1,4,16,32,512]{4,3,2,1,0:T(8,128)(2,1)S(1)}, bf16[1,4,16,32,512]{4,3,2,1,0:T(8,128)(2,1)}, u32[]{:S(2)}) copy-start(bf16[1,4,16,32,512]{4,3,2,1,0:T(8,128)(2,1)} %get-tuple-element.33) | copy-start | bytes 6291460
  207.9 3.3 %copy-start.2 = (bf16[1,4,16,32,512]{4,3,2,1,0:T(8,128)(2,1)S(1)}, bf16[1,4,16,32,512]{4,3,2,1,0:T(8,128)(2,1)}, u32[]{:S(2)}) copy-start(bf16[1,4,16,32,512]{4,3,2,1,0:T(8,128)(2,1)} %get-tuple-element.31) | copy-start | bytes 6291460
  209.5 3.3 %copy-start.1 = (bf16[1,4,16,32,512]{4,3,2,1,0:T(8,128)(2,1)S(1)}, bf16[1,4,16,32,512]{4,3,2,1,0:T(8,128)(2,1)}, u32[]{:S(2)}) copy-start(bf16[1,4,16,32,512]{4,3,2,1,0:T(8,128)(2,1)} %get-tuple-element.32) | copy-start | bytes 6291460
  211.2 3.3 %copy-start = (bf16[1,4,16,32,512]{4,3,2,1,0:T(8,128)(2,1)S(1)}, bf16[1,4,16,32,512]{4,3,2,1,0:T(8,128)(2,1)}, u32[]{:S(2)}) copy-start(bf16[1,4,16,32,512]{4,3,2,1,0:T(8,128)(2,1)} %get-tuple-element.29) | copy-start | bytes 6291460
  (4 other events, 10.4 us)
Sparse Core Ops, SparseCore 0:
  23.0 74.6 all-gather.1
  172.5 89.8 all-reduce.3
where the time goes:
time: 273 us; the launch traced here: 272 us
  waiting for transfers between devices  105 us (38%)
  matrix products  85.1 us (31%)
  local copies, waits for them, and re-layouts  39.3 us (14%)
  between operations  14.6 us (5%)
  starting transfers between devices  12.4 us (5%)
  blocking collectives  10.2 us (4%)
  other arithmetic  5.83 us (2%)
    all_gather x1, waiting for transfers between devices, on_device(): panel = lax.all_gather(rim_g, 'chan', axis=4, tiled=True)  53 us
    dot_general x27, matrix products, on_device(): lax.dot_general(moved_g, w_local[k], (((1,), (1,)), ((), ())), preferred_...  44.2 us
    psum x1, waiting for transfers between devices, on_device(): weight_grad = lax.psum(dw_part, ('samp', 'vox')) * factor  43.6 us
    dot_general x27, matrix products, on_device(): lax.dot_general(shifted, inner_g, (((0,), (0,)), ((), ())), preferred_ele...  40.9 us
    slice x2, local copies, waits for them, and re-layouts, window(): padded[:, 1 + a:1 + a + slab_depth, 1 + b:1 + b + grid_rows, 1 + c:1 + c...  21.5 us
    all_gather x1, local copies, waits for them, and re-layouts, on_device(): panel = lax.all_gather(rim_g, 'chan', axis=4, tiled=True)  12.2 us
    all_to_all x1, blocking collectives, on_device(): lax.all_to_all(activations, 'chan', split_axis=4, concat_axis=2, tiled=True)  10.2 us
    ppermute x2, starting transfers between devices, with_halo(): lax.ppermute(tail, axis, [(i, (i + 1) % count) for i in range(ends)])  9.72 us
  transfers between devices with their start and end apart: 6, of which 6 were waited for; matrix products, arithmetic and copies ran while one was open for 18% of the time, Pallas kernels for 0%

commit v1 on v0

v1 whole, which is shorter than its diff:
```python
import jax
import jax.numpy as jnp
from jax import lax
from jax.experimental import pallas as pl
from jax.experimental.pallas import tpu as pltpu
from jax.sharding import PartitionSpec as P

F32, BF16 = jnp.float32, jnp.bfloat16
STEPS, BIAS = 249.0, 125.0
VM = pl.BlockSpec(memory_space=pltpu.VMEM)
LIMIT = 48 * 1024 * 1024


def call(body, outs, n_in, scratch=(), flops=0, nbytes=1 << 20):
    return pl.pallas_call(
        body,
        out_shape=outs,
        in_specs=[VM] * n_in,
        out_specs=jax.tree.map(lambda _: VM, outs),
        scratch_shapes=list(scratch),
        compiler_params=pltpu.CompilerParams(vmem_limit_bytes=LIMIT),
        cost_estimate=pl.CostEstimate(flops=flops, bytes_accessed=nbytes, transcendentals=0),
    )


def encode(value, exponent):
    q = jnp.sqrt(jnp.abs(value) * jnp.exp2(-exponent)) * STEPS
    whole = jnp.floor(q)
    code = jnp.exp2(whole - BIAS) * (1.0 + (q - whole))
    return jnp.where(value < 0, -code, code).astype(BF16)


def decode(code, exponent):
    code = code.astype(F32)
    size = jnp.abs(code)
    whole = jnp.floor(jnp.log2(size))
    q = (whole + BIAS) + (size * jnp.exp2(-whole) - 1.0)
    square = q * q * (jnp.exp2(exponent) / (STEPS * STEPS))
    return jnp.where(code < 0, -square, square)


def top_exponent(value):
    most = jnp.max(jnp.max(jnp.abs(value), axis=0, keepdims=True), axis=1, keepdims=True)
    return jnp.ceil(jnp.log2(jnp.maximum(most, 1e-30)))


def pack_body(g_ref, x_ref, gs_ref, xs_ref):
    g = g_ref[...]
    for t in range(2):
        gs_ref[512 * t : 512 * (t + 1), :] = jnp.concatenate([g[2 * t], g[2 * t + 1]], axis=1)
    x = x_ref[...]
    for c in range(8):
        xs_ref[c] = jnp.concatenate([x[p, :, 32 * c : 32 * (c + 1)] for p in range(4)], axis=1)


def weight_body(at_ref, w_ref, out_ref):
    none = jnp.zeros((32, 128), BF16)
    for bc in range(9):
        for s in range(4):
            for j in range(4):
                lanes = slice(128 * j, 128 * (j + 1))
                low = w_ref[9 * s + bc, :, lanes] if s < 3 else none
                high = w_ref[9 * (s - 1) + bc, :, lanes] if s > 0 else none
                rows = slice(128 * bc + 32 * s, 128 * bc + 32 * (s + 1))
                out_ref[rows, 256 * j : 256 * j + 128] = jnp.concatenate([low[:, :64], high[:, :64]], axis=1)
                out_ref[rows, 256 * j + 128 : 256 * j + 256] = jnp.concatenate([low[:, 64:], high[:, 64:]], axis=1)


def weights(column, weight):
    return pl.pallas_call(
        weight_body,
        out_shape=jax.ShapeDtypeStruct((1152, 1024), BF16),
        grid_spec=pltpu.PrefetchScalarGridSpec(
            num_scalar_prefetch=1,
            grid=(1,),
            in_specs=[pl.BlockSpec((27, 32, 512), lambda i, at: (0, at[0], 0))],
            out_specs=pl.BlockSpec((1152, 1024), lambda i, at: (0, 0)),
        ),
        compiler_params=pltpu.CompilerParams(vmem_limit_bytes=LIMIT),
        cost_estimate=pl.CostEstimate(flops=0, bytes_accessed=1 << 22, transcendentals=0),
    )(column.reshape(1), weight)


def shifted_z(block, c):
    if c == 0:
        return block
    cells = block.astype(F32).reshape(16, 32, 128)
    edge = jnp.zeros((16, 1, 128), F32)
    moved = [cells[:, 1:], edge] if c > 0 else [edge, cells[:, :31]]
    return jnp.concatenate(moved, axis=1).reshape(512, 128).astype(block.dtype)


def patches_body(x_ref, left_ref, right_ref, out_ref):
    x = x_ref[...]
    pairs = (
        jnp.concatenate([left_ref[:, 96:], x[:, :96]], axis=1),
        jnp.concatenate([x[:, 32:], right_ref[:, :32]], axis=1),
    )
    edge = jnp.zeros((128, 32), BF16)
    for t, block in enumerate(pairs):
        lanes = slice(512 * t, 512 * (t + 1))
        for c in range(3):
            turned = shifted_z(block, c - 1).T
            out_ref[128 * c : 128 * (c + 1), lanes] = jnp.concatenate([edge, turned[:, :480]], axis=1)
            out_ref[128 * (3 + c) : 128 * (4 + c), lanes] = turned
            out_ref[128 * (6 + c) : 128 * (7 + c), lanes] = jnp.concatenate([turned[:, 32:], edge], axis=1)


def gather_panel(spot_ref, parts, panel_ref):
    for i, part in enumerate(parts):
        panel_ref[:, pl.ds(pl.multiple_of(spot_ref[i] * 128, 128), 128)] = part[...]


def kernel_grad_body(spot_ref, l_ref, *refs):
    parts, out_ref, panel_ref, prod_ref = refs[:8], refs[8], refs[9], refs[10]
    gather_panel(spot_ref, parts, panel_ref)
    lane = lax.broadcasted_iota(jnp.int32, (1, 1, 1, 128), 3) < 64
    for j in range(4):
        prod_ref[...] = jnp.dot(l_ref[...], panel_ref[:, 256 * j : 256 * (j + 1)], preferred_element_type=F32)
        even = prod_ref[:, :128].reshape(9, 4, 32, 128)
        odd = prod_ref[:, 128:].reshape(9, 4, 32, 128)
        straight = jnp.where(lane, even[:, 0:3], odd[:, 1:4])
        crossed = jnp.where(lane, odd[:, 0:3], even[:, 1:4])
        total = straight.reshape(864, 128) + pltpu.roll(crossed.reshape(864, 128), 64, 1)
        total = total * (32768.0**-0.5)
        exponent = top_exponent(total)
        code = encode(total, exponent).astype(F32).reshape(27, 4, 8, 128)
        for r in range(4):
            out_ref[4 * r + j, :216, :] = code[:, r].reshape(216, 128).astype(BF16)
            out_ref[4 * r + j, 216:224, :] = jnp.broadcast_to(exponent, (8, 128)).astype(BF16)


def shard_sum_body(in_ref, out_ref):
    total = jnp.zeros((216, 128), F32)
    for i in range(16):
        block = in_ref[i].astype(F32)
        total = total + decode(block[:216], block[216:217, :])
    exponent = top_exponent(total)
    code = jnp.concatenate([encode(total, exponent).astype(F32), jnp.broadcast_to(exponent, (8, 128))], axis=0).astype(BF16)
    for i in range(16):
        out_ref[i] = code


def kernel_out_body(in_ref, out_ref):
    for r in range(4):
        for j in range(4):
            block = in_ref[4 * r + j].astype(F32)
            value = decode(block[:216], block[216:217, :]).reshape(9, 3, 8, 128)
            for a in range(3):
                out_ref[9 * a : 9 * (a + 1), 8 * r : 8 * (r + 1), 128 * j : 128 * (j + 1)] = value[:, a]


def data_grad_body(spot_ref, w_ref, *refs):
    parts, own_ref, low_ref, high_ref, panel_ref, acc_ref = refs[:8], *refs[8:13]
    gather_panel(spot_ref, parts, panel_ref)
    acc_ref[...] = jnp.zeros_like(acc_ref)
    for first in range(0, 9, 2):
        taps = range(first, min(first + 2, 9))
        prod = lax.dot_general(
            panel_ref[...], w_ref[128 * first : 128 * (first + len(taps)), :],
            (((1,), (1,)), ((), ())), preferred_element_type=F32,
        )
        for i, bc in enumerate(taps):
            b, c = bc // 3, bc % 3
            for t in range(2):
                acc_ref[c, t, 32 * b : 32 * b + 512, :] += prod[512 * t : 512 * (t + 1), 128 * i : 128 * (i + 1)]
    sums = []
    for t in range(2):
        sums.append(
            shifted_z(acc_ref[0, t, 32:544, :], 1) + acc_ref[1, t, 32:544, :] + shifted_z(acc_ref[2, t, 32:544, :], -1)
        )
    lane = lax.broadcasted_iota(jnp.int32, (1, 128), 1)
    low, high = sums
    own_ref[...] = jnp.where(lane < 96, pltpu.roll(low, 96, 1), 0.0) + jnp.where(lane >= 32, pltpu.roll(high, 32, 1), 0.0)
    low_ref[...] = jnp.concatenate([low[128 * i : 128 * (i + 1), :32] for i in range(4)], axis=1)
    high_ref[...] = jnp.concatenate([high[128 * i : 128 * (i + 1), 96:] for i in range(4)], axis=1)


def data_out_body(own_ref, low_ref, high_ref, out_ref):
    for p in range(4):
        plane = own_ref[:, 32 * p : 32 * (p + 1)]
        if p in (0, 3):
            extra = low_ref if p == 0 else high_ref
            plane = plane + jnp.concatenate([extra[:, 32 * i : 32 * (i + 1)] for i in range(4)], axis=0)
        out_ref[p] = plane


def on_device(activations, out_grad, weight):
    column = lax.axis_index("chan")
    chip, core = column // 2, column % 2
    struct = jax.ShapeDtypeStruct

    packed_g, packed_x = call(
        pack_body, (struct((1024, 128), BF16), struct((8, 64, 128), BF16)), 2
    )(out_grad.reshape(4, 512, 64), activations.reshape(4, 64, 256))

    def hop(value, chips, cores):
        return lax.ppermute(
            value, "chan", [(i, ((i // 2 + chips) % 4) * 2 + (i % 2 ^ cores)) for i in range(8)]
        )

    mine = [packed_g] + [hop(packed_g, d, 0) for d in (1, 3, 2)]
    parts = mine + [hop(v, 0, 1) for v in mine]
    froms = [chip, (chip + 3) % 4, (chip + 1) % 4, (chip + 2) % 4]
    spots = jnp.stack([2 * f + core for f in froms] + [2 * f + 1 - core for f in froms]).astype(jnp.int32)

    cells = lax.all_to_all(packed_x, "chan", split_axis=0, concat_axis=0, tiled=True).reshape(512, 128)
    left = lax.ppermute(cells, "vox", [(i, i + 1) for i in range(7)])
    right = lax.ppermute(cells, "vox", [(i + 1, i) for i in range(7)])
    patches = call(patches_body, struct((1152, 1024), BF16), 3)(cells, left, right)

    smem = pl.BlockSpec(memory_space=pltpu.SMEM)

    def with_spots(body, outs, scratch, operand, flops):
        return pl.pallas_call(
            body,
            out_shape=outs,
            in_specs=[smem] + [VM] * 9,
            out_specs=jax.tree.map(lambda _: VM, outs),
            scratch_shapes=scratch,
            compiler_params=pltpu.CompilerParams(vmem_limit_bytes=LIMIT),
            cost_estimate=pl.CostEstimate(flops=flops, bytes_accessed=6 << 20, transcendentals=0),
        )(spots, operand, *parts)

    codes = with_spots(
        kernel_grad_body, struct((16, 224, 128), BF16),
        [pltpu.VMEM((1024, 1024), BF16), pltpu.VMEM((1152, 256), F32)], patches, 2 * 1152 * 1024 * 1024,
    )
    own, low, high = with_spots(
        data_grad_body, (struct((512, 128), F32), struct((128, 128), F32), struct((128, 128), F32)),
        [pltpu.VMEM((1024, 1024), BF16), pltpu.VMEM((3, 2, 576, 128), F32)], weights(column, weight), 2 * 1280 * 1024 * 1024,
    )
    swapped = lax.all_to_all(codes, ("samp", "vox"), split_axis=0, concat_axis=0, tiled=True)
    shards = call(shard_sum_body, struct((16, 224, 128), BF16), 1)(swapped)
    final = lax.all_to_all(shards, ("samp", "vox"), split_axis=0, concat_axis=0, tiled=True)
    weight_grad = call(kernel_out_body, struct((27, 32, 512), F32), 1)(final)

    to_high = lax.ppermute(low, "vox", [(i + 1, i) for i in range(7)])
    to_low = lax.ppermute(high, "vox", [(i, i + 1) for i in range(7)])
    data_grad = call(data_out_body, struct((4, 512, 32), F32), 3)(own, to_low, to_high)
    return data_grad.reshape(1, 4, 16, 32, 32), weight_grad


def solution(mesh):
    placed = (P("samp", "vox", "chan", None, None), P("samp", "vox", None, None, "chan"), P())
    return jax.shard_map(
        on_device,
        mesh=mesh,
        in_specs=placed,
        out_specs=(P("samp", "vox", None, None, "chan"), P(None, "chan", None)),
        check_vma=False,
    )
```

time: 273 us -> 93.3 us (0.34)
  the two profiles are of different devices: /device:TPU:0 before, /device:TPU:96 now
where the time goes in v1:
time: 93.3 us; the launch traced here: 92.9 us
  blocking collectives  28.8 us (31%)
  starting transfers between devices  24.6 us (26%)
  Pallas kernels  18.7 us (20%)
  waiting for transfers between devices  17.9 us (19%)
  local copies, waits for them, and re-layouts  2.02 us (2%)
    all_to_all x1, blocking collectives, on_device(): lax.all_to_all(codes, ('samp', 'vox'), split_axis=0, concat_axis=0, tiled...  16.5 us
    all_to_all x1, blocking collectives, on_device(): lax.all_to_all(packed_x, 'chan', split_axis=0, concat_axis=0, tiled=True)  12.3 us
    pallas_call x2, Pallas kernels, with_spots(): pl.pallas_call(body, out_shape=outs, in_specs=[smem] + [VM] * 9, out_spec...  9.96 us
    ppermute x1, waiting for transfers between devices, on_device(): right = lax.ppermute(cells, 'vox', [(i + 1, i) for i in range(7)])  8 us
    ppermute x1, waiting for transfers between devices, on_device(): to_high = lax.ppermute(low, 'vox', [(i + 1, i) for i in range(7)])  7.83 us
    ppermute x7, starting transfers between devices, hop(): lax.ppermute(value, 'chan', [(i, (i // 2 + chips) % 4 * 2 + (i % 2 ^ core...  6.2 us
    all_to_all x1, starting transfers between devices, on_device(): lax.all_to_all(shards, ('samp', 'vox'), split_axis=0, concat_axis=0, tile...  5.55 us
    ppermute x1, starting transfers between devices, on_device(): to_low = lax.ppermute(high, 'vox', [(i, i + 1) for i in range(7)])  4.88 us
  transfers between devices with their start and end apart: 12, of which 3 were waited for; matrix products, arithmetic and copies ran while one was open for 0% of the time, Pallas kernels for 9%

profile of v1, /device:TPU:96, one launch (start us, length us, event | category | flops | bytes accessed | tf_op | source)
XLA Modules:
  0.0 92.9 jit_solution(4810814938759857908)
XLA Ops:
  0.6 1.0 %copy-done = bf16[1,4,16,32,64]{4,3,2,1,0:T(8,128)(2,1)S(1)} copy-done((bf16[1,4,16,32,64]{4,3,2,1,0:T(8,128)(2,1)S(1)}, bf16[1,4,16,32,64]{4,3,2,1,0:T(8,128)(2,1)}, u32[]{:S(2)}) %copy-start) | copy-done | bytes 262168
  1.7 0.9 copy-done.1
  2.6 0.4 shard_map.51
  3.0 1.6 %collective-permute-start = (bf16[1024,128]{1,0:T(8,128)(2,1)S(1)}, bf16[1024,128]{1,0:T(8,128)(2,1)S(1)}, u32[]{:S(2)}, u32[]{:S(2)}) collective-permute-start(bf16[1024,128]{1,0:T(8,128)(2,1)S(1)} %get-tuple-element.7.refs_0_), channel_id=1, source_target_pairs={{0,2},{1,3},{2,4},{3,5},{4,6},{5,7},{6,0},{7,1},{8,10},{9,11},{10,... | collective-permute-start | bytes 786440 | tf_op jit(solution)/shard_map/ppermute | solution.py:198
  4.6 1.7 %collective-permute-start.1 = (bf16[1024,128]{1,0:T(8,128)(2,1)S(1)}, bf16[1024,128]{1,0:T(8,128)(2,1)S(1)}, u32[]{:S(2)}, u32[]{:S(2)}) collective-permute-start(bf16[1024,128]{1,0:T(8,128)(2,1)S(1)} %get-tuple-element.7.refs_0_), channel_id=1, source_target_pairs={{0,6},{1,7},{2,0},{3,1},{4,2},{5,3},{6,4},{7,5},{8,14},{9,15},{10,... | collective-permute-start | bytes 786440 | tf_op jit(solution)/shard_map/ppermute | solution.py:198
  6.3 1.8 %collective-permute-start.2 = (bf16[1024,128]{1,0:T(8,128)(2,1)S(1)}, bf16[1024,128]{1,0:T(8,128)(2,1)S(1)}, u32[]{:S(2)}, u32[]{:S(2)}) collective-permute-start(bf16[1024,128]{1,0:T(8,128)(2,1)S(1)} %get-tuple-element.7.refs_0_), channel_id=1, source_target_pairs={{0,4},{1,5},{2,6},{3,7},{4,0},{5,1},{6,2},{7,3},{8,12},{9,13},{10,... | collective-permute-start | bytes 786440 | tf_op jit(solution)/shard_map/ppermute | solution.py:198
  8.1 12.3 %all_to_all.15 = bf16[8,64,128]{2,1,0:T(8,128)(2,1)S(1)} all-to-all(bf16[8,64,128]{2,1,0:T(8,128)(2,1)S(1)} %get-tuple-element.11), channel_id=1, replica_groups=mesh['samp'=2,'vox'=8,'chan'=8] {'chan'}, dimensions={0} | all-to-all | bytes 262144 | tf_op jit(solution)/shard_map/all_to_all | solution.py:207
  20.4 3.7 %collective-permute-start.9 = (bf16[512,128]{1,0:T(8,128)(2,1)S(1)}, bf16[512,128]{1,0:T(8,128)(2,1)S(1)}, u32[]{:S(2)}, u32[]{:S(2)}) collective-permute-start(bf16[512,128]{1,0:T(8,128)(2,1)S(1)} %bitcast.14), channel_id=1, source_target_pairs={{0,8},{8,16},{16,24},{24,32},{32,40},{40,48},{48,56},{1,9},{9,17},... | collective-permute-start | bytes 393224 | tf_op jit(solution)/shard_map/ppermute | solution.py:208
  24.1 0.1 collective-permute-start.3
  24.2 0.0 collective-permute-done.refs_1_
  24.2 0.5 collective-permute-start.4
  24.7 0.1 collective-permute-start.5
  24.8 0.4 collective-permute-start.6
  25.2 2.1 %collective-permute-done.9.left_ref = bf16[512,128]{1,0:T(8,128)(2,1)S(1)} collective-permute-done((bf16[512,128]{1,0:T(8,128)(2,1)S(1)}, bf16[512,128]{1,0:T(8,128)(2,1)S(1)}, u32[]{:S(2)}, u32[]{:S(2)}) %collective-permute-start.9) | collective-permute-done | bytes 131104 | tf_op jit(solution)/shard_map/ppermute | solution.py:208
  27.3 2.3 %collective-permute-start.10 = (bf16[512,128]{1,0:T(8,128)(2,1)S(1)}, bf16[512,128]{1,0:T(8,128)(2,1)S(1)}, u32[]{:S(2)}, u32[]{:S(2)}) collective-permute-start(bf16[512,128]{1,0:T(8,128)(2,1)S(1)} %bitcast.15), channel_id=1, source_target_pairs={{8,0},{16,8},{24,16},{32,24},{40,32},{48,40},{56,48},{9,1},{17,9},... | collective-permute-start | bytes 393224 | tf_op jit(solution)/shard_map/ppermute | solution.py:209
  29.7 0.1 stack.35.spot_ref
  29.8 8.0 %collective-permute-done.10.right_ref = bf16[512,128]{1,0:T(8,128)(2,1)S(1)} collective-permute-done((bf16[512,128]{1,0:T(8,128)(2,1)S(1)}, bf16[512,128]{1,0:T(8,128)(2,1)S(1)}, u32[]{:S(2)}, u32[]{:S(2)}) %collective-permute-start.10) | collective-permute-done | bytes 131104 | tf_op jit(solution)/shard_map/ppermute | solution.py:209
  37.8 0.8 shard_map.54.l_ref
  38.6 0.0 collective-permute-done.4.refs_5_
  38.6 0.0 collective-permute-done.5.refs_6_
  38.7 5.8 %shard_map.55 = bf16[16,224,128]{2,1,0:T(8,128)(2,1)S(1)} custom-call(s32[8]{0:T(128)S(1)} %stack.35.spot_ref, bf16[1152,1024]{1,0:T(8,128)(2,1)S(1)} %shard_map.54.l_ref, bf16[1024,128]{1,0:T(8,128)(2,1)S(1)} %get-tuple-element.7.refs_0_, bf16[1024,128]{1,0:T(8,128)(2,1)S(1)} %collective-permute-done.refs_1_, ...), custom_call_target="tpu_custom_call" | custom-call | flops 2415919104 | bytes 6291456 | tf_op jit(solution)/shard_map/pallas_call | solution.py:215
  44.5 16.5 %all_to_all.16.in_ref = bf16[16,224,128]{2,1,0:T(8,128)(2,1)S(1)} all-to-all(bf16[16,224,128]{2,1,0:T(8,128)(2,1)S(1)} %shard_map.55), channel_id=1, replica_groups=mesh['samp'=2,'vox'=8,'chan'=8] {'samp','vox'}, dimensions={0} | all-to-all | bytes 1835008 | tf_op jit(solution)/shard_map/all_to_all | solution.py:233
  61.0 2.3 %shard_map.56 = bf16[16,224,128]{2,1,0:T(8,128)(2,1)} custom-call(bf16[16,224,128]{2,1,0:T(8,128)(2,1)S(1)} %all_to_all.16.in_ref), custom_call_target="tpu_custom_call" | custom-call | bytes 1048576 | tf_op jit(solution)/shard_map/pallas_call | solution.py:234
  63.3 5.6 %all-to-all-start.2 = ((bf16[16,224,128]{2,1,0:T(8,128)(2,1)}), bf16[16,224,128]{2,1,0:T(8,128)(2,1)S(1)}, u32[]{:S(2)}, u32[]{:S(2)}) async-start(bf16[16,224,128]{2,1,0:T(8,128)(2,1)} %shard_map.56), calls=%async_computation.2 | async-start | bytes 1835008 | tf_op jit(solution)/shard_map/all_to_all | solution.py:235
  68.8 1.7 %shard_map.50.w_ref = bf16[1152,1024]{1,0:T(8,128)(2,1)S(1)} custom-call(s32[1]{0:T(128)} %bitcast.8.at_ref, bf16[27,256,512]{2,1,0:T(8,128)(2,1)} %w_ref.1), custom_call_target="tpu_custom_call" | custom-call | bytes 4194304 | tf_op jit(solution)/shard_map/pallas_call | solution.py:70
  70.5 4.2 %shard_map.52 = (f32[512,128]{1,0:T(8,128)S(1)}, f32[128,128]{1,0:T(8,128)S(1)}, f32[128,128]{1,0:T(8,128)S(1)}) custom-call(s32[8]{0:T(128)S(1)} %stack.35.spot_ref, bf16[1152,1024]{1,0:T(8,128)(2,1)S(1)} %shard_map.50.w_ref, bf16[1024,128]{1,0:T(8,128)(2,1)S(1)} %get-tuple-element.7.refs_0_, bf16[1024,128]{1,0:T(8,128)(2,1)S(1)} %collective-permute-done.refs_1_, ...), custom_call_target="tpu_custom_call" | custom-call | flops 2684354560 | bytes 6291456 | tf_op jit(solution)/shard_map/pallas_call | solution.py:215
  74.7 4.9 %collective-permute-start.7 = (f32[128,128]{1,0:T(8,128)S(1)}, f32[128,128]{1,0:T(8,128)S(1)}, u32[]{:S(2)}, u32[]{:S(2)}) collective-permute-start(f32[128,128]{1,0:T(8,128)S(1)} %get-tuple-element.9), channel_id=1, source_target_pairs={{0,8},{8,16},{16,24},{24,32},{32,40},{40,48},{48,56},{1,9},{9,17},... | collective-permute-start | bytes 196616 | tf_op jit(solution)/shard_map/ppermute | solution.py:239
  79.6 1.9 %collective-permute-start.8 = (f32[128,128]{1,0:T(8,128)S(1)}, f32[128,128]{1,0:T(8,128)S(1)}, u32[]{:S(2)}, u32[]{:S(2)}) collective-permute-start(f32[128,128]{1,0:T(8,128)S(1)} %get-tuple-element.10), channel_id=1, source_target_pairs={{8,0},{16,8},{24,16},{32,24},{40,32},{48,40},{56,48},{9,1},{17,9},... | collective-permute-start | bytes 196616 | tf_op jit(solution)/shard_map/ppermute | solution.py:238
  81.5 0.0 collective-permute-done.7.low_ref
  81.6 7.8 %collective-permute-done.8.high_ref = f32[128,128]{1,0:T(8,128)S(1)} collective-permute-done((f32[128,128]{1,0:T(8,128)S(1)}, f32[128,128]{1,0:T(8,128)S(1)}, u32[]{:S(2)}, u32[]{:S(2)}) %collective-permute-start.8) | collective-permute-done | bytes 65568 | tf_op jit(solution)/shard_map/ppermute | solution.py:238
  89.4 1.4 %shard_map.53 = f32[4,512,32]{2,1,0:T(8,128)} custom-call(f32[512,128]{1,0:T(8,128)S(1)} %get-tuple-element.8.own_ref, f32[128,128]{1,0:T(8,128)S(1)} %collective-permute-done.7.low_ref, f32[128,128]{1,0:T(8,128)S(1)} %collective-permute-done.8.high_ref), custom_call_target="tpu_custom_call" | custom-call | bytes 1048576 | tf_op jit(solution)/shard_map/pallas_call | solution.py:240
  90.8 2.1 %shard_map.57 = f32[27,32,512]{2,1,0:T(8,128)} custom-call(bf16[16,224,128]{2,1,0:T(8,128)(2,1)S(1)} %all-to-all-done.2.in_ref), custom_call_target="tpu_custom_call" | custom-call | bytes 1048576 | tf_op jit(solution)/shard_map/pallas_call | solution.py:236
  (7 shorter events, 0.0 us)
Async XLA Ops:
  0.6 1.0 %copy-start = (bf16[1,4,16,32,64]{4,3,2,1,0:T(8,128)(2,1)S(1)}, bf16[1,4,16,32,64]{4,3,2,1,0:T(8,128)(2,1)}, u32[]{:S(2)}) copy-start(bf16[1,4,16,32,64]{4,3,2,1,0:T(8,128)(2,1)} %param.4) | copy-start | bytes 786436
  1.7 0.9 copy-start.1
  3.0 21.2 %collective-permute-start = (bf16[1024,128]{1,0:T(8,128)(2,1)S(1)}, bf16[1024,128]{1,0:T(8,128)(2,1)S(1)}, u32[]{:S(2)}, u32[]{:S(2)}) collective-permute-start(bf16[1024,128]{1,0:T(8,128)(2,1)S(1)} %get-tuple-element.7.refs_0_), channel_id=1, source_target_pairs={{0,2},{1,3},{2,4},{3,5},{4,6},{5,7},{6,0},{7,1},{8,10},{9,11},{10,... | collective-permute-start | bytes 786440 | tf_op jit(solution)/shard_map/ppermute | solution.py:198
  4.6 20.1 %collective-permute-start.1 = (bf16[1024,128]{1,0:T(8,128)(2,1)S(1)}, bf16[1024,128]{1,0:T(8,128)(2,1)S(1)}, u32[]{:S(2)}, u32[]{:S(2)}) collective-permute-start(bf16[1024,128]{1,0:T(8,128)(2,1)S(1)} %get-tuple-element.7.refs_0_), channel_id=1, source_target_pairs={{0,6},{1,7},{2,0},{3,1},{4,2},{5,3},{6,4},{7,5},{8,14},{9,15},{10,... | collective-permute-start | bytes 786440 | tf_op jit(solution)/shard_map/ppermute | solution.py:198
  6.3 18.5 %collective-permute-start.2 = (bf16[1024,128]{1,0:T(8,128)(2,1)S(1)}, bf16[1024,128]{1,0:T(8,128)(2,1)S(1)}, u32[]{:S(2)}, u32[]{:S(2)}) collective-permute-start(bf16[1024,128]{1,0:T(8,128)(2,1)S(1)} %get-tuple-element.7.refs_0_), channel_id=1, source_target_pairs={{0,4},{1,5},{2,6},{3,7},{4,0},{5,1},{6,2},{7,3},{8,12},{9,13},{10,... | collective-permute-start | bytes 786440 | tf_op jit(solution)/shard_map/ppermute | solution.py:198
  20.4 6.9 %collective-permute-start.9 = (bf16[512,128]{1,0:T(8,128)(2,1)S(1)}, bf16[512,128]{1,0:T(8,128)(2,1)S(1)}, u32[]{:S(2)}, u32[]{:S(2)}) collective-permute-start(bf16[512,128]{1,0:T(8,128)(2,1)S(1)} %bitcast.14), channel_id=1, source_target_pairs={{0,8},{8,16},{16,24},{24,32},{32,40},{40,48},{48,56},{1,9},{9,17},... | collective-permute-start | bytes 393224 | tf_op jit(solution)/shard_map/ppermute | solution.py:208
  24.1 14.5 %collective-permute-start.3 = (bf16[1024,128]{1,0:T(8,128)(2,1)S(1)}, bf16[1024,128]{1,0:T(8,128)(2,1)S(1)}, u32[]{:S(2)}, u32[]{:S(2)}) collective-permute-start(bf16[1024,128]{1,0:T(8,128)(2,1)S(1)} %get-tuple-element.7.refs_0_), channel_id=1, source_target_pairs={{0,1},{1,0},{2,3},{3,2},{4,5},{5,4},{6,7},{7,6},{8,9},{9,8},{10,11... | collective-permute-start | bytes 786440 | tf_op jit(solution)/shard_map/ppermute | solution.py:198
  24.2 14.4 %collective-permute-start.4 = (bf16[1024,128]{1,0:T(8,128)(2,1)S(1)}, bf16[1024,128]{1,0:T(8,128)(2,1)S(1)}, u32[]{:S(2)}, u32[]{:S(2)}) collective-permute-start(bf16[1024,128]{1,0:T(8,128)(2,1)S(1)} %collective-permute-done.refs_1_), channel_id=1, source_target_pairs={{0,1},{1,0},{2,3},{3,2},{4,5},{5,4},{6,7},{7,6},{8,9},{9,8},{10,11... | collective-permute-start | bytes 786440 | tf_op jit(solution)/shard_map/ppermute | solution.py:198
  24.7 13.9 %collective-permute-start.5 = (bf16[1024,128]{1,0:T(8,128)(2,1)S(1)}, bf16[1024,128]{1,0:T(8,128)(2,1)S(1)}, u32[]{:S(2)}, u32[]{:S(2)}) collective-permute-start(bf16[1024,128]{1,0:T(8,128)(2,1)S(1)} %collective-permute-done.1.refs_2_), channel_id=1, source_target_pairs={{0,1},{1,0},{2,3},{3,2},{4,5},{5,4},{6,7},{7,6},{8,9},{9,8},{10,11... | collective-permute-start | bytes 786440 | tf_op jit(solution)/shard_map/ppermute | solution.py:198
  24.8 13.8 %collective-permute-start.6 = (bf16[1024,128]{1,0:T(8,128)(2,1)S(1)}, bf16[1024,128]{1,0:T(8,128)(2,1)S(1)}, u32[]{:S(2)}, u32[]{:S(2)}) collective-permute-start(bf16[1024,128]{1,0:T(8,128)(2,1)S(1)} %collective-permute-done.2.refs_3_), channel_id=1, source_target_pairs={{0,1},{1,0},{2,3},{3,2},{4,5},{5,4},{6,7},{7,6},{8,9},{9,8},{10,11... | collective-permute-start | bytes 786440 | tf_op jit(solution)/shard_map/ppermute | solution.py:198
  27.3 10.5 %collective-permute-start.10 = (bf16[512,128]{1,0:T(8,128)(2,1)S(1)}, bf16[512,128]{1,0:T(8,128)(2,1)S(1)}, u32[]{:S(2)}, u32[]{:S(2)}) collective-permute-start(bf16[512,128]{1,0:T(8,128)(2,1)S(1)} %bitcast.15), channel_id=1, source_target_pairs={{8,0},{16,8},{24,16},{32,24},{40,32},{48,40},{56,48},{9,1},{17,9},... | collective-permute-start | bytes 393224 | tf_op jit(solution)/shard_map/ppermute | solution.py:209
  63.3 27.5 %all-to-all-start.2 = ((bf16[16,224,128]{2,1,0:T(8,128)(2,1)}), bf16[16,224,128]{2,1,0:T(8,128)(2,1)S(1)}, u32[]{:S(2)}, u32[]{:S(2)}) async-start(bf16[16,224,128]{2,1,0:T(8,128)(2,1)} %shard_map.56), calls=%async_computation.2 | async-start | bytes 1835008 | tf_op jit(solution)/shard_map/all_to_all | solution.py:235
  74.7 6.8 %collective-permute-start.7 = (f32[128,128]{1,0:T(8,128)S(1)}, f32[128,128]{1,0:T(8,128)S(1)}, u32[]{:S(2)}, u32[]{:S(2)}) collective-permute-start(f32[128,128]{1,0:T(8,128)S(1)} %get-tuple-element.9), channel_id=1, source_target_pairs={{0,8},{8,16},{16,24},{24,32},{32,40},{40,48},{48,56},{1,9},{9,17},... | collective-permute-start | bytes 196616 | tf_op jit(solution)/shard_map/ppermute | solution.py:239
  79.6 9.8 %collective-permute-start.8 = (f32[128,128]{1,0:T(8,128)S(1)}, f32[128,128]{1,0:T(8,128)S(1)}, u32[]{:S(2)}, u32[]{:S(2)}) collective-permute-start(f32[128,128]{1,0:T(8,128)S(1)} %get-tuple-element.10), channel_id=1, source_target_pairs={{8,0},{16,8},{24,16},{32,24},{40,32},{48,40},{56,48},{9,1},{17,9},... | collective-permute-start | bytes 196616 | tf_op jit(solution)/shard_map/ppermute | solution.py:238

commit v2 on v0

v2 whole, which is shorter than its diff:
```python
import jax
import jax.numpy as jnp
from jax import lax
from jax.experimental import pallas as pl
from jax.experimental.pallas import tpu as pltpu
from jax.sharding import PartitionSpec as P

F32, BF16 = jnp.float32, jnp.bfloat16
STEPS, BIAS = 249.0, 125.0
VM = pl.BlockSpec(memory_space=pltpu.VMEM)
SM = pl.BlockSpec(memory_space=pltpu.SMEM)
ANY = pl.BlockSpec(memory_space=pl.ANY)
HBM = pl.BlockSpec(memory_space=pltpu.HBM)


def call(body, outs, ins, scratch=(), flops=0, nbytes=1 << 20, mib=4):
    return pl.pallas_call(
        body,
        out_shape=outs,
        in_specs=ins,
        out_specs=jax.tree.map(lambda _: VM, outs),
        scratch_shapes=list(scratch),
        compiler_params=pltpu.CompilerParams(vmem_limit_bytes=mib << 20),
        cost_estimate=pl.CostEstimate(flops=flops, bytes_accessed=nbytes, transcendentals=0),
    )


def encode(value, exponent):
    q = jnp.sqrt(jnp.abs(value) * jnp.exp2(-exponent)) * STEPS
    whole = jnp.floor(q)
    code = jnp.exp2(whole - BIAS) * (1.0 + (q - whole))
    return jnp.where(value < 0, -code, code)


def decode(code, exponent):
    size = jnp.abs(code)
    whole = jnp.floor(jnp.log2(size))
    q = (whole + BIAS) + (size * jnp.exp2(-whole) - 1.0)
    square = q * q * (jnp.exp2(exponent) / (STEPS * STEPS))
    return jnp.where(code < 0, -square, square)


def top_exponent(most):
    most = jnp.max(jnp.max(most, axis=0, keepdims=True), axis=1, keepdims=True)
    return jnp.ceil(jnp.log2(jnp.maximum(most, 1e-30)))


def chip_panel(core, own, other):
    return jnp.where(core == 0, jnp.concatenate([own, other], axis=1), jnp.concatenate([other, own], axis=1))


def split_channels(core, block, keep_ref, give_ref):
    for p in range(4):
        rows = block[p]
        even = jnp.concatenate([rows[:, 64 * k : 64 * k + 32] for k in range(4)], axis=1)
        odd = jnp.concatenate([rows[:, 64 * k + 32 : 64 * k + 64] for k in range(4)], axis=1)
        keep_ref[p] = jnp.where(core == 0, even, odd)
        give_ref[p] = jnp.where(core == 0, odd, even)


def first_body(at_ref, g_ref, other_ref, x_ref, panel_ref, low_ref, high_ref, keep_ref, give_ref):
    for p in range(4):
        panel_ref[p] = chip_panel(at_ref[1], g_ref[p], other_ref[p])
    low_ref[...] = panel_ref[0]
    high_ref[...] = panel_ref[3]
    split_channels(at_ref[1], x_ref, keep_ref, give_ref)


def write_patches(panel_ref, left_ref, right_ref, out_ref):
    edge = jnp.zeros((16, 1, 128), F32)
    blank = jnp.zeros((32, 128), BF16)
    for plane in range(-1, 5):
        if plane < 0:
            block = left_ref[...]
        elif plane > 3:
            block = right_ref[...]
        else:
            block = panel_ref[plane]
        cells = block.astype(F32).reshape(16, 32, 128)
        moved = (
            jnp.concatenate([cells[:, 1:], edge], axis=1).reshape(512, 128).astype(BF16),
            block,
            jnp.concatenate([edge, cells[:, :31]], axis=1).reshape(512, 128).astype(BF16),
        )
        for t in range(2):
            slot = plane + 1 - 2 * t
            if not 0 <= slot < 4:
                continue
            rows = 512 * t
            for c in range(3):
                for b in range(3):
                    at = 512 * (3 * b + c) + 128 * slot
                    lanes = slice(at, at + 128)
                    if b == 0:
                        out_ref[rows : rows + 480, lanes] = moved[c][32:]
                        out_ref[rows + 480 : rows + 512, lanes] = blank
                    elif b == 1:
                        out_ref[rows : rows + 512, lanes] = moved[c]
                    else:
                        out_ref[rows : rows + 32, lanes] = blank
                        out_ref[rows + 32 : rows + 512, lanes] = moved[c][:480]


def split_body(at_ref, _, __, *refs):
    blocks, keep_ref, give_ref = refs[:3], refs[3], refs[4]
    for i, block in enumerate(blocks):
        split_channels(at_ref[1], block, keep_ref.at[i], give_ref.at[i])


def kernel_grad_body(spot_ref, p_ref, own_ref, other_ref, keep_ref, got_ref, out_ref, x_ref, xt_ref, sum_ref):
    parts = [own_ref] + [keep_ref.at[i] for i in range(3)] + [other_ref] + [got_ref.at[i] for i in range(3)]
    for i, part in enumerate(parts):
        for p in range(4):
            rows = pl.ds(pl.multiple_of(512 * (p // 2) + spot_ref[i] * 64, 64), 64)
            x_ref[rows, 128 * (p % 2) : 128 * (p % 2) + 128] = part[p]
    for i in range(2):
        xt_ref[128 * i : 128 * (i + 1), :] = x_ref[:, 128 * i : 128 * (i + 1)].T
    most = jnp.zeros((128, 128), F32)
    for bc in range(9):
        prod = jnp.dot(xt_ref[...], p_ref[:, 512 * bc : 512 * (bc + 1)], preferred_element_type=F32)
        for a in range(3):
            even, odd = 128 * (2 - a), 128 * (3 - a)
            total = (prod[:128, even : even + 128] + prod[128:, odd : odd + 128]) * (32768.0**-0.5)
            sum_ref[9 * a + bc] = total
            most = jnp.maximum(most, jnp.abs(total))
    exponent = top_exponent(most)
    for k in range(27):
        sum_ref[k] = encode(sum_ref[k], exponent)
    sum_ref[27] = jnp.full((128, 128), 2.0**-BIAS, F32)
    stamp = jnp.broadcast_to(exponent, (8, 128))
    for jr in range(4):
        for k in range(4):
            rows = slice(32 * k + 8 * jr, 32 * k + 8 * jr + 8)
            for jt in range(4):
                tiles = [sum_ref[7 * jt + i, rows, :] for i in range(7)] + [stamp]
                out_ref[(4 * jr + jt) * 4 + k] = jnp.concatenate(tiles, axis=0).astype(BF16)


def shard_sum_body(in_ref, _, out_ref, sum_ref):
    most = jnp.zeros((56, 128), F32)
    for k in range(4):
        total = jnp.zeros((56, 128), F32)
        for j in range(16):
            code = in_ref[4 * j + k].astype(F32)
            total = total + decode(code[:56], code[56:57])
        sum_ref[k] = total
        most = jnp.maximum(most, jnp.abs(total))
    exponent = top_exponent(most)
    stamp = jnp.broadcast_to(exponent, (8, 128))
    for k in range(4):
        code = jnp.concatenate([encode(sum_ref[k], exponent), stamp], axis=0).astype(BF16)
        for j in range(16):
            out_ref[j, 64 * k : 64 * (k + 1), :] = code


def kernel_out_body(in_ref, out_ref):
    for jr in range(4):
        for jt in range(4):
            for k in range(4):
                code = in_ref[4 * jr + jt, 64 * k : 64 * (k + 1), :].astype(F32)
                value = decode(code[:56], code[56:57])
                for i in range(7 if jt < 3 else 6):
                    out_ref[7 * jt + i, 8 * jr : 8 * jr + 8, 128 * k : 128 * (k + 1)] = value[8 * i : 8 * i + 8]


def data_grad_body(at_ref, panel_ref, left_ref, right_ref, weight_ref, _, *refs):
    outs, cut_ref, w_ref, p_ref, sem = refs[:4], *refs[4:8]
    chip, core = at_ref[0], at_ref[1]
    copy = pltpu.make_async_copy(weight_ref.at[:, :, pl.ds(pl.multiple_of(chip * 128, 128), 128)], cut_ref, sem)
    copy.start()
    write_patches(panel_ref, left_ref, right_ref, p_ref)
    copy.wait()
    none = jnp.zeros((32, 128), BF16)
    for d in range(4):
        rows = pl.ds(pl.multiple_of(64 * lax.rem(chip + d, 4) + 32 * core, 32), 32)
        for bc in range(9):
            for e in range(2):
                for slot in range(4):
                    a = e + 2 - slot
                    lanes = slice(512 * bc + 128 * slot, 512 * bc + 128 * slot + 128)
                    w_ref[128 * e + 32 * d : 128 * e + 32 * d + 32, lanes] = (
                        cut_ref[9 * a + bc, rows, :] if 0 <= a < 3 else none
                    )
    prod = lax.dot_general(p_ref[...], w_ref[...], (((1,), (1,)), ((), ())), preferred_element_type=F32)
    planes = [prod[512 * (p // 2) : 512 * (p // 2) + 512, 128 * (p % 2) : 128 * (p % 2) + 128] for p in range(4)]
    for d, out_ref in enumerate(outs):
        slab = jnp.concatenate([plane[:, 32 * d : 32 * (d + 1)] for plane in planes], axis=1)
        if d == 0:
            out_ref[...] = slab
        else:
            exponent = top_exponent(jnp.abs(slab))
            out_ref[:512, :] = encode(slab, exponent).astype(BF16)
            out_ref[512:, :] = jnp.broadcast_to(exponent, (16, 128)).astype(BF16)


def data_out_body(own_ref, *refs):
    total = own_ref[...]
    for ref in refs[:3]:
        code = ref[...].astype(F32)
        total = total + decode(code[:512], code[512:513])
    for p in range(4):
        refs[3][p] = total[:, 32 * p : 32 * (p + 1)]


def on_device(activations, out_grad, weight):
    column = lax.axis_index("chan")
    chip, core = column // 2, column % 2
    at = jnp.stack([chip, core]).astype(jnp.int32)
    froms = [chip, (chip + 3) % 4, (chip + 1) % 4, (chip + 2) % 4]
    spots = jnp.stack([2 * f + core for f in froms] + [2 * f + 1 - core for f in froms]).astype(jnp.int32)
    struct = jax.ShapeDtypeStruct
    whole = ("samp", "vox", "chan")
    cores = [[8 * j + 2 * k + h for j in range(16) for k in range(4)] for h in range(2)]

    def hop(value, chips, cores):
        return lax.ppermute(
            value, "chan", [(i, ((i // 2 + chips) % 4) * 2 + (i % 2 ^ cores)) for i in range(8)]
        )

    x = activations.reshape(4, 64, 256)
    g = out_grad.reshape(4, 512, 64)
    g_other = hop(g, 0, 1)
    near = [hop(x, d, 0) for d in (1, 3, 2)]
    rim, kept = struct((512, 128), BF16), struct((4, 64, 128), BF16)
    panel, low, high, own, other = call(
        first_body, (struct((4, 512, 128), BF16), rim, rim, kept, kept), [SM, VM, VM, VM]
    )(at, g, g_other, x)
    left = lax.ppermute(high, "vox", [(i, i + 1) for i in range(7)])
    right = lax.ppermute(low, "vox", [(i + 1, i) for i in range(7)])
    other = hop(other, 0, 1)
    three = struct((3, 4, 64, 128), BF16)
    keep, give = call(split_body, (three, three), [SM, ANY, ANY] + [VM] * 3)(at, left, right, *near)
    got = hop(give, 0, 1)
    patches = call(write_patches, struct((1024, 4608), BF16), [VM] * 3)(panel, left, right)

    codes = call(
        kernel_grad_body, struct((64, 64, 128), BF16), [SM] + [VM] * 5,
        [pltpu.VMEM((1024, 256), BF16), pltpu.VMEM((256, 1024), BF16), pltpu.VMEM((28, 128, 128), F32)],
        2 * 2304 * 1024 * 512, 12 << 20, 10,
    )(spots, patches, own, other, keep, got)
    swapped = lax.all_to_all(codes, whole, split_axis=0, concat_axis=0, tiled=True, axis_index_groups=cores)
    slab, coded = struct((512, 128), F32), struct((528, 128), BF16)
    slabs = call(
        data_grad_body, (slab, coded, coded, coded), [SM, VM, VM, VM, HBM, ANY],
        [
            pltpu.VMEM((27, 256, 128), BF16), pltpu.VMEM((256, 4608), BF16), pltpu.VMEM((1024, 4608), BF16),
            pltpu.SemaphoreType.DMA,
        ],
        2 * 2304 * 1024 * 512, 12 << 20, 57,
    )(at, panel, left, right, weight, codes)
    shards = call(
        shard_sum_body, struct((16, 256, 128), BF16), [VM, ANY], [pltpu.VMEM((4, 56, 128), F32)]
    )(swapped, slabs[0])
    final = lax.all_to_all(shards, ("samp", "vox"), split_axis=0, concat_axis=0, tiled=True)
    weight_grad = call(kernel_out_body, struct((27, 32, 512), F32), [VM])(final)
    data_grad = call(data_out_body, struct((4, 512, 32), F32), [VM] * 4)(
        slabs[0], *[hop(slabs[d], d, 0) for d in (1, 3, 2)]
    )
    return data_grad.reshape(1, 4, 16, 32, 32), weight_grad


def solution(mesh):
    placed = (P("samp", "vox", "chan", None, None), P("samp", "vox", None, None, "chan"), P())
    return jax.shard_map(
        on_device,
        mesh=mesh,
        in_specs=placed,
        out_specs=(P("samp", "vox", None, None, "chan"), P(None, "chan", None)),
        check_vma=False,
    )
```

time: 273 us -> 84.5 us (0.31)
  matrix products: 85.1 us -> 0 us
  waiting for transfers between devices: 105 us -> 27.1 us
  local copies, waits for them, and re-layouts: 39.3 us -> 3.95 us
  Pallas kernels: 0 us -> 22.2 us
  starting transfers between devices: 12.4 us -> 29.9 us
  between operations: 14.6 us -> 0.78 us
  blocking collectives: 10.2 us -> 0 us
  other arithmetic: 5.83 us -> 0.07 us
    dot_general x54 -> x0, matrix products: 85.1 us -> none  [the longest x27 44.2 us: on_device(): lax.dot_general(moved_g, w_local[k], (((1,), (1,)), ((), ())), preferred_...]
    all_gather x1 -> x0, waiting for transfers between devices: 53 us -> none  [on_device(): panel = lax.all_gather(rim_g, 'chan', axis=4, tiled=True)]
    psum x1 -> x0, waiting for transfers between devices: 43.6 us -> none  [on_device(): weight_grad = lax.psum(dw_part, ('samp', 'vox')) * factor]
    pallas_call x0 -> x8, Pallas kernels: none -> 22.2 us  [the longest x1 7.51 us: on_device(): call(data_grad_body, (slab, coded, coded, coded), [SM, VM, VM, VM, HBM, A...]
    slice x4 -> x0, local copies, waits for them, and re-layouts: 21.6 us -> none  [the longest x2 21.5 us: window(): padded[:, 1 + a:1 + a + slab_depth, 1 + b:1 + b + grid_rows, 1 + c:1 + c...]
    all_to_all x0 -> x2, starting transfers between devices: none -> 15.6 us  [the longest x1 11.9 us: on_device(): lax.all_to_all(codes, whole, split_axis=0, concat_axis=0, tiled=True, axi...]
    all_to_all x0 -> x2, waiting for transfers between devices: none -> 14.8 us  [the longest x1 11.4 us: on_device(): lax.all_to_all(codes, whole, split_axis=0, concat_axis=0, tiled=True, axi...]
    all_gather x1 -> x0, local copies, waits for them, and re-layouts: 12.2 us -> none  [on_device(): panel = lax.all_gather(rim_g, 'chan', axis=4, tiled=True)]
  transfers between devices with their start and end apart: 6 -> 13, of which waited for: 6 -> 6; matrix products, arithmetic and copies ran while one was open for 18% -> 0% of each run, Pallas kernels for 0% -> 14%
where the time goes in v2:
time: 84.5 us; the launch traced here: 84 us
  starting transfers between devices  29.9 us (35%)
  waiting for transfers between devices  27.1 us (32%)
  Pallas kernels  22.2 us (26%)
  local copies, waits for them, and re-layouts  3.95 us (5%)
    all_to_all x1, starting transfers between devices, on_device(): lax.all_to_all(codes, whole, split_axis=0, concat_axis=0, tiled=True, axi...  11.9 us
    all_to_all x1, waiting for transfers between devices, on_device(): lax.all_to_all(codes, whole, split_axis=0, concat_axis=0, tiled=True, axi...  11.4 us
    ppermute x9, starting transfers between devices, hop(): lax.ppermute(value, 'chan', [(i, (i // 2 + chips) % 4 * 2 + (i % 2 ^ core...  9.19 us
    pallas_call x1, Pallas kernels, on_device(): call(data_grad_body, (slab, coded, coded, coded), [SM, VM, VM, VM, HBM, A...  7.51 us
    ppermute x9, waiting for transfers between devices, hop(): lax.ppermute(value, 'chan', [(i, (i // 2 + chips) % 4 * 2 + (i % 2 ^ core...  6.74 us
    pallas_call x1, Pallas kernels, on_device(): call(kernel_grad_body, struct((64, 64, 128), BF16), [SM] + [VM] * 5, [plt...  5.56 us
    ppermute x1, waiting for transfers between devices, on_device(): right = lax.ppermute(low, 'vox', [(i + 1, i) for i in range(7)])  4.36 us
    unnamed x16, local copies, waits for them, and re-layouts  3.86 us
  transfers between devices with their start and end apart: 13, of which 6 were waited for; matrix products, arithmetic and copies ran while one was open for 0% of the time, Pallas kernels for 14%

profile of v2, /device:TPU:0, one launch (start us, length us, event | category | flops | bytes accessed | tf_op | source)
XLA Modules:
  0.0 84.0 jit_solution(3976051560047687456)
XLA Ops:
  0.6 0.1 collective-permute-start
  0.7 3.2 %collective-permute-start.6 = (bf16[4,64,256]{2,1,0:T(8,128)(2,1)}, bf16[4,64,256]{2,1,0:T(8,128)(2,1)S(1)}, u32[]{:S(2)}, u32[]{:S(2)}) collective-permute-start(bf16[4,64,256]{2,1,0:T(8,128)(2,1)} %bitcast.15), channel_id=1, source_target_pairs={{0,4},{1,5},{2,6},{3,7},{4,0},{5,1},{6,2},{7,3},{8,12},{9,13},{10,... | collective-permute-start | bytes 393224 | tf_op jit(solution)/shard_map/ppermute | solution.py:216
  3.9 1.1 %collective-permute-start.5 = (bf16[4,64,256]{2,1,0:T(8,128)(2,1)}, bf16[4,64,256]{2,1,0:T(8,128)(2,1)S(1)}, u32[]{:S(2)}, u32[]{:S(2)}) collective-permute-start(bf16[4,64,256]{2,1,0:T(8,128)(2,1)} %bitcast.16), channel_id=1, source_target_pairs={{0,6},{1,7},{2,0},{3,1},{4,2},{5,3},{6,4},{7,5},{8,14},{9,15},{10,... | collective-permute-start | bytes 393224 | tf_op jit(solution)/shard_map/ppermute | solution.py:216
  5.1 0.9 %collective-permute-start.4 = (bf16[4,64,256]{2,1,0:T(8,128)(2,1)}, bf16[4,64,256]{2,1,0:T(8,128)(2,1)S(1)}, u32[]{:S(2)}, u32[]{:S(2)}) collective-permute-start(bf16[4,64,256]{2,1,0:T(8,128)(2,1)} %bitcast.17), channel_id=1, source_target_pairs={{0,2},{1,3},{2,4},{3,5},{4,6},{5,7},{6,0},{7,1},{8,10},{9,11},{10,... | collective-permute-start | bytes 393224 | tf_op jit(solution)/shard_map/ppermute | solution.py:216
  5.9 0.1 pad_add_fusion.at_ref
  6.0 1.0 %copy-done.5 = bf16[1,4,16,32,64]{4,3,2,1,0:T(8,128)(2,1)S(1)} copy-done((bf16[1,4,16,32,64]{4,3,2,1,0:T(8,128)(2,1)S(1)}, bf16[1,4,16,32,64]{4,3,2,1,0:T(8,128)(2,1)}, u32[]{:S(2)}) %copy-start.5) | copy-done | bytes 262168
  7.1 0.9 %copy-done.6 = bf16[1,4,2,32,256]{4,3,2,1,0:T(8,128)(2,1)S(1)} copy-done((bf16[1,4,2,32,256]{4,3,2,1,0:T(8,128)(2,1)S(1)}, bf16[1,4,2,32,256]{4,3,2,1,0:T(8,128)(2,1)}, u32[]{:S(2)}) %copy-start.6) | copy-done | bytes 131096
  8.0 1.0 %shard_map.50 = (bf16[4,512,128]{2,1,0:T(8,128)(2,1)S(1)}, bf16[512,128]{1,0:T(8,128)(2,1)S(1)}, bf16[512,128]{1,0:T(8,128)(2,1)S(1)}, bf16[4,64,128]{2,1,0:T(8,128)(2,1)S(1)}, bf16[4,64,128]{2,1,0:T(8,128)(2,1)S(1)}) custom-call(s32[2]{0:T(128)S(1)} %pad_add_fusion.at_ref, bf16[4,512,64]{2,1,0:T(8,128)(2,1)S(1)} %bitcast.14, ...), custom_call_target="tpu_custom_call" | custom-call | bytes 1048576 | tf_op jit(solution)/shard_map/pallas_call | solution.py:225
  9.0 3.8 %collective-permute-start.1 = (bf16[512,128]{1,0:T(8,128)(2,1)S(1)}, bf16[512,128]{1,0:T(8,128)(2,1)S(1)}, u32[]{:S(2)}, u32[]{:S(2)}) collective-permute-start(bf16[512,128]{1,0:T(8,128)(2,1)S(1)} %get-tuple-element.14), channel_id=1, source_target_pairs={{0,8},{8,16},{16,24},{24,32},{32,40},{40,48},{48,56},{1,9},{9,17},... | collective-permute-start | bytes 393224 | tf_op jit(solution)/shard_map/ppermute | solution.py:228
  12.8 1.3 %collective-permute-start.2 = (bf16[512,128]{1,0:T(8,128)(2,1)S(1)}, bf16[512,128]{1,0:T(8,128)(2,1)S(1)}, u32[]{:S(2)}, u32[]{:S(2)}) collective-permute-start(bf16[512,128]{1,0:T(8,128)(2,1)S(1)} %get-tuple-element.15), channel_id=1, source_target_pairs={{8,0},{16,8},{24,16},{32,24},{40,32},{48,40},{56,48},{9,1},{17,9},... | collective-permute-start | bytes 393224 | tf_op jit(solution)/shard_map/ppermute | solution.py:229
  14.1 1.2 %collective-permute-done.1.left_ref._ = bf16[512,128]{1,0:T(8,128)(2,1)S(1)} collective-permute-done((bf16[512,128]{1,0:T(8,128)(2,1)S(1)}, bf16[512,128]{1,0:T(8,128)(2,1)S(1)}, u32[]{:S(2)}, u32[]{:S(2)}) %collective-permute-start.1) | collective-permute-done | bytes 131104 | tf_op jit(solution)/shard_map/ppermute | solution.py:228
  15.3 4.4 %collective-permute-done.2.right_ref.__ = bf16[512,128]{1,0:T(8,128)(2,1)S(1)} collective-permute-done((bf16[512,128]{1,0:T(8,128)(2,1)S(1)}, bf16[512,128]{1,0:T(8,128)(2,1)S(1)}, u32[]{:S(2)}, u32[]{:S(2)}) %collective-permute-start.2) | collective-permute-done | bytes 131104 | tf_op jit(solution)/shard_map/ppermute | solution.py:229
  19.7 0.8 shard_map.52
  20.5 0.1 collective-permute-start.7
  20.6 0.5 collective-permute-start.3
  21.1 0.1 stack.47.spot_ref
  21.2 1.3 %shard_map.51.p_ref = bf16[1024,4608]{1,0:T(8,128)(2,1)S(1)} custom-call(bf16[4,512,128]{2,1,0:T(8,128)(2,1)S(1)} %get-tuple-element.13.panel_ref, bf16[512,128]{1,0:T(8,128)(2,1)S(1)} %collective-permute-done.1.left_ref._, bf16[512,128]{1,0:T(8,128)(2,1)S(1)} %collective-permute-done.2.right_ref.__), custom_call_target="tpu_custom_call" | custom-call | bytes 1048576 | tf_op jit(solution)/shard_map/pallas_call | solution.py:234
  22.5 5.6 %shard_map.53._ = bf16[64,64,128]{2,1,0:T(8,128)(2,1)} custom-call(s32[8]{0:T(128)S(1)} %stack.47.spot_ref, bf16[1024,4608]{1,0:T(8,128)(2,1)S(1)} %shard_map.51.p_ref, bf16[4,64,128]{2,1,0:T(8,128)(2,1)S(1)} %get-tuple-element.16.own_ref, bf16[4,64,128]{2,1,0:T(8,128)(2,1)S(1)} %collective-permute-done.3.other_ref, ...), custom_call_target="tpu_custom_call" | custom-call | flops 2415919104 | bytes 12582912 | tf_op jit(solution)/shard_map/pallas_call | solution.py:236
  28.1 11.9 %all-to-all-start = ((bf16[64,64,128]{2,1,0:T(8,128)(2,1)}), bf16[64,64,128]{2,1,0:T(8,128)(2,1)S(1)}, u32[]{:S(2)}, u32[]{:S(2)}) async-start(bf16[64,64,128]{2,1,0:T(8,128)(2,1)} %shard_map.53._), calls=%async_computation | async-start | bytes 2097152 | tf_op jit(solution)/shard_map/all_to_all | solution.py:241
  40.0 7.5 %shard_map.54 = (f32[512,128]{1,0:T(8,128)}, bf16[528,128]{1,0:T(8,128)(2,1)}, bf16[528,128]{1,0:T(8,128)(2,1)}, bf16[528,128]{1,0:T(8,128)(2,1)}) custom-call(s32[2]{0:T(128)} %copy-done.7, bf16[4,512,128]{2,1,0:T(8,128)(2,1)} %copy-done.4, bf16[512,128]{1,0:T(8,128)(2,1)} %copy-done.2, bf16[512,128]{1,0:T(8,128)(2,1)} %copy-done.3, ...), custom_call_target="tpu_custom_call" | custom-call | flops 2415919104 | bytes 12582912 | tf_op jit(solution)/shard_map/pallas_call | solution.py:243
  47.6 11.4 %all-to-all-done.in_ref = bf16[64,64,128]{2,1,0:T(8,128)(2,1)S(1)} async-done(((bf16[64,64,128]{2,1,0:T(8,128)(2,1)}), bf16[64,64,128]{2,1,0:T(8,128)(2,1)S(1)}, u32[]{:S(2)}, u32[]{:S(2)}) %all-to-all-start) | async-done | bytes 1048608 | tf_op jit(solution)/shard_map/all_to_all | solution.py:241
  59.0 0.9 %copy-done = f32[512,128]{1,0:T(8,128)S(1)} copy-done((f32[512,128]{1,0:T(8,128)S(1)}, f32[512,128]{1,0:T(8,128)}, u32[]{:S(2)}) %copy-start) | copy-done | bytes 262168
  60.0 2.3 %shard_map.56 = bf16[16,256,128]{2,1,0:T(8,128)(2,1)} custom-call(bf16[64,64,128]{2,1,0:T(8,128)(2,1)S(1)} %all-to-all-done.in_ref, f32[512,128]{1,0:T(8,128)S(1)} %copy-done), custom_call_target="tpu_custom_call" | custom-call | bytes 1048576 | tf_op jit(solution)/shard_map/pallas_call | solution.py:251
  62.2 3.7 %all-to-all-start.1 = ((bf16[16,256,128]{2,1,0:T(8,128)(2,1)}), bf16[16,256,128]{2,1,0:T(8,128)(2,1)S(1)}, u32[]{:S(2)}, u32[]{:S(2)}) async-start(bf16[16,256,128]{2,1,0:T(8,128)(2,1)} %shard_map.56), calls=%async_computation.1 | async-start | bytes 2097152 | tf_op jit(solution)/shard_map/all_to_all | solution.py:254
  65.9 0.6 collective-permute-start.8
  66.6 2.7 %collective-permute-start.9 = (bf16[528,128]{1,0:T(8,128)(2,1)}, bf16[528,128]{1,0:T(8,128)(2,1)S(1)}, u32[]{:S(2)}, u32[]{:S(2)}) collective-permute-start(bf16[528,128]{1,0:T(8,128)(2,1)} %get-tuple-element.22), channel_id=1, source_target_pairs={{0,6},{1,7},{2,0},{3,1},{4,2},{5,3},{6,4},{7,5},{8,14},{9,15},{10,... | collective-permute-start | bytes 405512 | tf_op jit(solution)/shard_map/ppermute | solution.py:216
  69.2 4.6 %collective-permute-done.8.refs_0_ = bf16[528,128]{1,0:T(8,128)(2,1)S(1)} collective-permute-done((bf16[528,128]{1,0:T(8,128)(2,1)}, bf16[528,128]{1,0:T(8,128)(2,1)S(1)}, u32[]{:S(2)}, u32[]{:S(2)}) %collective-permute-start.8) | collective-permute-done | bytes 135200 | tf_op jit(solution)/shard_map/ppermute | solution.py:216
  73.9 2.1 %collective-permute-done.10.refs_2_ = bf16[528,128]{1,0:T(8,128)(2,1)S(1)} collective-permute-done((bf16[528,128]{1,0:T(8,128)(2,1)}, bf16[528,128]{1,0:T(8,128)(2,1)S(1)}, u32[]{:S(2)}, u32[]{:S(2)}) %collective-permute-start.10) | collective-permute-done | bytes 135200 | tf_op jit(solution)/shard_map/ppermute | solution.py:216
  75.9 0.9 %copy-done.1 = f32[512,128]{1,0:T(8,128)S(1)} copy-done((f32[512,128]{1,0:T(8,128)S(1)}, f32[512,128]{1,0:T(8,128)}, u32[]{:S(2)}) %copy-start.1) | copy-done | bytes 262168
  76.9 1.6 %shard_map.55 = f32[4,512,32]{2,1,0:T(8,128)} custom-call(f32[512,128]{1,0:T(8,128)S(1)} %copy-done.1, bf16[528,128]{1,0:T(8,128)(2,1)S(1)} %collective-permute-done.8.refs_0_, bf16[528,128]{1,0:T(8,128)(2,1)S(1)} %collective-permute-done.9.refs_1_, bf16[528,128]{1,0:T(8,128)(2,1)S(1)} %collective-permute-done.10.refs_2_), custom_call_target="tpu_custom_call" | custom-call | bytes 1048576 | tf_op jit(solution)/shard_map/pallas_call | solution.py:256
  78.5 3.3 %all-to-all-done.1.in_ref = bf16[16,256,128]{2,1,0:T(8,128)(2,1)S(1)} async-done(((bf16[16,256,128]{2,1,0:T(8,128)(2,1)}), bf16[16,256,128]{2,1,0:T(8,128)(2,1)S(1)}, u32[]{:S(2)}, u32[]{:S(2)}) %all-to-all-start.1) | async-done | bytes 1048608 | tf_op jit(solution)/shard_map/all_to_all | solution.py:254
  81.9 2.1 %shard_map.57 = f32[27,32,512]{2,1,0:T(8,128)} custom-call(bf16[16,256,128]{2,1,0:T(8,128)(2,1)S(1)} %all-to-all-done.1.in_ref), custom_call_target="tpu_custom_call" | custom-call | bytes 1048576 | tf_op jit(solution)/shard_map/pallas_call | solution.py:255
  (20 shorter events, 0.0 us)
Async XLA Ops:
  0.6 5.4 %collective-permute-start = (bf16[4,512,64]{2,1,0:T(8,128)(2,1)}, bf16[4,512,64]{2,1,0:T(8,128)(2,1)S(1)}, u32[]{:S(2)}, u32[]{:S(2)}) collective-permute-start(bf16[4,512,64]{2,1,0:T(8,128)(2,1)} %bitcast.13), channel_id=1, source_target_pairs={{0,1},{1,0},{2,3},{3,2},{4,5},{5,4},{6,7},{7,6},{8,9},{9,8},{10,11... | collective-permute-start | bytes 786440 | tf_op jit(solution)/shard_map/ppermute | solution.py:216
  0.7 13.4 %collective-permute-start.6 = (bf16[4,64,256]{2,1,0:T(8,128)(2,1)}, bf16[4,64,256]{2,1,0:T(8,128)(2,1)S(1)}, u32[]{:S(2)}, u32[]{:S(2)}) collective-permute-start(bf16[4,64,256]{2,1,0:T(8,128)(2,1)} %bitcast.15), channel_id=1, source_target_pairs={{0,4},{1,5},{2,6},{3,7},{4,0},{5,1},{6,2},{7,3},{8,12},{9,13},{10,... | collective-permute-start | bytes 393224 | tf_op jit(solution)/shard_map/ppermute | solution.py:216
  3.9 10.2 %collective-permute-start.5 = (bf16[4,64,256]{2,1,0:T(8,128)(2,1)}, bf16[4,64,256]{2,1,0:T(8,128)(2,1)S(1)}, u32[]{:S(2)}, u32[]{:S(2)}) collective-permute-start(bf16[4,64,256]{2,1,0:T(8,128)(2,1)} %bitcast.16), channel_id=1, source_target_pairs={{0,6},{1,7},{2,0},{3,1},{4,2},{5,3},{6,4},{7,5},{8,14},{9,15},{10,... | collective-permute-start | bytes 393224 | tf_op jit(solution)/shard_map/ppermute | solution.py:216
  5.1 9.1 %collective-permute-start.4 = (bf16[4,64,256]{2,1,0:T(8,128)(2,1)}, bf16[4,64,256]{2,1,0:T(8,128)(2,1)S(1)}, u32[]{:S(2)}, u32[]{:S(2)}) collective-permute-start(bf16[4,64,256]{2,1,0:T(8,128)(2,1)} %bitcast.17), channel_id=1, source_target_pairs={{0,2},{1,3},{2,4},{3,5},{4,6},{5,7},{6,0},{7,1},{8,10},{9,11},{10,... | collective-permute-start | bytes 393224 | tf_op jit(solution)/shard_map/ppermute | solution.py:216
  6.0 22.1 %copy-start.7 = (s32[2]{0:T(128)}, s32[2]{0:T(128)S(1)}, u32[]{:S(2)}) copy-start(s32[2]{0:T(128)S(1)} %pad_add_fusion.at_ref) | copy-start | bytes 28
  6.0 1.0 %copy-start.5 = (bf16[1,4,16,32,64]{4,3,2,1,0:T(8,128)(2,1)S(1)}, bf16[1,4,16,32,64]{4,3,2,1,0:T(8,128)(2,1)}, u32[]{:S(2)}) copy-start(bf16[1,4,16,32,64]{4,3,2,1,0:T(8,128)(2,1)} %param.4) | copy-start | bytes 786436
  7.1 0.9 %copy-start.6 = (bf16[1,4,2,32,256]{4,3,2,1,0:T(8,128)(2,1)S(1)}, bf16[1,4,2,32,256]{4,3,2,1,0:T(8,128)(2,1)}, u32[]{:S(2)}) copy-start(bf16[1,4,2,32,256]{4,3,2,1,0:T(8,128)(2,1)} %param.3) | copy-start | bytes 393220
  9.0 19.1 %copy-start.4 = (bf16[4,512,128]{2,1,0:T(8,128)(2,1)}, bf16[4,512,128]{2,1,0:T(8,128)(2,1)S(1)}, u32[]{:S(2)}) copy-start(bf16[4,512,128]{2,1,0:T(8,128)(2,1)S(1)} %get-tuple-element.13.panel_ref) | copy-start | bytes 1572868
  9.0 6.3 %collective-permute-start.1 = (bf16[512,128]{1,0:T(8,128)(2,1)S(1)}, bf16[512,128]{1,0:T(8,128)(2,1)S(1)}, u32[]{:S(2)}, u32[]{:S(2)}) collective-permute-start(bf16[512,128]{1,0:T(8,128)(2,1)S(1)} %get-tuple-element.14), channel_id=1, source_target_pairs={{0,8},{8,16},{16,24},{24,32},{32,40},{40,48},{48,56},{1,9},{9,17},... | collective-permute-start | bytes 393224 | tf_op jit(solution)/shard_map/ppermute | solution.py:228
  12.8 6.9 %collective-permute-start.2 = (bf16[512,128]{1,0:T(8,128)(2,1)S(1)}, bf16[512,128]{1,0:T(8,128)(2,1)S(1)}, u32[]{:S(2)}, u32[]{:S(2)}) collective-permute-start(bf16[512,128]{1,0:T(8,128)(2,1)S(1)} %get-tuple-element.15), channel_id=1, source_target_pairs={{8,0},{16,8},{24,16},{32,24},{40,32},{48,40},{56,48},{9,1},{17,9},... | collective-permute-start | bytes 393224 | tf_op jit(solution)/shard_map/ppermute | solution.py:229
  15.3 12.8 %copy-start.2 = (bf16[512,128]{1,0:T(8,128)(2,1)}, bf16[512,128]{1,0:T(8,128)(2,1)S(1)}, u32[]{:S(2)}) copy-start(bf16[512,128]{1,0:T(8,128)(2,1)S(1)} %collective-permute-done.1.left_ref._) | copy-start | bytes 393220
  19.7 8.4 %copy-start.3 = (bf16[512,128]{1,0:T(8,128)(2,1)}, bf16[512,128]{1,0:T(8,128)(2,1)S(1)}, u32[]{:S(2)}) copy-start(bf16[512,128]{1,0:T(8,128)(2,1)S(1)} %collective-permute-done.2.right_ref.__) | copy-start | bytes 393220
  20.5 2.0 %collective-permute-start.7 = (bf16[3,4,64,128]{3,2,1,0:T(8,128)(2,1)S(1)}, bf16[3,4,64,128]{3,2,1,0:T(8,128)(2,1)S(1)}, u32[]{:S(2)}, u32[]{:S(2)}) collective-permute-start(bf16[3,4,64,128]{3,2,1,0:T(8,128)(2,1)S(1)} %get-tuple-element.19), channel_id=1, source_target_pairs={{0,1},{1,0},{2,3},{3,2},{4,5},{5,4},{6,7},{7,6},{8,9},{9,8},{10,11... | collective-permute-start | bytes 589832 | tf_op jit(solution)/shard_map/ppermute | solution.py:216
  20.6 1.9 %collective-permute-start.3 = (bf16[4,64,128]{2,1,0:T(8,128)(2,1)S(1)}, bf16[4,64,128]{2,1,0:T(8,128)(2,1)S(1)}, u32[]{:S(2)}, u32[]{:S(2)}) collective-permute-start(bf16[4,64,128]{2,1,0:T(8,128)(2,1)S(1)} %get-tuple-element.17), channel_id=1, source_target_pairs={{0,1},{1,0},{2,3},{3,2},{4,5},{5,4},{6,7},{7,6},{8,9},{9,8},{10,11... | collective-permute-start | bytes 196616 | tf_op jit(solution)/shard_map/ppermute | solution.py:216
  28.1 30.9 %all-to-all-start = ((bf16[64,64,128]{2,1,0:T(8,128)(2,1)}), bf16[64,64,128]{2,1,0:T(8,128)(2,1)S(1)}, u32[]{:S(2)}, u32[]{:S(2)}) async-start(bf16[64,64,128]{2,1,0:T(8,128)(2,1)} %shard_map.53._), calls=%async_computation | async-start | bytes 2097152 | tf_op jit(solution)/shard_map/all_to_all | solution.py:241
  59.0 1.0 %copy-start = (f32[512,128]{1,0:T(8,128)S(1)}, f32[512,128]{1,0:T(8,128)}, u32[]{:S(2)}) copy-start(f32[512,128]{1,0:T(8,128)} %get-tuple-element.20.own_ref._) | copy-start | bytes 786436
  62.2 19.6 %all-to-all-start.1 = ((bf16[16,256,128]{2,1,0:T(8,128)(2,1)}), bf16[16,256,128]{2,1,0:T(8,128)(2,1)S(1)}, u32[]{:S(2)}, u32[]{:S(2)}) async-start(bf16[16,256,128]{2,1,0:T(8,128)(2,1)} %shard_map.56), calls=%async_computation.1 | async-start | bytes 2097152 | tf_op jit(solution)/shard_map/all_to_all | solution.py:254
  65.9 8.0 %collective-permute-start.8 = (bf16[528,128]{1,0:T(8,128)(2,1)}, bf16[528,128]{1,0:T(8,128)(2,1)S(1)}, u32[]{:S(2)}, u32[]{:S(2)}) collective-permute-start(bf16[528,128]{1,0:T(8,128)(2,1)} %get-tuple-element.21), channel_id=1, source_target_pairs={{0,2},{1,3},{2,4},{3,5},{4,6},{5,7},{6,0},{7,1},{8,10},{9,11},{10,... | collective-permute-start | bytes 405512 | tf_op jit(solution)/shard_map/ppermute | solution.py:216
  66.6 7.3 %collective-permute-start.9 = (bf16[528,128]{1,0:T(8,128)(2,1)}, bf16[528,128]{1,0:T(8,128)(2,1)S(1)}, u32[]{:S(2)}, u32[]{:S(2)}) collective-permute-start(bf16[528,128]{1,0:T(8,128)(2,1)} %get-tuple-element.22), channel_id=1, source_target_pairs={{0,6},{1,7},{2,0},{3,1},{4,2},{5,3},{6,4},{7,5},{8,14},{9,15},{10,... | collective-permute-start | bytes 405512 | tf_op jit(solution)/shard_map/ppermute | solution.py:216
  69.2 6.7 %collective-permute-start.10 = (bf16[528,128]{1,0:T(8,128)(2,1)}, bf16[528,128]{1,0:T(8,128)(2,1)S(1)}, u32[]{:S(2)}, u32[]{:S(2)}) collective-permute-start(bf16[528,128]{1,0:T(8,128)(2,1)} %get-tuple-element.23), channel_id=1, source_target_pairs={{0,4},{1,5},{2,6},{3,7},{4,0},{5,1},{6,2},{7,3},{8,12},{9,13},{10,... | collective-permute-start | bytes 405512 | tf_op jit(solution)/shard_map/ppermute | solution.py:216
  75.9 1.0 %copy-start.1 = (f32[512,128]{1,0:T(8,128)S(1)}, f32[512,128]{1,0:T(8,128)}, u32[]{:S(2)}) copy-start(f32[512,128]{1,0:T(8,128)} %get-tuple-element.20.own_ref._) | copy-start | bytes 786436

commit v3 on v2

v3 whole, which is shorter than its diff:
```python
import jax
import jax.numpy as jnp
from jax import lax
from jax.experimental import pallas as pl
from jax.experimental.pallas import tpu as pltpu
from jax.sharding import PartitionSpec as P

F32, BF16 = jnp.float32, jnp.bfloat16
STEPS, BIAS = 249.0, 125.0
TINY = 1024
PAIR = 11070000
VM = pl.BlockSpec(memory_space=pltpu.VMEM)
SM = pl.BlockSpec(memory_space=pltpu.SMEM)
ANY = pl.BlockSpec(memory_space=pl.ANY)
HBM = pl.BlockSpec(memory_space=pltpu.HBM)


def call(body, outs, ins, scratch=(), flops=0, nbytes=1 << 20, mib=4, aliases=None):
    return pl.pallas_call(
        body,
        out_shape=outs,
        in_specs=ins,
        out_specs=jax.tree.map(lambda _: VM, outs),
        scratch_shapes=list(scratch),
        input_output_aliases=aliases or {},
        compiler_params=pltpu.CompilerParams(vmem_limit_bytes=mib << 20),
        cost_estimate=pl.CostEstimate(flops=flops, bytes_accessed=nbytes, transcendentals=0),
    )


def encode(value, exponent):
    size = jnp.abs(value) * jnp.exp2(-exponent) + 1e-30
    code = jnp.exp2(size * lax.rsqrt(size) * STEPS - BIAS)
    return jnp.where(value < 0, -code, code)


def decode(code, exponent):
    q = jnp.log2(jnp.abs(code)) + BIAS
    square = q * q * (jnp.exp2(exponent) / (STEPS * STEPS))
    return jnp.where(code < 0, -square, square)


def top_exponent(most):
    most = jnp.max(jnp.max(most, axis=0, keepdims=True), axis=1, keepdims=True)
    return jnp.ceil(jnp.log2(jnp.maximum(most, 1e-30)))


def chip_panel(core, own, other):
    return jnp.where(core == 0, jnp.concatenate([own, other], axis=1), jnp.concatenate([other, own], axis=1))


def split_channels(core, block, keep_ref, give_ref):
    for p in range(4):
        rows = block[p]
        even = jnp.concatenate([rows[:, 64 * k : 64 * k + 32] for k in range(4)], axis=1)
        odd = jnp.concatenate([rows[:, 64 * k + 32 : 64 * k + 64] for k in range(4)], axis=1)
        keep_ref[p] = jnp.where(core == 0, even, odd)
        give_ref[p] = jnp.where(core == 0, odd, even)


def pack_body(g_ref, panel_ref, low_ref, high_ref):
    for p in range(4):
        panel_ref[p] = jnp.concatenate([g_ref[p, :256], g_ref[p, 256:]], axis=1)
    low_ref[...] = panel_ref[0]
    high_ref[...] = panel_ref[3]


def write_plane(at_ref, own, other, out_ref, lane):
    halves = [chip_panel(at_ref[1], own[:, i : i + 64], other[:, i : i + 64]) for i in (0, 64)]
    block = jnp.concatenate(halves, axis=0)
    edge = jnp.zeros((16, 1, 128), F32)
    blank = jnp.zeros((32, 128), BF16)
    cells = block.astype(F32).reshape(16, 32, 128)
    moved = (
        jnp.concatenate([cells[:, 1:], edge], axis=1).reshape(512, 128).astype(BF16),
        block,
        jnp.concatenate([edge, cells[:, :31]], axis=1).reshape(512, 128).astype(BF16),
    )
    for c in range(3):
        out_ref[c, 0:32, lane : lane + 128] = blank
        out_ref[c, 32:544, lane : lane + 128] = moved[c]
        out_ref[c, 544:576, lane : lane + 128] = blank


def inner_body(at_ref, panel_ref, other_ref, x_ref, out_ref, keep_ref, give_ref, token_ref):
    for p in range(4):
        keep_ref[p] = split_channels(at_ref[1], x_ref[p], True)
        give_ref[p] = split_channels(at_ref[1], x_ref[p], False)
    for p in range(4):
        write_plane(at_ref, panel_ref[p], other_ref[p], out_ref, 128 * p)
    token_ref[...] = jnp.zeros((8, 128), F32)


def write_edges(at_ref, inner_ref, rims, edge_ref):
    edge_ref[0, :, :, 128:] = inner_ref[:, :, :128]
    edge_ref[1, :, :, :128] = inner_ref[:, :, 384:]
    write_plane(at_ref, rims[0][0], rims[1][0], edge_ref.at[0], 0)
    write_plane(at_ref, rims[0][1], rims[1][1], edge_ref.at[1], 128)


def patches(inner_ref, edge_ref, t, i, bc):
    window = slice(64 - 32 * (bc // 3), 576 - 32 * (bc // 3))
    return inner_ref[bc % 3, window, 128:384] if t != i else edge_ref[t, bc % 3, window, :]


def split_channels(core, block, own):
    parts = [
        jnp.concatenate([block[:, 64 * k + 32 * h : 64 * k + 32 * h + 32] for k in range(4)], axis=1) for h in range(2)
    ]
    return jnp.where((core == 0) == own, parts[0], parts[1])


def pair_body(left_ref, right_ref, out_ref):
    out_ref[0] = left_ref[...]
    out_ref[1] = right_ref[...]


def give_body(at_ref, _, *refs):
    for i in range(3):
        for p in range(4):
            refs[3][i, p] = split_channels(at_ref[1], refs[i][p], False)


def kernel_grad_body(spot_ref, at_ref, inner_ref, *refs):
    rims, keep_ref, blocks, own_got_ref, got_ref, out_ref, token_ref, edge_ref, x_ref, xt_ref, sum_ref = (
        refs[:2], refs[2], refs[3:6], *refs[6:]
    )
    write_edges(at_ref, inner_ref, rims, edge_ref)
    for i in range(8):
        for p in range(4):
            if i % 4 == 0:
                part = (own_got_ref if i else keep_ref)[p]
            else:
                part = split_channels(at_ref[1], blocks[i - 1][p], True) if i < 4 else got_ref[i - 5, p]
            rows = pl.ds(pl.multiple_of(512 * (p // 2) + spot_ref[i] * 64, 64), 64)
            x_ref[rows, 128 * (p % 2) : 128 * (p % 2) + 128] = part
    token_ref[...] = jnp.zeros((8, 128), F32)
    for i in range(2):
        xt_ref[128 * i : 128 * (i + 1), :] = x_ref[:, 128 * i : 128 * (i + 1)].T
    most = jnp.zeros((128, 128), F32)
    for bc in range(9):
        prod = jnp.concatenate([
            sum(
                jnp.dot(
                    xt_ref[:, 512 * t : 512 * (t + 1)], patches(inner_ref, edge_ref, t, i, bc), preferred_element_type=F32
                )
                for t in range(2)
            )
            for i in range(2)
        ], axis=1)
        for a in range(3):
            even, odd = 128 * (2 - a), 128 * (3 - a)
            total = (prod[:128, even : even + 128] + prod[128:, odd : odd + 128]) * (32768.0**-0.5)
            sum_ref[9 * a + bc] = total
            most = jnp.maximum(most, jnp.abs(total))
    exponent = top_exponent(most)
    for k in range(27):
        sum_ref[k] = encode(sum_ref[k], exponent)
    stamp = jnp.broadcast_to(exponent, (2, 128))
    for jr in range(4):
        for k in range(4):
            rows = slice(32 * k + 8 * jr, 32 * k + 8 * jr + 8)
            rest = jnp.concatenate([sum_ref[24 + i, rows, :] for i in range(3)], axis=0)
            for jt in range(4):
                tiles = [sum_ref[6 * jt + i, rows, :] for i in range(6)] + [rest[6 * jt : 6 * jt + 6], stamp]
                out_ref[(4 * jr + jt) * 4 + k] = jnp.concatenate(tiles, axis=0).astype(BF16)


def shard_sum_body(in_ref, _, out_ref, sum_ref):
    used = lax.broadcasted_iota(jnp.int32, (56, 128), 0) < 54
    most = jnp.zeros((56, 128), F32)
    for k in range(4):
        total = jnp.zeros((56, 128), F32)
        for j in range(16):
            code = in_ref[4 * j + k].astype(F32)
            total = total + decode(code, code[54:55])
        total = jnp.where(used, total, 0.0)
        sum_ref[k] = total
        most = jnp.maximum(most, jnp.abs(total))
    exponent = top_exponent(most)
    for k in range(4):
        code = jnp.where(used, encode(sum_ref[k], exponent), exponent).astype(BF16)
        for j in range(16):
            out_ref[j, k] = code


def kernel_out_body(in_ref, out_ref):
    for jr in range(4):
        for k in range(4):
            at = (slice(8 * jr, 8 * jr + 8), slice(128 * k, 128 * (k + 1)))
            rest = []
            for jt in range(4):
                code = in_ref[4 * jr + jt, k].astype(F32)
                value = decode(code, code[54:55])
                for i in range(6):
                    out_ref[6 * jt + i, at[0], at[1]] = value[8 * i : 8 * i + 8]
                rest.append(value[48:54])
            rest = jnp.concatenate(rest, axis=0)
            for i in range(3):
                out_ref[24 + i, at[0], at[1]] = rest[8 * i : 8 * i + 8]


def data_grad_body(at_ref, inner_ref, rims_ref, rims_other_ref, weight_ref, _, *refs):
    outs, token_ref, cut_ref, w_ref, edge_ref, sem = refs[:4], *refs[4:9]
    chip, core = at_ref[0], at_ref[1]
    copy = pltpu.make_async_copy(weight_ref.at[:, :, pl.ds(pl.multiple_of(chip * 128, 128), 128)], cut_ref, sem)
    copy.start()
    write_edges(at_ref, inner_ref, (rims_ref, rims_other_ref), edge_ref)
    token_ref[...] = jnp.zeros((8, 128), F32)
    copy.wait()
    none = jnp.zeros((32, 128), BF16)
    for d in range(4):
        rows = pl.ds(pl.multiple_of(64 * lax.rem(chip + d, 4) + 32 * core, 32), 32)
        for bc in range(9):
            for e in range(2):
                for slot in range(4):
                    a = e + 2 - slot
                    lanes = slice(512 * bc + 128 * slot, 512 * bc + 128 * slot + 128)
                    w_ref[128 * e + 32 * d : 128 * e + 32 * d + 32, lanes] = (
                        cut_ref[9 * a + bc, rows, :] if 0 <= a < 3 else none
                    )
    planes = []
    for t in range(2):
        prod = jnp.zeros((512, 256), F32)
        for bc in range(9):
            for i in range(2):
                prod = prod + lax.dot_general(
                    patches(inner_ref, edge_ref, t, i, bc), w_ref[:, 512 * bc + 256 * i : 512 * bc + 256 * i + 256],
                    (((1,), (1,)), ((), ())), preferred_element_type=F32,
                )
        planes += [prod[:, :128], prod[:, 128:]]
    for d, out_ref in enumerate(outs):
        slab = jnp.concatenate([plane[:, 32 * d : 32 * (d + 1)] for plane in planes], axis=1)
        if d == 0:
            out_ref[...] = slab
        else:
            exponent = top_exponent(jnp.abs(slab))
            out_ref[:512, :] = encode(slab, exponent).astype(BF16)
            out_ref[512:, :] = jnp.broadcast_to(exponent, (16, 128)).astype(BF16)


def data_out_body(own_ref, *refs):
    total = own_ref[...]
    for ref in refs[:3]:
        code = ref[...].astype(F32)
        total = total + decode(code[:512], code[512:513])
    for p in range(4):
        refs[3][p] = total[:, 32 * p : 32 * (p + 1)]


def on_device(activations, out_grad, weight):
    column = lax.axis_index("chan")
    chip, core = column // 2, column % 2
    at = jnp.stack([chip, core]).astype(jnp.int32)
    froms = [chip, (chip + 3) % 4, (chip + 1) % 4, (chip + 2) % 4]
    spots = jnp.stack([2 * f + core for f in froms] + [2 * f + 1 - core for f in froms]).astype(jnp.int32)
    struct = jax.ShapeDtypeStruct
    whole = ("samp", "vox", "chan")
    cores = [[8 * j + 2 * k + h for j in range(16) for k in range(4)] for h in range(2)]

    def hop(value, chips, cores):
        return lax.ppermute(
            value, "chan", [(i, ((i // 2 + chips) % 4) * 2 + (i % 2 ^ cores)) for i in range(8)]
        )

    x = activations.reshape(4, 64, 256)
    g = out_grad.reshape(4, 512, 64)
    near = [hop(x, d, 0) for d in (1, 3, 2)]
    rim, token = struct((256, 128), BF16), struct((8, 128), F32)
    panel, low, high = call(pack_body, (struct((4, 256, 128), BF16), rim, rim), [VM])(g)
    left = lax.ppermute(high, "vox", [(i, i + 1) for i in range(7)])
    right = lax.ppermute(low, "vox", [(i + 1, i) for i in range(7)])
    other = hop(panel, 0, 1)
    rims = call(pair_body, struct((2, 256, 128), BF16), [VM, VM], nbytes=PAIR)(left, right)
    rims = [rims, hop(rims, 0, 1)]
    kept = struct((4, 64, 128), BF16)
    inner, keep, own_give, built = call(
        inner_body, (struct((3, 576, 512), BF16), kept, kept, token), [SM, VM, VM, VM], nbytes=TINY
    )(at, panel, other, x)
    own_got = hop(own_give, 0, 1)
    give = call(give_body, struct((3, 4, 64, 128), BF16), [SM, VM] + [VM] * 3, nbytes=TINY)(at, built, *near)
    got = hop(give, 0, 1)

    edges = pltpu.VMEM((2, 3, 576, 256), BF16)
    codes, made = call(
        kernel_grad_body, (struct((64, 56, 128), BF16), token), [SM, SM] + [VM] * 9,
        [edges, pltpu.VMEM((1024, 256), BF16), pltpu.VMEM((256, 1024), BF16), pltpu.VMEM((27, 128, 128), F32)],
        2 * 2304 * 1024 * 512, 12 << 20, 12,
    )(spots, at, inner, *rims, keep, *near, own_got, got)
    swapped = lax.all_to_all(codes, whole, split_axis=0, concat_axis=0, tiled=True, axis_index_groups=cores)
    slab, coded = struct((512, 128), F32), struct((528, 128), BF16)
    *slabs, done = call(
        data_grad_body, (slab, coded, coded, coded, token), [SM] + [VM] * 3 + [HBM, VM],
        [pltpu.VMEM((27, 256, 128), BF16), pltpu.VMEM((256, 4608), BF16), edges, pltpu.SemaphoreType.DMA],
        2 * 2304 * 1024 * 512, 12 << 20, 24,
    )(at, inner, *rims, weight, made)
    shards = call(
        shard_sum_body, struct((16, 4, 56, 128), BF16), [VM, VM], [pltpu.VMEM((4, 56, 128), F32)]
    )(swapped, done)
    final = lax.all_to_all(shards, ("samp", "vox"), split_axis=0, concat_axis=0, tiled=True)
    weight_grad = call(kernel_out_body, struct((27, 32, 512), F32), [VM])(final)
    data_grad = call(data_out_body, struct((4, 512, 32), F32), [VM] * 4)(
        slabs[0], *[hop(slabs[d], d, 0) for d in (1, 3, 2)]
    )
    return data_grad.reshape(1, 4, 16, 32, 32), weight_grad


def solution(mesh):
    placed = (P("samp", "vox", "chan", None, None), P("samp", "vox", None, None, "chan"), P())
    return jax.shard_map(
        on_device,
        mesh=mesh,
        in_specs=placed,
        out_specs=(P("samp", "vox", None, None, "chan"), P(None, "chan", None)),
        check_vma=False,
    )
```

time: 84.5 us -> 75.8 us (0.90)
  Pallas kernels: 22.2 us -> 16.7 us
  waiting for transfers between devices: 27.1 us -> 22.6 us
  local copies, waits for them, and re-layouts: 3.95 us -> 6.61 us
  starting transfers between devices: 29.9 us -> 28.5 us
    pallas_call x6 -> x7, Pallas kernels: 18.5 us -> 13.5 us  [the longest x1 5.2 us: on_device(): call(data_grad_body, (slab, coded, coded, coded, token), [SM] + [VM] * 3...]
    unnamed x16 -> x12, local copies, waits for them, and re-layouts: 3.86 us -> 6.52 us
    ppermute x1, waiting for transfers between devices: 4.36 us -> 1.88 us  [on_device(): right = lax.ppermute(low, 'vox', [(i + 1, i) for i in range(7)])]
    all_to_all x1, waiting for transfers between devices: 11.4 us -> 9.1 us  [on_device(): lax.all_to_all(codes, whole, split_axis=0, concat_axis=0, tiled=True, axi...]
    ppermute x1, waiting for transfers between devices: 1.16 us -> 0.01 us  [on_device(): left = lax.ppermute(high, 'vox', [(i, i + 1) for i in range(7)])]
    ppermute x9 -> x10, waiting for transfers between devices: 6.74 us -> 7.77 us  [hop(): lax.ppermute(value, 'chan', [(i, (i // 2 + chips) % 4 * 2 + (i % 2 ^ core...]
    ppermute x9 -> x10, starting transfers between devices: 9.19 us -> 8.66 us  [hop(): lax.ppermute(value, 'chan', [(i, (i // 2 + chips) % 4 * 2 + (i % 2 ^ core...]
  transfers between devices with their start and end apart: 13 -> 14, of which waited for: 6 -> 8; matrix products, arithmetic and copies ran while one was open for 0% -> 0% of each run, Pallas kernels for 14% -> 11%
where the time goes in v3:
time: 75.8 us; the launch traced here: 75.4 us
  starting transfers between devices  28.5 us (38%)
  waiting for transfers between devices  22.6 us (30%)
  Pallas kernels  16.7 us (22%)
  local copies, waits for them, and re-layouts  6.61 us (9%)
  between operations  0.84 us (1%)
    all_to_all x1, starting transfers between devices, on_device(): lax.all_to_all(codes, whole, split_axis=0, concat_axis=0, tiled=True, axi...  11.1 us
    all_to_all x1, waiting for transfers between devices, on_device(): lax.all_to_all(codes, whole, split_axis=0, concat_axis=0, tiled=True, axi...  9.1 us
    ppermute x10, starting transfers between devices, hop(): lax.ppermute(value, 'chan', [(i, (i // 2 + chips) % 4 * 2 + (i % 2 ^ core...  8.66 us
    ppermute x10, waiting for transfers between devices, hop(): lax.ppermute(value, 'chan', [(i, (i // 2 + chips) % 4 * 2 + (i % 2 ^ core...  7.77 us
    unnamed x12, local copies, waits for them, and re-layouts  6.52 us
    pallas_call x1, Pallas kernels, on_device(): call(data_grad_body, (slab, coded, coded, coded, token), [SM] + [VM] * 3...  5.2 us
    pallas_call x1, Pallas kernels, on_device(): call(kernel_grad_body, (struct((64, 56, 128), BF16), token), [SM, SM] + [...  4.49 us
    all_to_all x1, waiting for transfers between devices, on_device(): lax.all_to_all(shards, ('samp', 'vox'), split_axis=0, concat_axis=0, tile...  3.82 us
  transfers between devices with their start and end apart: 14, of which 8 were waited for; matrix products, arithmetic and copies ran while one was open for 0% of the time, Pallas kernels for 11%

profile of v3, /device:TPU:0, one launch (start us, length us, event | category | flops | bytes accessed | tf_op | source)
XLA Modules:
  0.0 75.4 jit_solution(3774277559434774391)
XLA Ops:
  0.6 1.0 %copy-done.2 = bf16[1,4,16,32,64]{4,3,2,1,0:T(8,128)(2,1)S(1)} copy-done((bf16[1,4,16,32,64]{4,3,2,1,0:T(8,128)(2,1)S(1)}, bf16[1,4,16,32,64]{4,3,2,1,0:T(8,128)(2,1)}, u32[]{:S(2)}) %copy-start.2) | copy-done | bytes 262168
  1.7 0.1 shard_map.50
  1.8 0.1 collective-permute-start
  1.9 1.6 %collective-permute-start.4 = (bf16[4,64,256]{2,1,0:T(8,128)(2,1)}, bf16[4,64,256]{2,1,0:T(8,128)(2,1)S(1)}, u32[]{:S(2)}, u32[]{:S(2)}) collective-permute-start(bf16[4,64,256]{2,1,0:T(8,128)(2,1)} %bitcast.14), channel_id=1, source_target_pairs={{0,2},{1,3},{2,4},{3,5},{4,6},{5,7},{6,0},{7,1},{8,10},{9,11},{10,... | collective-permute-start | bytes 393224 | tf_op jit(solution)/shard_map/ppermute | solution.py:262
  3.6 1.7 %collective-permute-start.5 = (bf16[4,64,256]{2,1,0:T(8,128)(2,1)}, bf16[4,64,256]{2,1,0:T(8,128)(2,1)S(1)}, u32[]{:S(2)}, u32[]{:S(2)}) collective-permute-start(bf16[4,64,256]{2,1,0:T(8,128)(2,1)} %bitcast.15), channel_id=1, source_target_pairs={{0,6},{1,7},{2,0},{3,1},{4,2},{5,3},{6,4},{7,5},{8,14},{9,15},{10,... | collective-permute-start | bytes 393224 | tf_op jit(solution)/shard_map/ppermute | solution.py:262
  5.2 1.9 %collective-permute-start.6 = (bf16[4,64,256]{2,1,0:T(8,128)(2,1)}, bf16[4,64,256]{2,1,0:T(8,128)(2,1)S(1)}, u32[]{:S(2)}, u32[]{:S(2)}) collective-permute-start(bf16[4,64,256]{2,1,0:T(8,128)(2,1)} %bitcast.16), channel_id=1, source_target_pairs={{0,4},{1,5},{2,6},{3,7},{4,0},{5,1},{6,2},{7,3},{8,12},{9,13},{10,... | collective-permute-start | bytes 393224 | tf_op jit(solution)/shard_map/ppermute | solution.py:262
  7.1 3.8 %collective-permute-start.1 = (bf16[256,128]{1,0:T(8,128)(2,1)S(1)}, bf16[256,128]{1,0:T(8,128)(2,1)S(1)}, u32[]{:S(2)}, u32[]{:S(2)}) collective-permute-start(bf16[256,128]{1,0:T(8,128)(2,1)S(1)} %get-tuple-element.18), channel_id=1, source_target_pairs={{0,8},{8,16},{16,24},{24,32},{32,40},{40,48},{48,56},{1,9},{9,17},... | collective-permute-start | bytes 196616 | tf_op jit(solution)/shard_map/ppermute | solution.py:271
  11.0 1.3 %collective-permute-start.2 = (bf16[256,128]{1,0:T(8,128)(2,1)S(1)}, bf16[256,128]{1,0:T(8,128)(2,1)S(1)}, u32[]{:S(2)}, u32[]{:S(2)}) collective-permute-start(bf16[256,128]{1,0:T(8,128)(2,1)S(1)} %get-tuple-element.19), channel_id=1, source_target_pairs={{8,0},{16,8},{24,16},{32,24},{40,32},{48,40},{56,48},{9,1},{17,9},... | collective-permute-start | bytes 196616 | tf_op jit(solution)/shard_map/ppermute | solution.py:272
  12.3 0.9 %copy-done.3 = bf16[1,4,2,32,256]{4,3,2,1,0:T(8,128)(2,1)S(1)} copy-done((bf16[1,4,2,32,256]{4,3,2,1,0:T(8,128)(2,1)S(1)}, bf16[1,4,2,32,256]{4,3,2,1,0:T(8,128)(2,1)}, u32[]{:S(2)}) %copy-start.3) | copy-done | bytes 131096
  13.2 1.1 %shard_map.51 = (bf16[3,576,512]{2,1,0:T(8,128)(2,1)S(1)}, bf16[4,64,128]{2,1,0:T(8,128)(2,1)S(1)}, bf16[4,64,128]{2,1,0:T(8,128)(2,1)S(1)}, f32[8,128]{1,0:T(8,128)S(1)}) custom-call(s32[2]{0:T(128)S(1)} %pad_add_fusion.at_ref, bf16[4,256,128]{2,1,0:T(8,128)(2,1)S(1)} %get-tuple-element.16.panel_ref, ...), custom_call_target="tpu_custom_call" | custom-call | bytes 1024 | tf_op jit(solution)/shard_map/pallas_call | solution.py:277
  14.4 0.8 %shard_map.53 = bf16[3,4,64,128]{3,2,1,0:T(8,128)(2,1)S(1)} custom-call(s32[2]{0:T(128)S(1)} %pad_add_fusion.at_ref, f32[8,128]{1,0:T(8,128)S(1)} %get-tuple-element.22._, bf16[4,64,256]{2,1,0:T(8,128)(2,1)S(1)} %collective-permute-done.4.refs_0_.refs_3_, bf16[4,64,256]{2,1,0:T(8,128)(2,1)S(1)} %collective-permute-done.5.refs_1_.refs_4_, ...), custom_call_target="tpu_custom_call" | custom-call | bytes 1024 | tf_op jit(solution)/shard_map/pallas_call | solution.py:281
  15.3 1.9 %collective-permute-done.2.right_ref = bf16[256,128]{1,0:T(8,128)(2,1)S(1)} collective-permute-done((bf16[256,128]{1,0:T(8,128)(2,1)S(1)}, bf16[256,128]{1,0:T(8,128)(2,1)S(1)}, u32[]{:S(2)}, u32[]{:S(2)}) %collective-permute-start.2) | collective-permute-done | bytes 65568 | tf_op jit(solution)/shard_map/ppermute | solution.py:272
  17.3 0.5 collective-permute-start.7
  17.9 0.8 collective-permute-done.3.refs_1_.rims_other_ref
  18.6 0.1 collective-permute-done.7.refs_6_
  18.7 4.5 %shard_map.54 = (bf16[64,56,128]{2,1,0:T(8,128)(2,1)S(1)}, f32[8,128]{1,0:T(8,128)S(1)}) custom-call(s32[8]{0:T(128)S(1)} %stack.47.spot_ref, s32[2]{0:T(128)S(1)} %pad_add_fusion.at_ref, bf16[3,576,512]{2,1,0:T(8,128)(2,1)S(1)} %get-tuple-element.17.inner_ref, bf16[2,256,128]{2,1,0:T(8,128)(2,1)S(1)} %shard_map.52.refs_0_.rims_ref, ...), custom_call_target="tpu_custom_call" | custom-call | flops 2415919104 | bytes 12582912 | tf_op jit(solution)/shard_map/pallas_call | solution.py:285
  23.2 0.9 %copy-done.1 = bf16[64,56,128]{2,1,0:T(8,128)(2,1)} copy-done((bf16[64,56,128]{2,1,0:T(8,128)(2,1)}, bf16[64,56,128]{2,1,0:T(8,128)(2,1)S(1)}, u32[]{:S(2)}) %copy-start.1) | copy-done | bytes 917528
  24.1 11.1 %all-to-all-start = ((bf16[64,56,128]{2,1,0:T(8,128)(2,1)}), bf16[64,56,128]{2,1,0:T(8,128)(2,1)S(1)}, u32[]{:S(2)}, u32[]{:S(2)}) async-start(bf16[64,56,128]{2,1,0:T(8,128)(2,1)} %copy-done.1), calls=%async_computation | async-start | bytes 1835008 | tf_op jit(solution)/shard_map/all_to_all | solution.py:290
  35.3 3.0 %copy-done = bf16[27,256,512]{2,1,0:T(8,128)(2,1)S(1)} copy-done((bf16[27,256,512]{2,1,0:T(8,128)(2,1)S(1)}, bf16[27,256,512]{2,1,0:T(8,128)(2,1)}, u32[]{:S(2)}) %copy-start) | copy-done | bytes 7077912
  38.3 5.2 %shard_map.55 = (f32[512,128]{1,0:T(8,128)S(1)}, bf16[528,128]{1,0:T(8,128)(2,1)S(1)}, bf16[528,128]{1,0:T(8,128)(2,1)S(1)}, bf16[528,128]{1,0:T(8,128)(2,1)S(1)}, f32[8,128]{1,0:T(8,128)S(1)}) custom-call(s32[2]{0:T(128)S(1)} %pad_add_fusion.at_ref, bf16[3,576,512]{2,1,0:T(8,128)(2,1)S(1)} %get-tuple-element.17.inner_ref, ...), custom_call_target="tpu_custom_call" | custom-call | flops 2415919104 | bytes 12582912 | tf_op jit(solution)/shard_map/pallas_call | solution.py:292
  43.5 0.6 copy-done.4
  44.2 9.1 %all-to-all-done.in_ref = bf16[64,56,128]{2,1,0:T(8,128)(2,1)S(1)} async-done(((bf16[64,56,128]{2,1,0:T(8,128)(2,1)}), bf16[64,56,128]{2,1,0:T(8,128)(2,1)S(1)}, u32[]{:S(2)}, u32[]{:S(2)}) %all-to-all-start) | async-done | bytes 917536 | tf_op jit(solution)/shard_map/all_to_all | solution.py:290
  53.3 1.8 %shard_map.57 = bf16[16,4,56,128]{3,2,1,0:T(8,128)(2,1)} custom-call(bf16[64,56,128]{2,1,0:T(8,128)(2,1)S(1)} %all-to-all-done.in_ref, f32[8,128]{1,0:T(8,128)S(1)} %get-tuple-element.29._), custom_call_target="tpu_custom_call" | custom-call | bytes 1048576 | tf_op jit(solution)/shard_map/pallas_call | solution.py:297
  55.0 3.6 %all-to-all-start.1 = ((bf16[16,4,56,128]{3,2,1,0:T(8,128)(2,1)}), bf16[16,4,56,128]{3,2,1,0:T(8,128)(2,1)S(1)}, u32[]{:S(2)}, u32[]{:S(2)}) async-start(bf16[16,4,56,128]{3,2,1,0:T(8,128)(2,1)} %shard_map.57), calls=%async_computation.1 | async-start | bytes 1835008 | tf_op jit(solution)/shard_map/all_to_all | solution.py:300
  58.7 1.0 %collective-permute-start.10 = (bf16[528,128]{1,0:T(8,128)(2,1)S(1)}, bf16[528,128]{1,0:T(8,128)(2,1)S(1)}, u32[]{:S(2)}, u32[]{:S(2)}) collective-permute-start(bf16[528,128]{1,0:T(8,128)(2,1)S(1)} %copy-done.5), channel_id=1, source_target_pairs={{0,6},{1,7},{2,0},{3,1},{4,2},{5,3},{6,4},{7,5},{8,14},{9,15},{10,... | collective-permute-start | bytes 405512 | tf_op jit(solution)/shard_map/ppermute | solution.py:262
  59.6 1.7 %collective-permute-start.11 = (bf16[528,128]{1,0:T(8,128)(2,1)S(1)}, bf16[528,128]{1,0:T(8,128)(2,1)S(1)}, u32[]{:S(2)}, u32[]{:S(2)}) collective-permute-start(bf16[528,128]{1,0:T(8,128)(2,1)S(1)} %get-tuple-element.27), channel_id=1, source_target_pairs={{0,4},{1,5},{2,6},{3,7},{4,0},{5,1},{6,2},{7,3},{8,12},{9,13},{10,... | collective-permute-start | bytes 405512 | tf_op jit(solution)/shard_map/ppermute | solution.py:262
  61.4 3.1 %collective-permute-done.10.refs_1_ = bf16[528,128]{1,0:T(8,128)(2,1)S(1)} collective-permute-done((bf16[528,128]{1,0:T(8,128)(2,1)S(1)}, bf16[528,128]{1,0:T(8,128)(2,1)S(1)}, u32[]{:S(2)}, u32[]{:S(2)}) %collective-permute-start.10) | collective-permute-done | bytes 135200 | tf_op jit(solution)/shard_map/ppermute | solution.py:262
  64.5 2.4 %collective-permute-done.11.refs_2_ = bf16[528,128]{1,0:T(8,128)(2,1)S(1)} collective-permute-done((bf16[528,128]{1,0:T(8,128)(2,1)S(1)}, bf16[528,128]{1,0:T(8,128)(2,1)S(1)}, u32[]{:S(2)}, u32[]{:S(2)}) %collective-permute-start.11) | collective-permute-done | bytes 135200 | tf_op jit(solution)/shard_map/ppermute | solution.py:262
  66.9 1.4 %collective-permute-done.9.refs_0_ = bf16[528,128]{1,0:T(8,128)(2,1)S(1)} collective-permute-done((bf16[528,128]{1,0:T(8,128)(2,1)S(1)}, bf16[528,128]{1,0:T(8,128)(2,1)S(1)}, u32[]{:S(2)}, u32[]{:S(2)}) %collective-permute-start.9) | collective-permute-done | bytes 135200 | tf_op jit(solution)/shard_map/ppermute | solution.py:262
  68.3 1.4 %shard_map.56 = f32[4,512,32]{2,1,0:T(8,128)} custom-call(f32[512,128]{1,0:T(8,128)S(1)} %get-tuple-element.24.own_ref, bf16[528,128]{1,0:T(8,128)(2,1)S(1)} %collective-permute-done.9.refs_0_, bf16[528,128]{1,0:T(8,128)(2,1)S(1)} %collective-permute-done.10.refs_1_, bf16[528,128]{1,0:T(8,128)(2,1)S(1)} %collective-permute-done.11.refs_2_), custom_call_target="tpu_custom_call" | custom-call | bytes 1048576 | tf_op jit(solution)/shard_map/pallas_call | solution.py:302
  69.8 3.8 %all-to-all-done.1.in_ref = bf16[16,4,56,128]{3,2,1,0:T(8,128)(2,1)S(1)} async-done(((bf16[16,4,56,128]{3,2,1,0:T(8,128)(2,1)}), bf16[16,4,56,128]{3,2,1,0:T(8,128)(2,1)S(1)}, u32[]{:S(2)}, u32[]{:S(2)}) %all-to-all-start.1) | async-done | bytes 917536 | tf_op jit(solution)/shard_map/all_to_all | solution.py:300
  73.6 1.8 %shard_map.58 = f32[27,32,512]{2,1,0:T(8,128)} custom-call(bf16[16,4,56,128]{3,2,1,0:T(8,128)(2,1)S(1)} %all-to-all-done.1.in_ref), custom_call_target="tpu_custom_call" | custom-call | bytes 1048576 | tf_op jit(solution)/shard_map/pallas_call | solution.py:301
  (19 shorter events, 0.4 us)
Async XLA Ops:
  0.6 1.0 %copy-start.2 = (bf16[1,4,16,32,64]{4,3,2,1,0:T(8,128)(2,1)S(1)}, bf16[1,4,16,32,64]{4,3,2,1,0:T(8,128)(2,1)}, u32[]{:S(2)}) copy-start(bf16[1,4,16,32,64]{4,3,2,1,0:T(8,128)(2,1)} %param.4) | copy-start | bytes 786436
  1.8 9.2 %collective-permute-start = (bf16[4,256,128]{2,1,0:T(8,128)(2,1)S(1)}, bf16[4,256,128]{2,1,0:T(8,128)(2,1)S(1)}, u32[]{:S(2)}, u32[]{:S(2)}) collective-permute-start(bf16[4,256,128]{2,1,0:T(8,128)(2,1)S(1)} %get-tuple-element.16.panel_ref), channel_id=1, source_target_pairs={{0,1},{1,0},{2,3},{3,2},{4,5},{5,4},{6,7},{7,6},{8,9},{9,8},{10,11... | collective-permute-start | bytes 786440 | tf_op jit(solution)/shard_map/ppermute | solution.py:262
  1.9 12.4 %collective-permute-start.4 = (bf16[4,64,256]{2,1,0:T(8,128)(2,1)}, bf16[4,64,256]{2,1,0:T(8,128)(2,1)S(1)}, u32[]{:S(2)}, u32[]{:S(2)}) collective-permute-start(bf16[4,64,256]{2,1,0:T(8,128)(2,1)} %bitcast.14), channel_id=1, source_target_pairs={{0,2},{1,3},{2,4},{3,5},{4,6},{5,7},{6,0},{7,1},{8,10},{9,11},{10,... | collective-permute-start | bytes 393224 | tf_op jit(solution)/shard_map/ppermute | solution.py:262
  3.6 10.8 %collective-permute-start.5 = (bf16[4,64,256]{2,1,0:T(8,128)(2,1)}, bf16[4,64,256]{2,1,0:T(8,128)(2,1)S(1)}, u32[]{:S(2)}, u32[]{:S(2)}) collective-permute-start(bf16[4,64,256]{2,1,0:T(8,128)(2,1)} %bitcast.15), channel_id=1, source_target_pairs={{0,6},{1,7},{2,0},{3,1},{4,2},{5,3},{6,4},{7,5},{8,14},{9,15},{10,... | collective-permute-start | bytes 393224 | tf_op jit(solution)/shard_map/ppermute | solution.py:262
  5.2 9.2 %collective-permute-start.6 = (bf16[4,64,256]{2,1,0:T(8,128)(2,1)}, bf16[4,64,256]{2,1,0:T(8,128)(2,1)S(1)}, u32[]{:S(2)}, u32[]{:S(2)}) collective-permute-start(bf16[4,64,256]{2,1,0:T(8,128)(2,1)} %bitcast.16), channel_id=1, source_target_pairs={{0,4},{1,5},{2,6},{3,7},{4,0},{5,1},{6,2},{7,3},{8,12},{9,13},{10,... | collective-permute-start | bytes 393224 | tf_op jit(solution)/shard_map/ppermute | solution.py:262
  7.1 8.2 %collective-permute-start.1 = (bf16[256,128]{1,0:T(8,128)(2,1)S(1)}, bf16[256,128]{1,0:T(8,128)(2,1)S(1)}, u32[]{:S(2)}, u32[]{:S(2)}) collective-permute-start(bf16[256,128]{1,0:T(8,128)(2,1)S(1)} %get-tuple-element.18), channel_id=1, source_target_pairs={{0,8},{8,16},{16,24},{24,32},{32,40},{40,48},{48,56},{1,9},{9,17},... | collective-permute-start | bytes 196616 | tf_op jit(solution)/shard_map/ppermute | solution.py:271
  11.0 6.1 %collective-permute-start.2 = (bf16[256,128]{1,0:T(8,128)(2,1)S(1)}, bf16[256,128]{1,0:T(8,128)(2,1)S(1)}, u32[]{:S(2)}, u32[]{:S(2)}) collective-permute-start(bf16[256,128]{1,0:T(8,128)(2,1)S(1)} %get-tuple-element.19), channel_id=1, source_target_pairs={{8,0},{16,8},{24,16},{32,24},{40,32},{48,40},{56,48},{9,1},{17,9},... | collective-permute-start | bytes 196616 | tf_op jit(solution)/shard_map/ppermute | solution.py:272
  12.3 0.9 %copy-start.3 = (bf16[1,4,2,32,256]{4,3,2,1,0:T(8,128)(2,1)S(1)}, bf16[1,4,2,32,256]{4,3,2,1,0:T(8,128)(2,1)}, u32[]{:S(2)}) copy-start(bf16[1,4,2,32,256]{4,3,2,1,0:T(8,128)(2,1)} %param.3) | copy-start | bytes 393220
  15.2 3.5 %collective-permute-start.8 = (bf16[3,4,64,128]{3,2,1,0:T(8,128)(2,1)S(1)}, bf16[3,4,64,128]{3,2,1,0:T(8,128)(2,1)S(1)}, u32[]{:S(2)}, u32[]{:S(2)}) collective-permute-start(bf16[3,4,64,128]{3,2,1,0:T(8,128)(2,1)S(1)} %shard_map.53), channel_id=1, source_target_pairs={{0,1},{1,0},{2,3},{3,2},{4,5},{5,4},{6,7},{7,6},{8,9},{9,8},{10,11... | collective-permute-start | bytes 589832 | tf_op jit(solution)/shard_map/ppermute | solution.py:262
  17.2 1.4 %collective-permute-start.3 = (bf16[2,256,128]{2,1,0:T(8,128)(2,1)S(1)}, bf16[2,256,128]{2,1,0:T(8,128)(2,1)S(1)}, u32[]{:S(2)}, u32[]{:S(2)}) collective-permute-start(bf16[2,256,128]{2,1,0:T(8,128)(2,1)S(1)} %shard_map.52.refs_0_.rims_ref), channel_id=1, source_target_pairs={{0,1},{1,0},{2,3},{3,2},{4,5},{5,4},{6,7},{7,6},{8,9},{9,8},{10,11... | collective-permute-start | bytes 393224 | tf_op jit(solution)/shard_map/ppermute | solution.py:262
  17.3 1.4 %collective-permute-start.7 = (bf16[4,64,128]{2,1,0:T(8,128)(2,1)S(1)}, bf16[4,64,128]{2,1,0:T(8,128)(2,1)S(1)}, u32[]{:S(2)}, u32[]{:S(2)}) collective-permute-start(bf16[4,64,128]{2,1,0:T(8,128)(2,1)S(1)} %get-tuple-element.21), channel_id=1, source_target_pairs={{0,1},{1,0},{2,3},{3,2},{4,5},{5,4},{6,7},{7,6},{8,9},{9,8},{10,11... | collective-permute-start | bytes 196616 | tf_op jit(solution)/shard_map/ppermute | solution.py:262
  23.2 0.9 %copy-start.1 = (bf16[64,56,128]{2,1,0:T(8,128)(2,1)}, bf16[64,56,128]{2,1,0:T(8,128)(2,1)S(1)}, u32[]{:S(2)}) copy-start(bf16[64,56,128]{2,1,0:T(8,128)(2,1)S(1)} %get-tuple-element.28) | copy-start | bytes 2752516
  24.1 29.1 %all-to-all-start = ((bf16[64,56,128]{2,1,0:T(8,128)(2,1)}), bf16[64,56,128]{2,1,0:T(8,128)(2,1)S(1)}, u32[]{:S(2)}, u32[]{:S(2)}) async-start(bf16[64,56,128]{2,1,0:T(8,128)(2,1)} %copy-done.1), calls=%async_computation | async-start | bytes 1835008 | tf_op jit(solution)/shard_map/all_to_all | solution.py:290
  35.3 3.0 %copy-start = (bf16[27,256,512]{2,1,0:T(8,128)(2,1)S(1)}, bf16[27,256,512]{2,1,0:T(8,128)(2,1)}, u32[]{:S(2)}) copy-start(bf16[27,256,512]{2,1,0:T(8,128)(2,1)} %weight_ref.1) | copy-start | bytes 21233668
  43.5 0.6 copy-start.4
  53.3 5.4 %copy-start.5 = (bf16[528,128]{1,0:T(8,128)(2,1)S(1)}, bf16[528,128]{1,0:T(8,128)(2,1)}, u32[]{:S(2)}) copy-start(bf16[528,128]{1,0:T(8,128)(2,1)} %copy-done.4) | copy-start | bytes 405508
  55.0 18.5 %all-to-all-start.1 = ((bf16[16,4,56,128]{3,2,1,0:T(8,128)(2,1)}), bf16[16,4,56,128]{3,2,1,0:T(8,128)(2,1)S(1)}, u32[]{:S(2)}, u32[]{:S(2)}) async-start(bf16[16,4,56,128]{3,2,1,0:T(8,128)(2,1)} %shard_map.57), calls=%async_computation.1 | async-start | bytes 1835008 | tf_op jit(solution)/shard_map/all_to_all | solution.py:300
  58.7 5.8 %collective-permute-start.10 = (bf16[528,128]{1,0:T(8,128)(2,1)S(1)}, bf16[528,128]{1,0:T(8,128)(2,1)S(1)}, u32[]{:S(2)}, u32[]{:S(2)}) collective-permute-start(bf16[528,128]{1,0:T(8,128)(2,1)S(1)} %copy-done.5), channel_id=1, source_target_pairs={{0,6},{1,7},{2,0},{3,1},{4,2},{5,3},{6,4},{7,5},{8,14},{9,15},{10,... | collective-permute-start | bytes 405512 | tf_op jit(solution)/shard_map/ppermute | solution.py:262
  59.6 7.3 %collective-permute-start.11 = (bf16[528,128]{1,0:T(8,128)(2,1)S(1)}, bf16[528,128]{1,0:T(8,128)(2,1)S(1)}, u32[]{:S(2)}, u32[]{:S(2)}) collective-permute-start(bf16[528,128]{1,0:T(8,128)(2,1)S(1)} %get-tuple-element.27), channel_id=1, source_target_pairs={{0,4},{1,5},{2,6},{3,7},{4,0},{5,1},{6,2},{7,3},{8,12},{9,13},{10,... | collective-permute-start | bytes 405512 | tf_op jit(solution)/shard_map/ppermute | solution.py:262
  61.4 6.9 %collective-permute-start.9 = (bf16[528,128]{1,0:T(8,128)(2,1)S(1)}, bf16[528,128]{1,0:T(8,128)(2,1)S(1)}, u32[]{:S(2)}, u32[]{:S(2)}) collective-permute-start(bf16[528,128]{1,0:T(8,128)(2,1)S(1)} %get-tuple-element.25), channel_id=1, source_target_pairs={{0,2},{1,3},{2,4},{3,5},{4,6},{5,7},{6,0},{7,1},{8,10},{9,11},{10,... | collective-permute-start | bytes 405512 | tf_op jit(solution)/shard_map/ppermute | solution.py:262

commit v4 on v3

--- a/solution.py
+++ b/solution.py
@@ -10,9 +10,12 @@
 TINY = 1024
 PAIR = 11070000
 VM = pl.BlockSpec(memory_space=pltpu.VMEM)
-SM = pl.BlockSpec(memory_space=pltpu.SMEM)
-ANY = pl.BlockSpec(memory_space=pl.ANY)
 HBM = pl.BlockSpec(memory_space=pltpu.HBM)
+
+
+def place():
+    chan = lax.axis_index("chan")
+    return lax.div(chan, 2), lax.rem(chan, 2), lax.rem(lax.axis_index("vox"), 2)
 
 
 def call(body, outs, ins, scratch=(), flops=0, nbytes=1 << 20, mib=4, aliases=None):
@@ -59,14 +62,15 @@
 
 
 def pack_body(g_ref, panel_ref, low_ref, high_ref):
+    odd = place()[2] == 1
     for p in range(4):
         panel_ref[p] = jnp.concatenate([g_ref[p, :256], g_ref[p, 256:]], axis=1)
-    low_ref[...] = panel_ref[0]
-    high_ref[...] = panel_ref[3]
-
-
-def write_plane(at_ref, own, other, out_ref, lane):
-    halves = [chip_panel(at_ref[1], own[:, i : i + 64], other[:, i : i + 64]) for i in (0, 64)]
+    low_ref[...] = jnp.where(odd, panel_ref[3], panel_ref[0])
+    high_ref[...] = jnp.where(odd, panel_ref[0], panel_ref[3])
+
+
+def write_plane(own, other, out_ref, lane):
+    halves = [chip_panel(place()[1], own[:, i : i + 64], other[:, i : i + 64]) for i in (0, 64)]
     block = jnp.concatenate(halves, axis=0)
     edge = jnp.zeros((16, 1, 128), F32)
     blank = jnp.zeros((32, 128), BF16)
@@ -82,20 +86,20 @@
         out_ref[c, 544:576, lane : lane + 128] = blank
 
 
-def inner_body(at_ref, panel_ref, other_ref, x_ref, out_ref, keep_ref, give_ref, token_ref):
-    for p in range(4):
-        keep_ref[p] = split_channels(at_ref[1], x_ref[p], True)
-        give_ref[p] = split_channels(at_ref[1], x_ref[p], False)
-    for p in range(4):
-        write_plane(at_ref, panel_ref[p], other_ref[p], out_ref, 128 * p)
+def inner_body(panel_ref, other_ref, x_ref, out_ref, keep_ref, give_ref, token_ref):
+    for p in range(4):
+        keep_ref[p] = split_channels(place()[1], x_ref[p], True)
+        give_ref[p] = split_channels(place()[1], x_ref[p], False)
+    for p in range(4):
+        write_plane(panel_ref[p], other_ref[p], out_ref, 128 * p)
     token_ref[...] = jnp.zeros((8, 128), F32)
 
 
-def write_edges(at_ref, inner_ref, rims, edge_ref):
+def write_edges(inner_ref, rims, edge_ref):
     edge_ref[0, :, :, 128:] = inner_ref[:, :, :128]
     edge_ref[1, :, :, :128] = inner_ref[:, :, 384:]
-    write_plane(at_ref, rims[0][0], rims[1][0], edge_ref.at[0], 0)
-    write_plane(at_ref, rims[0][1], rims[1][1], edge_ref.at[1], 128)
+    write_plane(rims[0][0], rims[1][0], edge_ref.at[0], 0)
+    write_plane(rims[0][1], rims[1][1], edge_ref.at[1], 128)
 
 
 def patches(inner_ref, edge_ref, t, i, bc):
@@ -110,29 +114,32 @@
     return jnp.where((core == 0) == own, parts[0], parts[1])
 
 
-def pair_body(left_ref, right_ref, out_ref):
-    out_ref[0] = left_ref[...]
-    out_ref[1] = right_ref[...]
-
-
-def give_body(at_ref, _, *refs):
+def pair_body(first_ref, second_ref, out_ref):
+    odd = place()[2] == 1
+    out_ref[0] = jnp.where(odd, second_ref[...], first_ref[...])
+    out_ref[1] = jnp.where(odd, first_ref[...], second_ref[...])
+
+
+def give_body(_, *refs):
     for i in range(3):
         for p in range(4):
-            refs[3][i, p] = split_channels(at_ref[1], refs[i][p], False)
-
-
-def kernel_grad_body(spot_ref, at_ref, inner_ref, *refs):
+            refs[3][i, p] = split_channels(place()[1], refs[i][p], False)
+
+
+def kernel_grad_body(inner_ref, *refs):
     rims, keep_ref, blocks, own_got_ref, got_ref, out_ref, token_ref, edge_ref, x_ref, xt_ref, sum_ref = (
         refs[:2], refs[2], refs[3:6], *refs[6:]
     )
-    write_edges(at_ref, inner_ref, rims, edge_ref)
+    write_edges(inner_ref, rims, edge_ref)
+    chip, core, _ = place()
     for i in range(8):
+        spot = 2 * lax.rem(chip + (0, 3, 1, 2)[i % 4], 4) + (core if i < 4 else 1 - core)
         for p in range(4):
             if i % 4 == 0:
                 part = (own_got_ref if i else keep_ref)[p]
             else:
-                part = split_channels(at_ref[1], blocks[i - 1][p], True) if i < 4 else got_ref[i - 5, p]
-            rows = pl.ds(pl.multiple_of(512 * (p // 2) + spot_ref[i] * 64, 64), 64)
+                part = split_channels(place()[1], blocks[i - 1][p], True) if i < 4 else got_ref[i - 5, p]
+            rows = pl.ds(pl.multiple_of(512 * (p // 2) + spot * 64, 64), 64)
             x_ref[rows, 128 * (p % 2) : 128 * (p % 2) + 128] = part
     token_ref[...] = jnp.zeros((8, 128), F32)
     for i in range(2):
@@ -200,12 +207,12 @@
                 out_ref[24 + i, at[0], at[1]] = rest[8 * i : 8 * i + 8]
 
 
-def data_grad_body(at_ref, inner_ref, rims_ref, rims_other_ref, weight_ref, _, *refs):
+def data_grad_body(inner_ref, rims_ref, rims_other_ref, weight_ref, _, *refs):
     outs, token_ref, cut_ref, w_ref, edge_ref, sem = refs[:4], *refs[4:9]
-    chip, core = at_ref[0], at_ref[1]
+    chip, core, _ = place()
     copy = pltpu.make_async_copy(weight_ref.at[:, :, pl.ds(pl.multiple_of(chip * 128, 128), 128)], cut_ref, sem)
     copy.start()
-    write_edges(at_ref, inner_ref, (rims_ref, rims_other_ref), edge_ref)
+    write_edges(inner_ref, (rims_ref, rims_other_ref), edge_ref)
     token_ref[...] = jnp.zeros((8, 128), F32)
     copy.wait()
     none = jnp.zeros((32, 128), BF16)
@@ -249,11 +256,6 @@
 
 
 def on_device(activations, out_grad, weight):
-    column = lax.axis_index("chan")
-    chip, core = column // 2, column % 2
-    at = jnp.stack([chip, core]).astype(jnp.int32)
-    froms = [chip, (chip + 3) % 4, (chip + 1) % 4, (chip + 2) % 4]
-    spots = jnp.stack([2 * f + core for f in froms] + [2 * f + 1 - core for f in froms]).astype(jnp.int32)
     struct = jax.ShapeDtypeStruct
     whole = ("samp", "vox", "chan")
     cores = [[8 * j + 2 * k + h for j in range(16) for k in range(4)] for h in range(2)]
@@ -268,32 +270,32 @@
     near = [hop(x, d, 0) for d in (1, 3, 2)]
     rim, token = struct((256, 128), BF16), struct((8, 128), F32)
     panel, low, high = call(pack_body, (struct((4, 256, 128), BF16), rim, rim), [VM])(g)
-    left = lax.ppermute(high, "vox", [(i, i + 1) for i in range(7)])
-    right = lax.ppermute(low, "vox", [(i + 1, i) for i in range(7)])
+    left = lax.ppermute(low, "vox", [swap for i in (1, 3, 5) for swap in ((i, i + 1), (i + 1, i))])
+    right = lax.ppermute(high, "vox", [swap for i in (0, 2, 4, 6) for swap in ((i, i + 1), (i + 1, i))])
     other = hop(panel, 0, 1)
     rims = call(pair_body, struct((2, 256, 128), BF16), [VM, VM], nbytes=PAIR)(left, right)
     rims = [rims, hop(rims, 0, 1)]
     kept = struct((4, 64, 128), BF16)
     inner, keep, own_give, built = call(
-        inner_body, (struct((3, 576, 512), BF16), kept, kept, token), [SM, VM, VM, VM], nbytes=TINY
-    )(at, panel, other, x)
+        inner_body, (struct((3, 576, 512), BF16), kept, kept, token), [VM, VM, VM], nbytes=TINY
+    )(panel, other, x)
     own_got = hop(own_give, 0, 1)
-    give = call(give_body, struct((3, 4, 64, 128), BF16), [SM, VM] + [VM] * 3, nbytes=TINY)(at, built, *near)
+    give = call(give_body, struct((3, 4, 64, 128), BF16), [VM] * 4, nbytes=TINY)(built, *near)
     got = hop(give, 0, 1)
 
     edges = pltpu.VMEM((2, 3, 576, 256), BF16)
     codes, made = call(
-        kernel_grad_body, (struct((64, 56, 128), BF16), token), [SM, SM] + [VM] * 9,
+        kernel_grad_body, (struct((64, 56, 128), BF16), token), [VM] * 9,
         [edges, pltpu.VMEM((1024, 256), BF16), pltpu.VMEM((256, 1024), BF16), pltpu.VMEM((27, 128, 128), F32)],
         2 * 2304 * 1024 * 512, 12 << 20, 12,
-    )(spots, at, inner, *rims, keep, *near, own_got, got)
+    )(inner, *rims, keep, *near, own_got, got)
     swapped = lax.all_to_all(codes, whole, split_axis=0, concat_axis=0, tiled=True, axis_index_groups=cores)
     slab, coded = struct((512, 128), F32), struct((528, 128), BF16)
     *slabs, done = call(
-        data_grad_body, (slab, coded, coded, coded, token), [SM] + [VM] * 3 + [HBM, VM],
+        data_grad_body, (slab, coded, coded, coded, token), [VM] * 3 + [HBM, VM],
         [pltpu.VMEM((27, 256, 128), BF16), pltpu.VMEM((256, 4608), BF16), edges, pltpu.SemaphoreType.DMA],
         2 * 2304 * 1024 * 512, 12 << 20, 24,
-    )(at, inner, *rims, weight, made)
+    )(inner, *rims, weight, made)
     shards = call(
         shard_sum_body, struct((16, 4, 56, 128), BF16), [VM, VM], [pltpu.VMEM((4, 56, 128), F32)]
     )(swapped, done)

time: 75.8 us -> 72.3 us (0.954)
  Pallas kernels: 16.7 us -> 14.6 us
  waiting for transfers between devices: 22.6 us -> 21.5 us
    pallas_call x4, Pallas kernels: 11.6 us -> 9.43 us  [the longest x1 4.66 us: on_device(): call(data_grad_body, (slab, coded, coded, coded, token), [VM] * 3 + [HBM,...]
    ppermute x2, waiting for transfers between devices: 1.89 us -> 0.36 us  [the longest x1 0.36 us: on_device(): lax.ppermute(high, 'vox', [swap for i in (0, 2, 4, 6) for swap in ((i, i...]
  transfers between devices with their start and end apart: 14 -> 14, of which waited for: 8 -> 8; matrix products, arithmetic and copies ran while one was open for 0% -> 0% of each run, Pallas kernels for 11% -> 10%
where the time goes in v4:
time: 72.3 us; the launch traced here: 71.9 us
  starting transfers between devices  28.5 us (39%)
  waiting for transfers between devices  21.5 us (30%)
  Pallas kernels  14.6 us (20%)
  local copies, waits for them, and re-layouts  6.53 us (9%)
  between operations  0.81 us (1%)
    all_to_all x1, starting transfers between devices, on_device(): lax.all_to_all(codes, whole, split_axis=0, concat_axis=0, tiled=True, axi...  10.4 us
    all_to_all x1, waiting for transfers between devices, on_device(): lax.all_to_all(codes, whole, split_axis=0, concat_axis=0, tiled=True, axi...  9.46 us
    ppermute x10, starting transfers between devices, hop(): lax.ppermute(value, 'chan', [(i, (i // 2 + chips) % 4 * 2 + (i % 2 ^ core...  8.67 us
    ppermute x10, waiting for transfers between devices, hop(): lax.ppermute(value, 'chan', [(i, (i // 2 + chips) % 4 * 2 + (i % 2 ^ core...  7.85 us
    unnamed x12, local copies, waits for them, and re-layouts  6.53 us
    ppermute x1, starting transfers between devices, on_device(): lax.ppermute(high, 'vox', [swap for i in (0, 2, 4, 6) for swap in ((i, i...  5.16 us
    pallas_call x1, Pallas kernels, on_device(): call(data_grad_body, (slab, coded, coded, coded, token), [VM] * 3 + [HBM,...  4.66 us
    pallas_call x1, Pallas kernels, on_device(): call(kernel_grad_body, (struct((64, 56, 128), BF16), token), [VM] * 9, [e...  3.94 us
  transfers between devices with their start and end apart: 14, of which 8 were waited for; matrix products, arithmetic and copies ran while one was open for 0% of the time, Pallas kernels for 10%

profile of v4, /device:TPU:0, one launch (start us, length us, event | category | flops | bytes accessed | tf_op | source)
XLA Modules:
  0.0 71.9 jit_solution(2425745942684682710)
XLA Ops:
  0.6 1.0 %copy-done.2 = bf16[1,4,16,32,64]{4,3,2,1,0:T(8,128)(2,1)S(1)} copy-done((bf16[1,4,16,32,64]{4,3,2,1,0:T(8,128)(2,1)S(1)}, bf16[1,4,16,32,64]{4,3,2,1,0:T(8,128)(2,1)}, u32[]{:S(2)}) %copy-start.2) | copy-done | bytes 262168
  1.7 0.1 shard_map.50
  1.9 1.6 %collective-permute-start.4 = (bf16[4,64,256]{2,1,0:T(8,128)(2,1)}, bf16[4,64,256]{2,1,0:T(8,128)(2,1)S(1)}, u32[]{:S(2)}, u32[]{:S(2)}) collective-permute-start(bf16[4,64,256]{2,1,0:T(8,128)(2,1)} %bitcast.4), channel_id=1, source_target_pairs={{0,2},{1,3},{2,4},{3,5},{4,6},{5,7},{6,0},{7,1},{8,10},{9,11},{10,... | collective-permute-start | bytes 393224 | tf_op jit(solution)/shard_map/ppermute | solution.py:264
  3.6 1.7 %collective-permute-start.5 = (bf16[4,64,256]{2,1,0:T(8,128)(2,1)}, bf16[4,64,256]{2,1,0:T(8,128)(2,1)S(1)}, u32[]{:S(2)}, u32[]{:S(2)}) collective-permute-start(bf16[4,64,256]{2,1,0:T(8,128)(2,1)} %bitcast.5), channel_id=1, source_target_pairs={{0,6},{1,7},{2,0},{3,1},{4,2},{5,3},{6,4},{7,5},{8,14},{9,15},{10,... | collective-permute-start | bytes 393224 | tf_op jit(solution)/shard_map/ppermute | solution.py:264
  5.2 1.9 %collective-permute-start.6 = (bf16[4,64,256]{2,1,0:T(8,128)(2,1)}, bf16[4,64,256]{2,1,0:T(8,128)(2,1)S(1)}, u32[]{:S(2)}, u32[]{:S(2)}) collective-permute-start(bf16[4,64,256]{2,1,0:T(8,128)(2,1)} %bitcast.6), channel_id=1, source_target_pairs={{0,4},{1,5},{2,6},{3,7},{4,0},{5,1},{6,2},{7,3},{8,12},{9,13},{10,... | collective-permute-start | bytes 393224 | tf_op jit(solution)/shard_map/ppermute | solution.py:264
  7.1 0.7 collective-permute-start.1
  7.8 5.2 %collective-permute-start.2 = (bf16[256,128]{1,0:T(8,128)(2,1)S(1)}, bf16[256,128]{1,0:T(8,128)(2,1)S(1)}, u32[]{:S(2)}, u32[]{:S(2)}) collective-permute-start(bf16[256,128]{1,0:T(8,128)(2,1)S(1)} %get-tuple-element.19), channel_id=1, source_target_pairs={{0,8},{8,0},{16,24},{24,16},{32,40},{40,32},{48,56},{56,48},{1,9},... | collective-permute-start | bytes 196616 | tf_op jit(solution)/shard_map/ppermute | solution.py:274
  13.0 0.9 %copy-done.3 = bf16[1,4,2,32,256]{4,3,2,1,0:T(8,128)(2,1)S(1)} copy-done((bf16[1,4,2,32,256]{4,3,2,1,0:T(8,128)(2,1)S(1)}, bf16[1,4,2,32,256]{4,3,2,1,0:T(8,128)(2,1)}, u32[]{:S(2)}) %copy-start.3) | copy-done | bytes 131096
  13.9 0.6 shard_map.51
  14.5 0.3 shard_map.53
  14.8 0.4 collective-permute-done.2.second_ref
  15.2 0.2 collective-permute-start.3
  15.4 0.4 collective-permute-start.7
  15.8 0.8 %collective-permute-done.3.refs_1_.rims_other_ref = bf16[2,256,128]{2,1,0:T(8,128)(2,1)S(1)} collective-permute-done((bf16[2,256,128]{2,1,0:T(8,128)(2,1)S(1)}, bf16[2,256,128]{2,1,0:T(8,128)(2,1)S(1)}, u32[]{:S(2)}, u32[]{:S(2)}) %collective-permute-start.3) | collective-permute-done | bytes 131104 | tf_op jit(solution)/shard_map/ppermute | solution.py:264
  16.7 0.1 collective-permute-done.7.refs_6_
  16.8 3.9 %shard_map.54 = (bf16[64,56,128]{2,1,0:T(8,128)(2,1)S(1)}, f32[8,128]{1,0:T(8,128)S(1)}) custom-call(bf16[3,576,512]{2,1,0:T(8,128)(2,1)S(1)} %get-tuple-element.17.inner_ref, bf16[2,256,128]{2,1,0:T(8,128)(2,1)S(1)} %shard_map.52.refs_0_.rims_ref, bf16[2,256,128]{2,1,0:T(8,128)(2,1)S(1)} %collective-permute-done.3.refs_1_.rims_other_ref, ...), custom_call_target="tpu_custom_call" | custom-call | flops 2415919104 | bytes 12582912 | tf_op jit(solution)/shard_map/pallas_call | solution.py:287
  20.7 0.9 %copy-done.1 = bf16[64,56,128]{2,1,0:T(8,128)(2,1)} copy-done((bf16[64,56,128]{2,1,0:T(8,128)(2,1)}, bf16[64,56,128]{2,1,0:T(8,128)(2,1)S(1)}, u32[]{:S(2)}) %copy-start.1) | copy-done | bytes 917528
  21.6 10.4 %all-to-all-start = ((bf16[64,56,128]{2,1,0:T(8,128)(2,1)}), bf16[64,56,128]{2,1,0:T(8,128)(2,1)S(1)}, u32[]{:S(2)}, u32[]{:S(2)}) async-start(bf16[64,56,128]{2,1,0:T(8,128)(2,1)} %copy-done.1), calls=%async_computation | async-start | bytes 1835008 | tf_op jit(solution)/shard_map/all_to_all | solution.py:292
  32.0 3.0 %copy-done = bf16[27,256,512]{2,1,0:T(8,128)(2,1)S(1)} copy-done((bf16[27,256,512]{2,1,0:T(8,128)(2,1)S(1)}, bf16[27,256,512]{2,1,0:T(8,128)(2,1)}, u32[]{:S(2)}) %copy-start) | copy-done | bytes 7077912
  35.0 4.7 %shard_map.55 = (f32[512,128]{1,0:T(8,128)S(1)}, bf16[528,128]{1,0:T(8,128)(2,1)S(1)}, bf16[528,128]{1,0:T(8,128)(2,1)S(1)}, bf16[528,128]{1,0:T(8,128)(2,1)S(1)}, f32[8,128]{1,0:T(8,128)S(1)}) custom-call(bf16[3,576,512]{2,1,0:T(8,128)(2,1)S(1)} %get-tuple-element.17.inner_ref, bf16[2,256,128]{2,1,0:T(8,128)(2,1)S(1)} %shard_map.52.refs_0_.rims_ref, ...), custom_call_target="tpu_custom_call" | custom-call | flops 2415919104 | bytes 12582912 | tf_op jit(solution)/shard_map/pallas_call | solution.py:294
  39.7 0.6 copy-done.4
  40.4 9.5 %all-to-all-done.in_ref = bf16[64,56,128]{2,1,0:T(8,128)(2,1)S(1)} async-done(((bf16[64,56,128]{2,1,0:T(8,128)(2,1)}), bf16[64,56,128]{2,1,0:T(8,128)(2,1)S(1)}, u32[]{:S(2)}, u32[]{:S(2)}) %all-to-all-start) | async-done | bytes 917536 | tf_op jit(solution)/shard_map/all_to_all | solution.py:292
  49.8 1.8 %shard_map.57 = bf16[16,4,56,128]{3,2,1,0:T(8,128)(2,1)} custom-call(bf16[64,56,128]{2,1,0:T(8,128)(2,1)S(1)} %all-to-all-done.in_ref, f32[8,128]{1,0:T(8,128)S(1)} %get-tuple-element.29._), custom_call_target="tpu_custom_call" | custom-call | bytes 1048576 | tf_op jit(solution)/shard_map/pallas_call | solution.py:299
  51.6 3.6 %all-to-all-start.1 = ((bf16[16,4,56,128]{3,2,1,0:T(8,128)(2,1)}), bf16[16,4,56,128]{3,2,1,0:T(8,128)(2,1)S(1)}, u32[]{:S(2)}, u32[]{:S(2)}) async-start(bf16[16,4,56,128]{3,2,1,0:T(8,128)(2,1)} %shard_map.57), calls=%async_computation.1 | async-start | bytes 1835008 | tf_op jit(solution)/shard_map/all_to_all | solution.py:302
  55.2 1.0 %collective-permute-start.10 = (bf16[528,128]{1,0:T(8,128)(2,1)S(1)}, bf16[528,128]{1,0:T(8,128)(2,1)S(1)}, u32[]{:S(2)}, u32[]{:S(2)}) collective-permute-start(bf16[528,128]{1,0:T(8,128)(2,1)S(1)} %copy-done.5), channel_id=1, source_target_pairs={{0,6},{1,7},{2,0},{3,1},{4,2},{5,3},{6,4},{7,5},{8,14},{9,15},{10,... | collective-permute-start | bytes 405512 | tf_op jit(solution)/shard_map/ppermute | solution.py:264
  56.2 1.7 %collective-permute-start.11 = (bf16[528,128]{1,0:T(8,128)(2,1)S(1)}, bf16[528,128]{1,0:T(8,128)(2,1)S(1)}, u32[]{:S(2)}, u32[]{:S(2)}) collective-permute-start(bf16[528,128]{1,0:T(8,128)(2,1)S(1)} %get-tuple-element.27), channel_id=1, source_target_pairs={{0,4},{1,5},{2,6},{3,7},{4,0},{5,1},{6,2},{7,3},{8,12},{9,13},{10,... | collective-permute-start | bytes 405512 | tf_op jit(solution)/shard_map/ppermute | solution.py:264
  57.9 3.1 %collective-permute-done.10.refs_1_ = bf16[528,128]{1,0:T(8,128)(2,1)S(1)} collective-permute-done((bf16[528,128]{1,0:T(8,128)(2,1)S(1)}, bf16[528,128]{1,0:T(8,128)(2,1)S(1)}, u32[]{:S(2)}, u32[]{:S(2)}) %collective-permute-start.10) | collective-permute-done | bytes 135200 | tf_op jit(solution)/shard_map/ppermute | solution.py:264
  61.1 2.4 %collective-permute-done.11.refs_2_ = bf16[528,128]{1,0:T(8,128)(2,1)S(1)} collective-permute-done((bf16[528,128]{1,0:T(8,128)(2,1)S(1)}, bf16[528,128]{1,0:T(8,128)(2,1)S(1)}, u32[]{:S(2)}, u32[]{:S(2)}) %collective-permute-start.11) | collective-permute-done | bytes 135200 | tf_op jit(solution)/shard_map/ppermute | solution.py:264
  63.5 1.4 %collective-permute-done.9.refs_0_ = bf16[528,128]{1,0:T(8,128)(2,1)S(1)} collective-permute-done((bf16[528,128]{1,0:T(8,128)(2,1)S(1)}, bf16[528,128]{1,0:T(8,128)(2,1)S(1)}, u32[]{:S(2)}, u32[]{:S(2)}) %collective-permute-start.9) | collective-permute-done | bytes 135200 | tf_op jit(solution)/shard_map/ppermute | solution.py:264
  64.8 1.4 %shard_map.56 = f32[4,512,32]{2,1,0:T(8,128)} custom-call(f32[512,128]{1,0:T(8,128)S(1)} %get-tuple-element.24.own_ref, bf16[528,128]{1,0:T(8,128)(2,1)S(1)} %collective-permute-done.9.refs_0_, bf16[528,128]{1,0:T(8,128)(2,1)S(1)} %collective-permute-done.10.refs_1_, bf16[528,128]{1,0:T(8,128)(2,1)S(1)} %collective-permute-done.11.refs_2_), custom_call_target="tpu_custom_call" | custom-call | bytes 1048576 | tf_op jit(solution)/shard_map/pallas_call | solution.py:304
  66.3 3.8 %all-to-all-done.1.in_ref = bf16[16,4,56,128]{3,2,1,0:T(8,128)(2,1)S(1)} async-done(((bf16[16,4,56,128]{3,2,1,0:T(8,128)(2,1)}), bf16[16,4,56,128]{3,2,1,0:T(8,128)(2,1)S(1)}, u32[]{:S(2)}, u32[]{:S(2)}) %all-to-all-start.1) | async-done | bytes 917536 | tf_op jit(solution)/shard_map/all_to_all | solution.py:302
  70.1 1.8 %shard_map.58 = f32[27,32,512]{2,1,0:T(8,128)} custom-call(bf16[16,4,56,128]{3,2,1,0:T(8,128)(2,1)S(1)} %all-to-all-done.1.in_ref), custom_call_target="tpu_custom_call" | custom-call | bytes 1048576 | tf_op jit(solution)/shard_map/pallas_call | solution.py:303
  (17 shorter events, 0.2 us)
Async XLA Ops:
  0.6 1.0 %copy-start.2 = (bf16[1,4,16,32,64]{4,3,2,1,0:T(8,128)(2,1)S(1)}, bf16[1,4,16,32,64]{4,3,2,1,0:T(8,128)(2,1)}, u32[]{:S(2)}) copy-start(bf16[1,4,16,32,64]{4,3,2,1,0:T(8,128)(2,1)} %param.4) | copy-start | bytes 786436
  1.8 6.0 %collective-permute-start = (bf16[4,256,128]{2,1,0:T(8,128)(2,1)S(1)}, bf16[4,256,128]{2,1,0:T(8,128)(2,1)S(1)}, u32[]{:S(2)}, u32[]{:S(2)}) collective-permute-start(bf16[4,256,128]{2,1,0:T(8,128)(2,1)S(1)} %get-tuple-element.16.panel_ref), channel_id=1, source_target_pairs={{0,1},{1,0},{2,3},{3,2},{4,5},{5,4},{6,7},{7,6},{8,9},{9,8},{10,11... | collective-permute-start | bytes 786440 | tf_op jit(solution)/shard_map/ppermute | solution.py:264
  1.9 12.5 %collective-permute-start.4 = (bf16[4,64,256]{2,1,0:T(8,128)(2,1)}, bf16[4,64,256]{2,1,0:T(8,128)(2,1)S(1)}, u32[]{:S(2)}, u32[]{:S(2)}) collective-permute-start(bf16[4,64,256]{2,1,0:T(8,128)(2,1)} %bitcast.4), channel_id=1, source_target_pairs={{0,2},{1,3},{2,4},{3,5},{4,6},{5,7},{6,0},{7,1},{8,10},{9,11},{10,... | collective-permute-start | bytes 393224 | tf_op jit(solution)/shard_map/ppermute | solution.py:264
  3.6 10.9 %collective-permute-start.5 = (bf16[4,64,256]{2,1,0:T(8,128)(2,1)}, bf16[4,64,256]{2,1,0:T(8,128)(2,1)S(1)}, u32[]{:S(2)}, u32[]{:S(2)}) collective-permute-start(bf16[4,64,256]{2,1,0:T(8,128)(2,1)} %bitcast.5), channel_id=1, source_target_pairs={{0,6},{1,7},{2,0},{3,1},{4,2},{5,3},{6,4},{7,5},{8,14},{9,15},{10,... | collective-permute-start | bytes 393224 | tf_op jit(solution)/shard_map/ppermute | solution.py:264
  5.2 9.2 %collective-permute-start.6 = (bf16[4,64,256]{2,1,0:T(8,128)(2,1)}, bf16[4,64,256]{2,1,0:T(8,128)(2,1)S(1)}, u32[]{:S(2)}, u32[]{:S(2)}) collective-permute-start(bf16[4,64,256]{2,1,0:T(8,128)(2,1)} %bitcast.6), channel_id=1, source_target_pairs={{0,4},{1,5},{2,6},{3,7},{4,0},{5,1},{6,2},{7,3},{8,12},{9,13},{10,... | collective-permute-start | bytes 393224 | tf_op jit(solution)/shard_map/ppermute | solution.py:264
  7.1 7.7 %collective-permute-start.1 = (bf16[256,128]{1,0:T(8,128)(2,1)S(1)}, bf16[256,128]{1,0:T(8,128)(2,1)S(1)}, u32[]{:S(2)}, u32[]{:S(2)}) collective-permute-start(bf16[256,128]{1,0:T(8,128)(2,1)S(1)} %get-tuple-element.18), channel_id=1, source_target_pairs={{8,16},{16,8},{24,32},{32,24},{40,48},{48,40},{9,17},{17,9},{25,33... | collective-permute-start | bytes 196616 | tf_op jit(solution)/shard_map/ppermute | solution.py:273
  7.8 7.4 %collective-permute-start.2 = (bf16[256,128]{1,0:T(8,128)(2,1)S(1)}, bf16[256,128]{1,0:T(8,128)(2,1)S(1)}, u32[]{:S(2)}, u32[]{:S(2)}) collective-permute-start(bf16[256,128]{1,0:T(8,128)(2,1)S(1)} %get-tuple-element.19), channel_id=1, source_target_pairs={{0,8},{8,0},{16,24},{24,16},{32,40},{40,32},{48,56},{56,48},{1,9},... | collective-permute-start | bytes 196616 | tf_op jit(solution)/shard_map/ppermute | solution.py:274
  12.9 0.9 %copy-start.3 = (bf16[1,4,2,32,256]{4,3,2,1,0:T(8,128)(2,1)S(1)}, bf16[1,4,2,32,256]{4,3,2,1,0:T(8,128)(2,1)}, u32[]{:S(2)}) copy-start(bf16[1,4,2,32,256]{4,3,2,1,0:T(8,128)(2,1)} %param.3) | copy-start | bytes 393220
  14.7 2.0 %collective-permute-start.8 = (bf16[3,4,64,128]{3,2,1,0:T(8,128)(2,1)S(1)}, bf16[3,4,64,128]{3,2,1,0:T(8,128)(2,1)S(1)}, u32[]{:S(2)}, u32[]{:S(2)}) collective-permute-start(bf16[3,4,64,128]{3,2,1,0:T(8,128)(2,1)S(1)} %shard_map.53), channel_id=1, source_target_pairs={{0,1},{1,0},{2,3},{3,2},{4,5},{5,4},{6,7},{7,6},{8,9},{9,8},{10,11... | collective-permute-start | bytes 589832 | tf_op jit(solution)/shard_map/ppermute | solution.py:264
  15.2 1.4 %collective-permute-start.3 = (bf16[2,256,128]{2,1,0:T(8,128)(2,1)S(1)}, bf16[2,256,128]{2,1,0:T(8,128)(2,1)S(1)}, u32[]{:S(2)}, u32[]{:S(2)}) collective-permute-start(bf16[2,256,128]{2,1,0:T(8,128)(2,1)S(1)} %shard_map.52.refs_0_.rims_ref), channel_id=1, source_target_pairs={{0,1},{1,0},{2,3},{3,2},{4,5},{5,4},{6,7},{7,6},{8,9},{9,8},{10,11... | collective-permute-start | bytes 393224 | tf_op jit(solution)/shard_map/ppermute | solution.py:264
  15.4 1.3 %collective-permute-start.7 = (bf16[4,64,128]{2,1,0:T(8,128)(2,1)S(1)}, bf16[4,64,128]{2,1,0:T(8,128)(2,1)S(1)}, u32[]{:S(2)}, u32[]{:S(2)}) collective-permute-start(bf16[4,64,128]{2,1,0:T(8,128)(2,1)S(1)} %get-tuple-element.21), channel_id=1, source_target_pairs={{0,1},{1,0},{2,3},{3,2},{4,5},{5,4},{6,7},{7,6},{8,9},{9,8},{10,11... | collective-permute-start | bytes 196616 | tf_op jit(solution)/shard_map/ppermute | solution.py:264
  20.7 0.9 %copy-start.1 = (bf16[64,56,128]{2,1,0:T(8,128)(2,1)}, bf16[64,56,128]{2,1,0:T(8,128)(2,1)S(1)}, u32[]{:S(2)}) copy-start(bf16[64,56,128]{2,1,0:T(8,128)(2,1)S(1)} %get-tuple-element.28) | copy-start | bytes 2752516
  21.6 28.2 %all-to-all-start = ((bf16[64,56,128]{2,1,0:T(8,128)(2,1)}), bf16[64,56,128]{2,1,0:T(8,128)(2,1)S(1)}, u32[]{:S(2)}, u32[]{:S(2)}) async-start(bf16[64,56,128]{2,1,0:T(8,128)(2,1)} %copy-done.1), calls=%async_computation | async-start | bytes 1835008 | tf_op jit(solution)/shard_map/all_to_all | solution.py:292
  32.0 3.0 %copy-start = (bf16[27,256,512]{2,1,0:T(8,128)(2,1)S(1)}, bf16[27,256,512]{2,1,0:T(8,128)(2,1)}, u32[]{:S(2)}) copy-start(bf16[27,256,512]{2,1,0:T(8,128)(2,1)} %weight_ref.1) | copy-start | bytes 21233668
  39.7 0.6 copy-start.4
  49.8 5.4 %copy-start.5 = (bf16[528,128]{1,0:T(8,128)(2,1)S(1)}, bf16[528,128]{1,0:T(8,128)(2,1)}, u32[]{:S(2)}) copy-start(bf16[528,128]{1,0:T(8,128)(2,1)} %copy-done.4) | copy-start | bytes 405508
  51.6 18.5 %all-to-all-start.1 = ((bf16[16,4,56,128]{3,2,1,0:T(8,128)(2,1)}), bf16[16,4,56,128]{3,2,1,0:T(8,128)(2,1)S(1)}, u32[]{:S(2)}, u32[]{:S(2)}) async-start(bf16[16,4,56,128]{3,2,1,0:T(8,128)(2,1)} %shard_map.57), calls=%async_computation.1 | async-start | bytes 1835008 | tf_op jit(solution)/shard_map/all_to_all | solution.py:302
  55.2 5.8 %collective-permute-start.10 = (bf16[528,128]{1,0:T(8,128)(2,1)S(1)}, bf16[528,128]{1,0:T(8,128)(2,1)S(1)}, u32[]{:S(2)}, u32[]{:S(2)}) collective-permute-start(bf16[528,128]{1,0:T(8,128)(2,1)S(1)} %copy-done.5), channel_id=1, source_target_pairs={{0,6},{1,7},{2,0},{3,1},{4,2},{5,3},{6,4},{7,5},{8,14},{9,15},{10,... | collective-permute-start | bytes 405512 | tf_op jit(solution)/shard_map/ppermute | solution.py:264
  56.2 7.3 %collective-permute-start.11 = (bf16[528,128]{1,0:T(8,128)(2,1)S(1)}, bf16[528,128]{1,0:T(8,128)(2,1)S(1)}, u32[]{:S(2)}, u32[]{:S(2)}) collective-permute-start(bf16[528,128]{1,0:T(8,128)(2,1)S(1)} %get-tuple-element.27), channel_id=1, source_target_pairs={{0,4},{1,5},{2,6},{3,7},{4,0},{5,1},{6,2},{7,3},{8,12},{9,13},{10,... | collective-permute-start | bytes 405512 | tf_op jit(solution)/shard_map/ppermute | solution.py:264
  57.9 6.9 %collective-permute-start.9 = (bf16[528,128]{1,0:T(8,128)(2,1)S(1)}, bf16[528,128]{1,0:T(8,128)(2,1)S(1)}, u32[]{:S(2)}, u32[]{:S(2)}) collective-permute-start(bf16[528,128]{1,0:T(8,128)(2,1)S(1)} %get-tuple-element.25), channel_id=1, source_target_pairs={{0,2},{1,3},{2,4},{3,5},{4,6},{5,7},{6,0},{7,1},{8,10},{9,11},{10,... | collective-permute-start | bytes 405512 | tf_op jit(solution)/shard_map/ppermute | solution.py:264

commit v5 on v4

--- a/solution.py
+++ b/solution.py
@@ -102,9 +102,12 @@
     write_plane(rims[0][1], rims[1][1], edge_ref.at[1], 128)
 
 
+def window(bc):
+    return slice(64 - 32 * (bc // 3), 576 - 32 * (bc // 3))
+
+
 def patches(inner_ref, edge_ref, t, i, bc):
-    window = slice(64 - 32 * (bc // 3), 576 - 32 * (bc // 3))
-    return inner_ref[bc % 3, window, 128:384] if t != i else edge_ref[t, bc % 3, window, :]
+    return inner_ref[bc % 3, window(bc), 128:384] if t != i else edge_ref[t, bc % 3, window(bc), :]
 
 
 def split_channels(core, block, own):
@@ -127,10 +130,11 @@
 
 
 def kernel_grad_body(inner_ref, *refs):
-    rims, keep_ref, blocks, own_got_ref, got_ref, out_ref, token_ref, edge_ref, x_ref, xt_ref, sum_ref = (
+    rims, keep_ref, blocks, own_got_ref, got_ref, out_ref, token_ref, rim_ref, x_ref, xt_ref, sum_ref = (
         refs[:2], refs[2], refs[3:6], *refs[6:]
     )
-    write_edges(inner_ref, rims, edge_ref)
+    for i in range(2):
+        write_plane(rims[0][i], rims[1][i], rim_ref.at[i], 0)
     chip, core, _ = place()
     for i in range(8):
         spot = 2 * lax.rem(chip + (0, 3, 1, 2)[i % 4], 4) + (core if i < 4 else 1 - core)
@@ -145,21 +149,35 @@
     for i in range(2):
         xt_ref[128 * i : 128 * (i + 1), :] = x_ref[:, 128 * i : 128 * (i + 1)].T
     most = jnp.zeros((128, 128), F32)
-    for bc in range(9):
-        prod = jnp.concatenate([
-            sum(
-                jnp.dot(
-                    xt_ref[:, 512 * t : 512 * (t + 1)], patches(inner_ref, edge_ref, t, i, bc), preferred_element_type=F32
-                )
-                for t in range(2)
+    low, high = xt_ref.at[:, :512], xt_ref.at[:, 512:]
+    ends = (low.at[:128], high.at[:128], low.at[128:], high.at[128:])
+
+    def multiply(left_ref, right):
+        return jnp.dot(left_ref[...], right, preferred_element_type=F32)
+
+    for start in range(0, 9, 2):
+        taps = range(start, min(start + 2, 9))
+
+        def beside(read):
+            return jnp.concatenate([read(bc % 3, window(bc)) for bc in taps], axis=1)
+
+        up = multiply(ends[1], beside(lambda c, cells: inner_ref[c, cells, 128:256]))
+        up = up + multiply(ends[0], beside(lambda c, cells: rim_ref[0, c, cells, :]))
+        down = multiply(ends[2], beside(lambda c, cells: inner_ref[c, cells, 256:384]))
+        down = down + multiply(ends[3], beside(lambda c, cells: rim_ref[1, c, cells, :]))
+        for i, bc in enumerate(taps):
+            one = slice(128 * i, 128 * i + 128)
+            first = multiply(low, inner_ref[bc % 3, window(bc), 0:256])
+            last = multiply(high, inner_ref[bc % 3, window(bc), 256:512])
+            totals = (
+                (first[:128, 128:] + last[:128, 128:]) + down[:, one],
+                (first[:128, :128] + first[128:, 128:]) + (last[:128, :128] + last[128:, 128:]),
+                (first[128:, :128] + last[128:, :128]) + up[:, one],
             )
-            for i in range(2)
-        ], axis=1)
-        for a in range(3):
-            even, odd = 128 * (2 - a), 128 * (3 - a)
-            total = (prod[:128, even : even + 128] + prod[128:, odd : odd + 128]) * (32768.0**-0.5)
-            sum_ref[9 * a + bc] = total
-            most = jnp.maximum(most, jnp.abs(total))
+            for a in range(3):
+                total = totals[a] * (32768.0**-0.5)
+                sum_ref[9 * a + bc] = total
+                most = jnp.maximum(most, jnp.abs(total))
     exponent = top_exponent(most)
     for k in range(27):
         sum_ref[k] = encode(sum_ref[k], exponent)
@@ -286,7 +304,7 @@
     edges = pltpu.VMEM((2, 3, 576, 256), BF16)
     codes, made = call(
         kernel_grad_body, (struct((64, 56, 128), BF16), token), [VM] * 9,
-        [edges, pltpu.VMEM((1024, 256), BF16), pltpu.VMEM((256, 1024), BF16), pltpu.VMEM((27, 128, 128), F32)],
+        [pltpu.VMEM((2, 3, 576, 128), BF16), pltpu.VMEM((1024, 256), BF16), pltpu.VMEM((256, 1024), BF16), pltpu.VMEM((27, 128, 128), F32)],
         2 * 2304 * 1024 * 512, 12 << 20, 12,
     )(inner, *rims, keep, *near, own_got, got)
     swapped = lax.all_to_all(codes, whole, split_axis=0, concat_axis=0, tiled=True, axis_index_groups=cores)

time: 72.3 us -> 71.8 us (level)
  no operation moved by 1% of the time
where the time goes in v5:
time: 71.8 us; the launch traced here: 71.4 us
  starting transfers between devices  28.3 us (39%)
  waiting for transfers between devices  21.7 us (30%)
  Pallas kernels  14.1 us (20%)
  local copies, waits for them, and re-layouts  6.53 us (9%)
  between operations  0.8 us (1%)
    all_to_all x1, starting transfers between devices, on_device(): lax.all_to_all(codes, whole, split_axis=0, concat_axis=0, tiled=True, axi...  10.2 us
    all_to_all x1, waiting for transfers between devices, on_device(): lax.all_to_all(codes, whole, split_axis=0, concat_axis=0, tiled=True, axi...  9.64 us
    ppermute x10, starting transfers between devices, hop(): lax.ppermute(value, 'chan', [(i, (i // 2 + chips) % 4 * 2 + (i % 2 ^ core...  8.67 us
    ppermute x10, waiting for transfers between devices, hop(): lax.ppermute(value, 'chan', [(i, (i // 2 + chips) % 4 * 2 + (i % 2 ^ core...  7.85 us
    unnamed x12, local copies, waits for them, and re-layouts  6.53 us
    ppermute x1, starting transfers between devices, on_device(): lax.ppermute(high, 'vox', [swap for i in (0, 2, 4, 6) for swap in ((i, i...  5.16 us
    pallas_call x1, Pallas kernels, on_device(): call(data_grad_body, (slab, coded, coded, coded, token), [VM] * 3 + [HBM,...  4.66 us
    all_to_all x1, waiting for transfers between devices, on_device(): lax.all_to_all(shards, ('samp', 'vox'), split_axis=0, concat_axis=0, tile...  3.83 us
  transfers between devices with their start and end apart: 14, of which 8 were waited for; matrix products, arithmetic and copies ran while one was open for 0% of the time, Pallas kernels for 10%

profile of v5, /device:TPU:0, one launch (start us, length us, event | category | flops | bytes accessed | tf_op | source)
XLA Modules:
  0.0 71.4 jit_solution(12794914821393956712)
XLA Ops:
  0.6 1.0 %copy-done.2 = bf16[1,4,16,32,64]{4,3,2,1,0:T(8,128)(2,1)S(1)} copy-done((bf16[1,4,16,32,64]{4,3,2,1,0:T(8,128)(2,1)S(1)}, bf16[1,4,16,32,64]{4,3,2,1,0:T(8,128)(2,1)}, u32[]{:S(2)}) %copy-start.2) | copy-done | bytes 262168
  1.7 0.1 shard_map.50
  1.9 1.6 %collective-permute-start.4 = (bf16[4,64,256]{2,1,0:T(8,128)(2,1)}, bf16[4,64,256]{2,1,0:T(8,128)(2,1)S(1)}, u32[]{:S(2)}, u32[]{:S(2)}) collective-permute-start(bf16[4,64,256]{2,1,0:T(8,128)(2,1)} %bitcast.4), channel_id=1, source_target_pairs={{0,2},{1,3},{2,4},{3,5},{4,6},{5,7},{6,0},{7,1},{8,10},{9,11},{10,... | collective-permute-start | bytes 393224 | tf_op jit(solution)/shard_map/ppermute | solution.py:282
  3.6 1.7 %collective-permute-start.5 = (bf16[4,64,256]{2,1,0:T(8,128)(2,1)}, bf16[4,64,256]{2,1,0:T(8,128)(2,1)S(1)}, u32[]{:S(2)}, u32[]{:S(2)}) collective-permute-start(bf16[4,64,256]{2,1,0:T(8,128)(2,1)} %bitcast.5), channel_id=1, source_target_pairs={{0,6},{1,7},{2,0},{3,1},{4,2},{5,3},{6,4},{7,5},{8,14},{9,15},{10,... | collective-permute-start | bytes 393224 | tf_op jit(solution)/shard_map/ppermute | solution.py:282
  5.2 1.9 %collective-permute-start.6 = (bf16[4,64,256]{2,1,0:T(8,128)(2,1)}, bf16[4,64,256]{2,1,0:T(8,128)(2,1)S(1)}, u32[]{:S(2)}, u32[]{:S(2)}) collective-permute-start(bf16[4,64,256]{2,1,0:T(8,128)(2,1)} %bitcast.6), channel_id=1, source_target_pairs={{0,4},{1,5},{2,6},{3,7},{4,0},{5,1},{6,2},{7,3},{8,12},{9,13},{10,... | collective-permute-start | bytes 393224 | tf_op jit(solution)/shard_map/ppermute | solution.py:282
  7.1 0.7 collective-permute-start.1
  7.8 5.2 %collective-permute-start.2 = (bf16[256,128]{1,0:T(8,128)(2,1)S(1)}, bf16[256,128]{1,0:T(8,128)(2,1)S(1)}, u32[]{:S(2)}, u32[]{:S(2)}) collective-permute-start(bf16[256,128]{1,0:T(8,128)(2,1)S(1)} %get-tuple-element.19), channel_id=1, source_target_pairs={{0,8},{8,0},{16,24},{24,16},{32,40},{40,32},{48,56},{56,48},{1,9},... | collective-permute-start | bytes 196616 | tf_op jit(solution)/shard_map/ppermute | solution.py:292
  13.0 0.9 %copy-done.3 = bf16[1,4,2,32,256]{4,3,2,1,0:T(8,128)(2,1)S(1)} copy-done((bf16[1,4,2,32,256]{4,3,2,1,0:T(8,128)(2,1)S(1)}, bf16[1,4,2,32,256]{4,3,2,1,0:T(8,128)(2,1)}, u32[]{:S(2)}) %copy-start.3) | copy-done | bytes 131096
  13.9 0.6 shard_map.51
  14.5 0.3 shard_map.53
  14.8 0.4 collective-permute-done.2.second_ref
  15.2 0.2 collective-permute-start.3
  15.4 0.4 collective-permute-start.7
  15.8 0.8 %collective-permute-done.3.refs_1_.rims_other_ref = bf16[2,256,128]{2,1,0:T(8,128)(2,1)S(1)} collective-permute-done((bf16[2,256,128]{2,1,0:T(8,128)(2,1)S(1)}, bf16[2,256,128]{2,1,0:T(8,128)(2,1)S(1)}, u32[]{:S(2)}, u32[]{:S(2)}) %collective-permute-start.3) | collective-permute-done | bytes 131104 | tf_op jit(solution)/shard_map/ppermute | solution.py:282
  16.7 0.1 collective-permute-done.7.refs_6_
  16.8 3.4 %shard_map.54 = (bf16[64,56,128]{2,1,0:T(8,128)(2,1)S(1)}, f32[8,128]{1,0:T(8,128)S(1)}) custom-call(bf16[3,576,512]{2,1,0:T(8,128)(2,1)S(1)} %get-tuple-element.17.inner_ref, bf16[2,256,128]{2,1,0:T(8,128)(2,1)S(1)} %shard_map.52.refs_0_.rims_ref, bf16[2,256,128]{2,1,0:T(8,128)(2,1)S(1)} %collective-permute-done.3.refs_1_.rims_other_ref, ...), custom_call_target="tpu_custom_call" | custom-call | flops 2415919104 | bytes 12582912 | tf_op jit(solution)/shard_map/pallas_call | solution.py:305
  20.2 0.9 %copy-done.1 = bf16[64,56,128]{2,1,0:T(8,128)(2,1)} copy-done((bf16[64,56,128]{2,1,0:T(8,128)(2,1)}, bf16[64,56,128]{2,1,0:T(8,128)(2,1)S(1)}, u32[]{:S(2)}) %copy-start.1) | copy-done | bytes 917528
  21.1 10.2 %all-to-all-start = ((bf16[64,56,128]{2,1,0:T(8,128)(2,1)}), bf16[64,56,128]{2,1,0:T(8,128)(2,1)S(1)}, u32[]{:S(2)}, u32[]{:S(2)}) async-start(bf16[64,56,128]{2,1,0:T(8,128)(2,1)} %copy-done.1), calls=%async_computation | async-start | bytes 1835008 | tf_op jit(solution)/shard_map/all_to_all | solution.py:310
  31.3 3.0 %copy-done = bf16[27,256,512]{2,1,0:T(8,128)(2,1)S(1)} copy-done((bf16[27,256,512]{2,1,0:T(8,128)(2,1)S(1)}, bf16[27,256,512]{2,1,0:T(8,128)(2,1)}, u32[]{:S(2)}) %copy-start) | copy-done | bytes 7077912
  34.3 4.7 %shard_map.55 = (f32[512,128]{1,0:T(8,128)S(1)}, bf16[528,128]{1,0:T(8,128)(2,1)S(1)}, bf16[528,128]{1,0:T(8,128)(2,1)S(1)}, bf16[528,128]{1,0:T(8,128)(2,1)S(1)}, f32[8,128]{1,0:T(8,128)S(1)}) custom-call(bf16[3,576,512]{2,1,0:T(8,128)(2,1)S(1)} %get-tuple-element.17.inner_ref, bf16[2,256,128]{2,1,0:T(8,128)(2,1)S(1)} %shard_map.52.refs_0_.rims_ref, ...), custom_call_target="tpu_custom_call" | custom-call | flops 2415919104 | bytes 12582912 | tf_op jit(solution)/shard_map/pallas_call | solution.py:312
  39.0 0.6 copy-done.4
  39.6 9.6 %all-to-all-done.in_ref = bf16[64,56,128]{2,1,0:T(8,128)(2,1)S(1)} async-done(((bf16[64,56,128]{2,1,0:T(8,128)(2,1)}), bf16[64,56,128]{2,1,0:T(8,128)(2,1)S(1)}, u32[]{:S(2)}, u32[]{:S(2)}) %all-to-all-start) | async-done | bytes 917536 | tf_op jit(solution)/shard_map/all_to_all | solution.py:310
  49.3 1.8 %shard_map.57 = bf16[16,4,56,128]{3,2,1,0:T(8,128)(2,1)} custom-call(bf16[64,56,128]{2,1,0:T(8,128)(2,1)S(1)} %all-to-all-done.in_ref, f32[8,128]{1,0:T(8,128)S(1)} %get-tuple-element.29._), custom_call_target="tpu_custom_call" | custom-call | bytes 1048576 | tf_op jit(solution)/shard_map/pallas_call | solution.py:317
  51.0 3.6 %all-to-all-start.1 = ((bf16[16,4,56,128]{3,2,1,0:T(8,128)(2,1)}), bf16[16,4,56,128]{3,2,1,0:T(8,128)(2,1)S(1)}, u32[]{:S(2)}, u32[]{:S(2)}) async-start(bf16[16,4,56,128]{3,2,1,0:T(8,128)(2,1)} %shard_map.57), calls=%async_computation.1 | async-start | bytes 1835008 | tf_op jit(solution)/shard_map/all_to_all | solution.py:320
  54.7 1.0 %collective-permute-start.10 = (bf16[528,128]{1,0:T(8,128)(2,1)S(1)}, bf16[528,128]{1,0:T(8,128)(2,1)S(1)}, u32[]{:S(2)}, u32[]{:S(2)}) collective-permute-start(bf16[528,128]{1,0:T(8,128)(2,1)S(1)} %copy-done.5), channel_id=1, source_target_pairs={{0,6},{1,7},{2,0},{3,1},{4,2},{5,3},{6,4},{7,5},{8,14},{9,15},{10,... | collective-permute-start | bytes 405512 | tf_op jit(solution)/shard_map/ppermute | solution.py:282
  55.7 1.7 %collective-permute-start.11 = (bf16[528,128]{1,0:T(8,128)(2,1)S(1)}, bf16[528,128]{1,0:T(8,128)(2,1)S(1)}, u32[]{:S(2)}, u32[]{:S(2)}) collective-permute-start(bf16[528,128]{1,0:T(8,128)(2,1)S(1)} %get-tuple-element.27), channel_id=1, source_target_pairs={{0,4},{1,5},{2,6},{3,7},{4,0},{5,1},{6,2},{7,3},{8,12},{9,13},{10,... | collective-permute-start | bytes 405512 | tf_op jit(solution)/shard_map/ppermute | solution.py:282
  57.4 3.1 %collective-permute-done.10.refs_1_ = bf16[528,128]{1,0:T(8,128)(2,1)S(1)} collective-permute-done((bf16[528,128]{1,0:T(8,128)(2,1)S(1)}, bf16[528,128]{1,0:T(8,128)(2,1)S(1)}, u32[]{:S(2)}, u32[]{:S(2)}) %collective-permute-start.10) | collective-permute-done | bytes 135200 | tf_op jit(solution)/shard_map/ppermute | solution.py:282
  60.5 2.4 %collective-permute-done.11.refs_2_ = bf16[528,128]{1,0:T(8,128)(2,1)S(1)} collective-permute-done((bf16[528,128]{1,0:T(8,128)(2,1)S(1)}, bf16[528,128]{1,0:T(8,128)(2,1)S(1)}, u32[]{:S(2)}, u32[]{:S(2)}) %collective-permute-start.11) | collective-permute-done | bytes 135200 | tf_op jit(solution)/shard_map/ppermute | solution.py:282
  62.9 1.4 %collective-permute-done.9.refs_0_ = bf16[528,128]{1,0:T(8,128)(2,1)S(1)} collective-permute-done((bf16[528,128]{1,0:T(8,128)(2,1)S(1)}, bf16[528,128]{1,0:T(8,128)(2,1)S(1)}, u32[]{:S(2)}, u32[]{:S(2)}) %collective-permute-start.9) | collective-permute-done | bytes 135200 | tf_op jit(solution)/shard_map/ppermute | solution.py:282
  64.3 1.4 %shard_map.56 = f32[4,512,32]{2,1,0:T(8,128)} custom-call(f32[512,128]{1,0:T(8,128)S(1)} %get-tuple-element.24.own_ref, bf16[528,128]{1,0:T(8,128)(2,1)S(1)} %collective-permute-done.9.refs_0_, bf16[528,128]{1,0:T(8,128)(2,1)S(1)} %collective-permute-done.10.refs_1_, bf16[528,128]{1,0:T(8,128)(2,1)S(1)} %collective-permute-done.11.refs_2_), custom_call_target="tpu_custom_call" | custom-call | bytes 1048576 | tf_op jit(solution)/shard_map/pallas_call | solution.py:322
  65.8 3.8 %all-to-all-done.1.in_ref = bf16[16,4,56,128]{3,2,1,0:T(8,128)(2,1)S(1)} async-done(((bf16[16,4,56,128]{3,2,1,0:T(8,128)(2,1)}), bf16[16,4,56,128]{3,2,1,0:T(8,128)(2,1)S(1)}, u32[]{:S(2)}, u32[]{:S(2)}) %all-to-all-start.1) | async-done | bytes 917536 | tf_op jit(solution)/shard_map/all_to_all | solution.py:320
  69.6 1.8 %shard_map.58 = f32[27,32,512]{2,1,0:T(8,128)} custom-call(bf16[16,4,56,128]{3,2,1,0:T(8,128)(2,1)S(1)} %all-to-all-done.1.in_ref), custom_call_target="tpu_custom_call" | custom-call | bytes 1048576 | tf_op jit(solution)/shard_map/pallas_call | solution.py:321
  (17 shorter events, 0.2 us)
Async XLA Ops:
  0.6 1.0 %copy-start.2 = (bf16[1,4,16,32,64]{4,3,2,1,0:T(8,128)(2,1)S(1)}, bf16[1,4,16,32,64]{4,3,2,1,0:T(8,128)(2,1)}, u32[]{:S(2)}) copy-start(bf16[1,4,16,32,64]{4,3,2,1,0:T(8,128)(2,1)} %param.4) | copy-start | bytes 786436
  1.8 6.0 %collective-permute-start = (bf16[4,256,128]{2,1,0:T(8,128)(2,1)S(1)}, bf16[4,256,128]{2,1,0:T(8,128)(2,1)S(1)}, u32[]{:S(2)}, u32[]{:S(2)}) collective-permute-start(bf16[4,256,128]{2,1,0:T(8,128)(2,1)S(1)} %get-tuple-element.16.panel_ref), channel_id=1, source_target_pairs={{0,1},{1,0},{2,3},{3,2},{4,5},{5,4},{6,7},{7,6},{8,9},{9,8},{10,11... | collective-permute-start | bytes 786440 | tf_op jit(solution)/shard_map/ppermute | solution.py:282
  1.9 12.5 %collective-permute-start.4 = (bf16[4,64,256]{2,1,0:T(8,128)(2,1)}, bf16[4,64,256]{2,1,0:T(8,128)(2,1)S(1)}, u32[]{:S(2)}, u32[]{:S(2)}) collective-permute-start(bf16[4,64,256]{2,1,0:T(8,128)(2,1)} %bitcast.4), channel_id=1, source_target_pairs={{0,2},{1,3},{2,4},{3,5},{4,6},{5,7},{6,0},{7,1},{8,10},{9,11},{10,... | collective-permute-start | bytes 393224 | tf_op jit(solution)/shard_map/ppermute | solution.py:282
  3.6 10.9 %collective-permute-start.5 = (bf16[4,64,256]{2,1,0:T(8,128)(2,1)}, bf16[4,64,256]{2,1,0:T(8,128)(2,1)S(1)}, u32[]{:S(2)}, u32[]{:S(2)}) collective-permute-start(bf16[4,64,256]{2,1,0:T(8,128)(2,1)} %bitcast.5), channel_id=1, source_target_pairs={{0,6},{1,7},{2,0},{3,1},{4,2},{5,3},{6,4},{7,5},{8,14},{9,15},{10,... | collective-permute-start | bytes 393224 | tf_op jit(solution)/shard_map/ppermute | solution.py:282
  5.2 9.2 %collective-permute-start.6 = (bf16[4,64,256]{2,1,0:T(8,128)(2,1)}, bf16[4,64,256]{2,1,0:T(8,128)(2,1)S(1)}, u32[]{:S(2)}, u32[]{:S(2)}) collective-permute-start(bf16[4,64,256]{2,1,0:T(8,128)(2,1)} %bitcast.6), channel_id=1, source_target_pairs={{0,4},{1,5},{2,6},{3,7},{4,0},{5,1},{6,2},{7,3},{8,12},{9,13},{10,... | collective-permute-start | bytes 393224 | tf_op jit(solution)/shard_map/ppermute | solution.py:282
  7.1 7.7 %collective-permute-start.1 = (bf16[256,128]{1,0:T(8,128)(2,1)S(1)}, bf16[256,128]{1,0:T(8,128)(2,1)S(1)}, u32[]{:S(2)}, u32[]{:S(2)}) collective-permute-start(bf16[256,128]{1,0:T(8,128)(2,1)S(1)} %get-tuple-element.18), channel_id=1, source_target_pairs={{8,16},{16,8},{24,32},{32,24},{40,48},{48,40},{9,17},{17,9},{25,33... | collective-permute-start | bytes 196616 | tf_op jit(solution)/shard_map/ppermute | solution.py:291
  7.8 7.4 %collective-permute-start.2 = (bf16[256,128]{1,0:T(8,128)(2,1)S(1)}, bf16[256,128]{1,0:T(8,128)(2,1)S(1)}, u32[]{:S(2)}, u32[]{:S(2)}) collective-permute-start(bf16[256,128]{1,0:T(8,128)(2,1)S(1)} %get-tuple-element.19), channel_id=1, source_target_pairs={{0,8},{8,0},{16,24},{24,16},{32,40},{40,32},{48,56},{56,48},{1,9},... | collective-permute-start | bytes 196616 | tf_op jit(solution)/shard_map/ppermute | solution.py:292
  12.9 0.9 %copy-start.3 = (bf16[1,4,2,32,256]{4,3,2,1,0:T(8,128)(2,1)S(1)}, bf16[1,4,2,32,256]{4,3,2,1,0:T(8,128)(2,1)}, u32[]{:S(2)}) copy-start(bf16[1,4,2,32,256]{4,3,2,1,0:T(8,128)(2,1)} %param.3) | copy-start | bytes 393220
  14.7 2.0 %collective-permute-start.8 = (bf16[3,4,64,128]{3,2,1,0:T(8,128)(2,1)S(1)}, bf16[3,4,64,128]{3,2,1,0:T(8,128)(2,1)S(1)}, u32[]{:S(2)}, u32[]{:S(2)}) collective-permute-start(bf16[3,4,64,128]{3,2,1,0:T(8,128)(2,1)S(1)} %shard_map.53), channel_id=1, source_target_pairs={{0,1},{1,0},{2,3},{3,2},{4,5},{5,4},{6,7},{7,6},{8,9},{9,8},{10,11... | collective-permute-start | bytes 589832 | tf_op jit(solution)/shard_map/ppermute | solution.py:282
  15.2 1.4 %collective-permute-start.3 = (bf16[2,256,128]{2,1,0:T(8,128)(2,1)S(1)}, bf16[2,256,128]{2,1,0:T(8,128)(2,1)S(1)}, u32[]{:S(2)}, u32[]{:S(2)}) collective-permute-start(bf16[2,256,128]{2,1,0:T(8,128)(2,1)S(1)} %shard_map.52.refs_0_.rims_ref), channel_id=1, source_target_pairs={{0,1},{1,0},{2,3},{3,2},{4,5},{5,4},{6,7},{7,6},{8,9},{9,8},{10,11... | collective-permute-start | bytes 393224 | tf_op jit(solution)/shard_map/ppermute | solution.py:282
  15.4 1.3 %collective-permute-start.7 = (bf16[4,64,128]{2,1,0:T(8,128)(2,1)S(1)}, bf16[4,64,128]{2,1,0:T(8,128)(2,1)S(1)}, u32[]{:S(2)}, u32[]{:S(2)}) collective-permute-start(bf16[4,64,128]{2,1,0:T(8,128)(2,1)S(1)} %get-tuple-element.21), channel_id=1, source_target_pairs={{0,1},{1,0},{2,3},{3,2},{4,5},{5,4},{6,7},{7,6},{8,9},{9,8},{10,11... | collective-permute-start | bytes 196616 | tf_op jit(solution)/shard_map/ppermute | solution.py:282
  20.2 0.9 %copy-start.1 = (bf16[64,56,128]{2,1,0:T(8,128)(2,1)}, bf16[64,56,128]{2,1,0:T(8,128)(2,1)S(1)}, u32[]{:S(2)}) copy-start(bf16[64,56,128]{2,1,0:T(8,128)(2,1)S(1)} %get-tuple-element.28) | copy-start | bytes 2752516
  21.1 28.2 %all-to-all-start = ((bf16[64,56,128]{2,1,0:T(8,128)(2,1)}), bf16[64,56,128]{2,1,0:T(8,128)(2,1)S(1)}, u32[]{:S(2)}, u32[]{:S(2)}) async-start(bf16[64,56,128]{2,1,0:T(8,128)(2,1)} %copy-done.1), calls=%async_computation | async-start | bytes 1835008 | tf_op jit(solution)/shard_map/all_to_all | solution.py:310
  31.3 3.0 %copy-start = (bf16[27,256,512]{2,1,0:T(8,128)(2,1)S(1)}, bf16[27,256,512]{2,1,0:T(8,128)(2,1)}, u32[]{:S(2)}) copy-start(bf16[27,256,512]{2,1,0:T(8,128)(2,1)} %weight_ref.1) | copy-start | bytes 21233668
  39.0 0.6 copy-start.4
  49.3 5.4 %copy-start.5 = (bf16[528,128]{1,0:T(8,128)(2,1)S(1)}, bf16[528,128]{1,0:T(8,128)(2,1)}, u32[]{:S(2)}) copy-start(bf16[528,128]{1,0:T(8,128)(2,1)} %copy-done.4) | copy-start | bytes 405508
  51.0 18.5 %all-to-all-start.1 = ((bf16[16,4,56,128]{3,2,1,0:T(8,128)(2,1)}), bf16[16,4,56,128]{3,2,1,0:T(8,128)(2,1)S(1)}, u32[]{:S(2)}, u32[]{:S(2)}) async-start(bf16[16,4,56,128]{3,2,1,0:T(8,128)(2,1)} %shard_map.57), calls=%async_computation.1 | async-start | bytes 1835008 | tf_op jit(solution)/shard_map/all_to_all | solution.py:320
  54.7 5.8 %collective-permute-start.10 = (bf16[528,128]{1,0:T(8,128)(2,1)S(1)}, bf16[528,128]{1,0:T(8,128)(2,1)S(1)}, u32[]{:S(2)}, u32[]{:S(2)}) collective-permute-start(bf16[528,128]{1,0:T(8,128)(2,1)S(1)} %copy-done.5), channel_id=1, source_target_pairs={{0,6},{1,7},{2,0},{3,1},{4,2},{5,3},{6,4},{7,5},{8,14},{9,15},{10,... | collective-permute-start | bytes 405512 | tf_op jit(solution)/shard_map/ppermute | solution.py:282
  55.7 7.3 %collective-permute-start.11 = (bf16[528,128]{1,0:T(8,128)(2,1)S(1)}, bf16[528,128]{1,0:T(8,128)(2,1)S(1)}, u32[]{:S(2)}, u32[]{:S(2)}) collective-permute-start(bf16[528,128]{1,0:T(8,128)(2,1)S(1)} %get-tuple-element.27), channel_id=1, source_target_pairs={{0,4},{1,5},{2,6},{3,7},{4,0},{5,1},{6,2},{7,3},{8,12},{9,13},{10,... | collective-permute-start | bytes 405512 | tf_op jit(solution)/shard_map/ppermute | solution.py:282
  57.4 6.9 %collective-permute-start.9 = (bf16[528,128]{1,0:T(8,128)(2,1)S(1)}, bf16[528,128]{1,0:T(8,128)(2,1)S(1)}, u32[]{:S(2)}, u32[]{:S(2)}) collective-permute-start(bf16[528,128]{1,0:T(8,128)(2,1)S(1)} %get-tuple-element.25), channel_id=1, source_target_pairs={{0,2},{1,3},{2,4},{3,5},{4,6},{5,7},{6,0},{7,1},{8,10},{9,11},{10,... | collective-permute-start | bytes 405512 | tf_op jit(solution)/shard_map/ppermute | solution.py:282

commit v6 on v5

--- a/solution.py
+++ b/solution.py
@@ -18,14 +18,13 @@
     return lax.div(chan, 2), lax.rem(chan, 2), lax.rem(lax.axis_index("vox"), 2)
 
 
-def call(body, outs, ins, scratch=(), flops=0, nbytes=1 << 20, mib=4, aliases=None):
+def call(body, outs, ins, scratch=(), flops=0, nbytes=1 << 20, mib=4, specs=None):
     return pl.pallas_call(
         body,
         out_shape=outs,
         in_specs=ins,
-        out_specs=jax.tree.map(lambda _: VM, outs),
+        out_specs=specs or jax.tree.map(lambda _: VM, outs),
         scratch_shapes=list(scratch),
-        input_output_aliases=aliases or {},
         compiler_params=pltpu.CompilerParams(vmem_limit_bytes=mib << 20),
         cost_estimate=pl.CostEstimate(flops=flops, bytes_accessed=nbytes, transcendentals=0),
     )
@@ -209,20 +208,27 @@
             out_ref[j, k] = code
 
 
-def kernel_out_body(in_ref, out_ref):
+def kernel_out_body(in_ref, out_ref, hold_ref, sems):
+    copies = []
     for jr in range(4):
+        rows = slice(8 * jr, 8 * jr + 8)
         for k in range(4):
-            at = (slice(8 * jr, 8 * jr + 8), slice(128 * k, 128 * (k + 1)))
+            lanes = slice(128 * k, 128 * (k + 1))
             rest = []
             for jt in range(4):
                 code = in_ref[4 * jr + jt, k].astype(F32)
                 value = decode(code, code[54:55])
                 for i in range(6):
-                    out_ref[6 * jt + i, at[0], at[1]] = value[8 * i : 8 * i + 8]
+                    hold_ref[6 * jt + i, rows, lanes] = value[8 * i : 8 * i + 8]
                 rest.append(value[48:54])
             rest = jnp.concatenate(rest, axis=0)
             for i in range(3):
-                out_ref[24 + i, at[0], at[1]] = rest[8 * i : 8 * i + 8]
+                hold_ref[24 + i, rows, lanes] = rest[8 * i : 8 * i + 8]
+        part = pl.ds(8 * jr, 8)
+        copies.append(pltpu.make_async_copy(hold_ref.at[:, part, :], out_ref.at[:, part, :], sems.at[jr]))
+        copies[-1].start()
+    for copy in copies:
+        copy.wait()
 
 
 def data_grad_body(inner_ref, rims_ref, rims_other_ref, weight_ref, _, *refs):
@@ -318,7 +324,10 @@
         shard_sum_body, struct((16, 4, 56, 128), BF16), [VM, VM], [pltpu.VMEM((4, 56, 128), F32)]
     )(swapped, done)
     final = lax.all_to_all(shards, ("samp", "vox"), split_axis=0, concat_axis=0, tiled=True)
-    weight_grad = call(kernel_out_body, struct((27, 32, 512), F32), [VM])(final)
+    weight_grad = call(
+        kernel_out_body, struct((27, 32, 512), F32), [VM],
+        [pltpu.VMEM((27, 32, 512), F32), pltpu.SemaphoreType.DMA((4,))], mib=6, specs=HBM,
+    )(final)
     data_grad = call(data_out_body, struct((4, 512, 32), F32), [VM] * 4)(
         slabs[0], *[hop(slabs[d], d, 0) for d in (1, 3, 2)]
     )

time: 71.8 us -> 71.4 us (level)
  no operation moved by 1% of the time
where the time goes in v6:
time: 71.4 us; the launch traced here: 71 us
  starting transfers between devices  28.3 us (40%)
  waiting for transfers between devices  21.7 us (30%)
  Pallas kernels  13.7 us (19%)
  local copies, waits for them, and re-layouts  6.53 us (9%)
  between operations  0.8 us (1%)
    all_to_all x1, starting transfers between devices, on_device(): lax.all_to_all(codes, whole, split_axis=0, concat_axis=0, tiled=True, axi...  10.2 us
    all_to_all x1, waiting for transfers between devices, on_device(): lax.all_to_all(codes, whole, split_axis=0, concat_axis=0, tiled=True, axi...  9.64 us
    ppermute x10, starting transfers between devices, hop(): lax.ppermute(value, 'chan', [(i, (i // 2 + chips) % 4 * 2 + (i % 2 ^ core...  8.67 us
    ppermute x10, waiting for transfers between devices, hop(): lax.ppermute(value, 'chan', [(i, (i // 2 + chips) % 4 * 2 + (i % 2 ^ core...  7.85 us
    unnamed x12, local copies, waits for them, and re-layouts  6.53 us
    ppermute x1, starting transfers between devices, on_device(): lax.ppermute(high, 'vox', [swap for i in (0, 2, 4, 6) for swap in ((i, i...  5.16 us
    pallas_call x1, Pallas kernels, on_device(): call(data_grad_body, (slab, coded, coded, coded, token), [VM] * 3 + [HBM,...  4.66 us
    all_to_all x1, waiting for transfers between devices, on_device(): lax.all_to_all(shards, ('samp', 'vox'), split_axis=0, concat_axis=0, tile...  3.83 us
  transfers between devices with their start and end apart: 14, of which 8 were waited for; matrix products, arithmetic and copies ran while one was open for 0% of the time, Pallas kernels for 10%

profile of v6, /device:TPU:0, one launch (start us, length us, event | category | flops | bytes accessed | tf_op | source)
XLA Modules:
  0.0 71.0 jit_solution(489732468382252740)
XLA Ops:
  0.6 1.0 %copy-done.2 = bf16[1,4,16,32,64]{4,3,2,1,0:T(8,128)(2,1)S(1)} copy-done((bf16[1,4,16,32,64]{4,3,2,1,0:T(8,128)(2,1)S(1)}, bf16[1,4,16,32,64]{4,3,2,1,0:T(8,128)(2,1)}, u32[]{:S(2)}) %copy-start.2) | copy-done | bytes 262168
  1.7 0.1 shard_map.50
  1.9 1.6 %collective-permute-start.4 = (bf16[4,64,256]{2,1,0:T(8,128)(2,1)}, bf16[4,64,256]{2,1,0:T(8,128)(2,1)S(1)}, u32[]{:S(2)}, u32[]{:S(2)}) collective-permute-start(bf16[4,64,256]{2,1,0:T(8,128)(2,1)} %bitcast.4), channel_id=1, source_target_pairs={{0,2},{1,3},{2,4},{3,5},{4,6},{5,7},{6,0},{7,1},{8,10},{9,11},{10,... | collective-permute-start | bytes 393224 | tf_op jit(solution)/shard_map/ppermute | solution.py:288
  3.6 1.7 %collective-permute-start.5 = (bf16[4,64,256]{2,1,0:T(8,128)(2,1)}, bf16[4,64,256]{2,1,0:T(8,128)(2,1)S(1)}, u32[]{:S(2)}, u32[]{:S(2)}) collective-permute-start(bf16[4,64,256]{2,1,0:T(8,128)(2,1)} %bitcast.5), channel_id=1, source_target_pairs={{0,6},{1,7},{2,0},{3,1},{4,2},{5,3},{6,4},{7,5},{8,14},{9,15},{10,... | collective-permute-start | bytes 393224 | tf_op jit(solution)/shard_map/ppermute | solution.py:288
  5.2 1.9 %collective-permute-start.6 = (bf16[4,64,256]{2,1,0:T(8,128)(2,1)}, bf16[4,64,256]{2,1,0:T(8,128)(2,1)S(1)}, u32[]{:S(2)}, u32[]{:S(2)}) collective-permute-start(bf16[4,64,256]{2,1,0:T(8,128)(2,1)} %bitcast.6), channel_id=1, source_target_pairs={{0,4},{1,5},{2,6},{3,7},{4,0},{5,1},{6,2},{7,3},{8,12},{9,13},{10,... | collective-permute-start | bytes 393224 | tf_op jit(solution)/shard_map/ppermute | solution.py:288
  7.1 0.7 collective-permute-start.1
  7.8 5.2 %collective-permute-start.2 = (bf16[256,128]{1,0:T(8,128)(2,1)S(1)}, bf16[256,128]{1,0:T(8,128)(2,1)S(1)}, u32[]{:S(2)}, u32[]{:S(2)}) collective-permute-start(bf16[256,128]{1,0:T(8,128)(2,1)S(1)} %get-tuple-element.19), channel_id=1, source_target_pairs={{0,8},{8,0},{16,24},{24,16},{32,40},{40,32},{48,56},{56,48},{1,9},... | collective-permute-start | bytes 196616 | tf_op jit(solution)/shard_map/ppermute | solution.py:298
  13.0 0.9 %copy-done.3 = bf16[1,4,2,32,256]{4,3,2,1,0:T(8,128)(2,1)S(1)} copy-done((bf16[1,4,2,32,256]{4,3,2,1,0:T(8,128)(2,1)S(1)}, bf16[1,4,2,32,256]{4,3,2,1,0:T(8,128)(2,1)}, u32[]{:S(2)}) %copy-start.3) | copy-done | bytes 131096
  13.9 0.6 shard_map.51
  14.5 0.3 shard_map.53
  14.8 0.4 collective-permute-done.2.second_ref
  15.2 0.2 collective-permute-start.3
  15.4 0.4 collective-permute-start.7
  15.8 0.8 %collective-permute-done.3.refs_1_.rims_other_ref = bf16[2,256,128]{2,1,0:T(8,128)(2,1)S(1)} collective-permute-done((bf16[2,256,128]{2,1,0:T(8,128)(2,1)S(1)}, bf16[2,256,128]{2,1,0:T(8,128)(2,1)S(1)}, u32[]{:S(2)}, u32[]{:S(2)}) %collective-permute-start.3) | collective-permute-done | bytes 131104 | tf_op jit(solution)/shard_map/ppermute | solution.py:288
  16.7 0.1 collective-permute-done.7.refs_6_
  16.8 3.4 %shard_map.54 = (bf16[64,56,128]{2,1,0:T(8,128)(2,1)S(1)}, f32[8,128]{1,0:T(8,128)S(1)}) custom-call(bf16[3,576,512]{2,1,0:T(8,128)(2,1)S(1)} %get-tuple-element.17.inner_ref, bf16[2,256,128]{2,1,0:T(8,128)(2,1)S(1)} %shard_map.52.refs_0_.rims_ref, bf16[2,256,128]{2,1,0:T(8,128)(2,1)S(1)} %collective-permute-done.3.refs_1_.rims_other_ref, ...), custom_call_target="tpu_custom_call" | custom-call | flops 2415919104 | bytes 12582912 | tf_op jit(solution)/shard_map/pallas_call | solution.py:311
  20.2 0.9 %copy-done.1 = bf16[64,56,128]{2,1,0:T(8,128)(2,1)} copy-done((bf16[64,56,128]{2,1,0:T(8,128)(2,1)}, bf16[64,56,128]{2,1,0:T(8,128)(2,1)S(1)}, u32[]{:S(2)}) %copy-start.1) | copy-done | bytes 917528
  21.1 10.2 %all-to-all-start = ((bf16[64,56,128]{2,1,0:T(8,128)(2,1)}), bf16[64,56,128]{2,1,0:T(8,128)(2,1)S(1)}, u32[]{:S(2)}, u32[]{:S(2)}) async-start(bf16[64,56,128]{2,1,0:T(8,128)(2,1)} %copy-done.1), calls=%async_computation | async-start | bytes 1835008 | tf_op jit(solution)/shard_map/all_to_all | solution.py:316
  31.3 3.0 %copy-done = bf16[27,256,512]{2,1,0:T(8,128)(2,1)S(1)} copy-done((bf16[27,256,512]{2,1,0:T(8,128)(2,1)S(1)}, bf16[27,256,512]{2,1,0:T(8,128)(2,1)}, u32[]{:S(2)}) %copy-start) | copy-done | bytes 7077912
  34.3 4.7 %shard_map.55 = (f32[512,128]{1,0:T(8,128)S(1)}, bf16[528,128]{1,0:T(8,128)(2,1)S(1)}, bf16[528,128]{1,0:T(8,128)(2,1)S(1)}, bf16[528,128]{1,0:T(8,128)(2,1)S(1)}, f32[8,128]{1,0:T(8,128)S(1)}) custom-call(bf16[3,576,512]{2,1,0:T(8,128)(2,1)S(1)} %get-tuple-element.17.inner_ref, bf16[2,256,128]{2,1,0:T(8,128)(2,1)S(1)} %shard_map.52.refs_0_.rims_ref, ...), custom_call_target="tpu_custom_call" | custom-call | flops 2415919104 | bytes 12582912 | tf_op jit(solution)/shard_map/pallas_call | solution.py:318
  39.0 0.6 copy-done.4
  39.6 9.6 %all-to-all-done.in_ref = bf16[64,56,128]{2,1,0:T(8,128)(2,1)S(1)} async-done(((bf16[64,56,128]{2,1,0:T(8,128)(2,1)}), bf16[64,56,128]{2,1,0:T(8,128)(2,1)S(1)}, u32[]{:S(2)}, u32[]{:S(2)}) %all-to-all-start) | async-done | bytes 917536 | tf_op jit(solution)/shard_map/all_to_all | solution.py:316
  49.3 1.8 %shard_map.57 = bf16[16,4,56,128]{3,2,1,0:T(8,128)(2,1)} custom-call(bf16[64,56,128]{2,1,0:T(8,128)(2,1)S(1)} %all-to-all-done.in_ref, f32[8,128]{1,0:T(8,128)S(1)} %get-tuple-element.29._), custom_call_target="tpu_custom_call" | custom-call | bytes 1048576 | tf_op jit(solution)/shard_map/pallas_call | solution.py:323
  51.0 3.6 %all-to-all-start.1 = ((bf16[16,4,56,128]{3,2,1,0:T(8,128)(2,1)}), bf16[16,4,56,128]{3,2,1,0:T(8,128)(2,1)S(1)}, u32[]{:S(2)}, u32[]{:S(2)}) async-start(bf16[16,4,56,128]{3,2,1,0:T(8,128)(2,1)} %shard_map.57), calls=%async_computation.1 | async-start | bytes 1835008 | tf_op jit(solution)/shard_map/all_to_all | solution.py:326
  54.7 1.0 %collective-permute-start.10 = (bf16[528,128]{1,0:T(8,128)(2,1)S(1)}, bf16[528,128]{1,0:T(8,128)(2,1)S(1)}, u32[]{:S(2)}, u32[]{:S(2)}) collective-permute-start(bf16[528,128]{1,0:T(8,128)(2,1)S(1)} %copy-done.5), channel_id=1, source_target_pairs={{0,6},{1,7},{2,0},{3,1},{4,2},{5,3},{6,4},{7,5},{8,14},{9,15},{10,... | collective-permute-start | bytes 405512 | tf_op jit(solution)/shard_map/ppermute | solution.py:288
  55.7 1.7 %collective-permute-start.11 = (bf16[528,128]{1,0:T(8,128)(2,1)S(1)}, bf16[528,128]{1,0:T(8,128)(2,1)S(1)}, u32[]{:S(2)}, u32[]{:S(2)}) collective-permute-start(bf16[528,128]{1,0:T(8,128)(2,1)S(1)} %get-tuple-element.27), channel_id=1, source_target_pairs={{0,4},{1,5},{2,6},{3,7},{4,0},{5,1},{6,2},{7,3},{8,12},{9,13},{10,... | collective-permute-start | bytes 405512 | tf_op jit(solution)/shard_map/ppermute | solution.py:288
  57.4 3.1 %collective-permute-done.10.refs_1_ = bf16[528,128]{1,0:T(8,128)(2,1)S(1)} collective-permute-done((bf16[528,128]{1,0:T(8,128)(2,1)S(1)}, bf16[528,128]{1,0:T(8,128)(2,1)S(1)}, u32[]{:S(2)}, u32[]{:S(2)}) %collective-permute-start.10) | collective-permute-done | bytes 135200 | tf_op jit(solution)/shard_map/ppermute | solution.py:288
  60.5 2.4 %collective-permute-done.11.refs_2_ = bf16[528,128]{1,0:T(8,128)(2,1)S(1)} collective-permute-done((bf16[528,128]{1,0:T(8,128)(2,1)S(1)}, bf16[528,128]{1,0:T(8,128)(2,1)S(1)}, u32[]{:S(2)}, u32[]{:S(2)}) %collective-permute-start.11) | collective-permute-done | bytes 135200 | tf_op jit(solution)/shard_map/ppermute | solution.py:288
  62.9 1.4 %collective-permute-done.9.refs_0_ = bf16[528,128]{1,0:T(8,128)(2,1)S(1)} collective-permute-done((bf16[528,128]{1,0:T(8,128)(2,1)S(1)}, bf16[528,128]{1,0:T(8,128)(2,1)S(1)}, u32[]{:S(2)}, u32[]{:S(2)}) %collective-permute-start.9) | collective-permute-done | bytes 135200 | tf_op jit(solution)/shard_map/ppermute | solution.py:288
  64.3 1.4 %shard_map.56 = f32[4,512,32]{2,1,0:T(8,128)} custom-call(f32[512,128]{1,0:T(8,128)S(1)} %get-tuple-element.24.own_ref, bf16[528,128]{1,0:T(8,128)(2,1)S(1)} %collective-permute-done.9.refs_0_, bf16[528,128]{1,0:T(8,128)(2,1)S(1)} %collective-permute-done.10.refs_1_, bf16[528,128]{1,0:T(8,128)(2,1)S(1)} %collective-permute-done.11.refs_2_), custom_call_target="tpu_custom_call" | custom-call | bytes 1048576 | tf_op jit(solution)/shard_map/pallas_call | solution.py:331
  65.8 3.8 %all-to-all-done.1.in_ref = bf16[16,4,56,128]{3,2,1,0:T(8,128)(2,1)S(1)} async-done(((bf16[16,4,56,128]{3,2,1,0:T(8,128)(2,1)}), bf16[16,4,56,128]{3,2,1,0:T(8,128)(2,1)S(1)}, u32[]{:S(2)}, u32[]{:S(2)}) %all-to-all-start.1) | async-done | bytes 917536 | tf_op jit(solution)/shard_map/all_to_all | solution.py:326
  69.6 1.4 %shard_map.58 = f32[27,32,512]{2,1,0:T(8,128)} custom-call(bf16[16,4,56,128]{3,2,1,0:T(8,128)(2,1)S(1)} %all-to-all-done.1.in_ref), custom_call_target="tpu_custom_call" | custom-call | bytes 1048576 | tf_op jit(solution)/shard_map/pallas_call | solution.py:327
  (17 shorter events, 0.2 us)
Async XLA Ops:
  0.6 1.0 %copy-start.2 = (bf16[1,4,16,32,64]{4,3,2,1,0:T(8,128)(2,1)S(1)}, bf16[1,4,16,32,64]{4,3,2,1,0:T(8,128)(2,1)}, u32[]{:S(2)}) copy-start(bf16[1,4,16,32,64]{4,3,2,1,0:T(8,128)(2,1)} %param.4) | copy-start | bytes 786436
  1.8 6.0 %collective-permute-start = (bf16[4,256,128]{2,1,0:T(8,128)(2,1)S(1)}, bf16[4,256,128]{2,1,0:T(8,128)(2,1)S(1)}, u32[]{:S(2)}, u32[]{:S(2)}) collective-permute-start(bf16[4,256,128]{2,1,0:T(8,128)(2,1)S(1)} %get-tuple-element.16.panel_ref), channel_id=1, source_target_pairs={{0,1},{1,0},{2,3},{3,2},{4,5},{5,4},{6,7},{7,6},{8,9},{9,8},{10,11... | collective-permute-start | bytes 786440 | tf_op jit(solution)/shard_map/ppermute | solution.py:288
  1.9 12.5 %collective-permute-start.4 = (bf16[4,64,256]{2,1,0:T(8,128)(2,1)}, bf16[4,64,256]{2,1,0:T(8,128)(2,1)S(1)}, u32[]{:S(2)}, u32[]{:S(2)}) collective-permute-start(bf16[4,64,256]{2,1,0:T(8,128)(2,1)} %bitcast.4), channel_id=1, source_target_pairs={{0,2},{1,3},{2,4},{3,5},{4,6},{5,7},{6,0},{7,1},{8,10},{9,11},{10,... | collective-permute-start | bytes 393224 | tf_op jit(solution)/shard_map/ppermute | solution.py:288
  3.6 10.9 %collective-permute-start.5 = (bf16[4,64,256]{2,1,0:T(8,128)(2,1)}, bf16[4,64,256]{2,1,0:T(8,128)(2,1)S(1)}, u32[]{:S(2)}, u32[]{:S(2)}) collective-permute-start(bf16[4,64,256]{2,1,0:T(8,128)(2,1)} %bitcast.5), channel_id=1, source_target_pairs={{0,6},{1,7},{2,0},{3,1},{4,2},{5,3},{6,4},{7,5},{8,14},{9,15},{10,... | collective-permute-start | bytes 393224 | tf_op jit(solution)/shard_map/ppermute | solution.py:288
  5.2 9.2 %collective-permute-start.6 = (bf16[4,64,256]{2,1,0:T(8,128)(2,1)}, bf16[4,64,256]{2,1,0:T(8,128)(2,1)S(1)}, u32[]{:S(2)}, u32[]{:S(2)}) collective-permute-start(bf16[4,64,256]{2,1,0:T(8,128)(2,1)} %bitcast.6), channel_id=1, source_target_pairs={{0,4},{1,5},{2,6},{3,7},{4,0},{5,1},{6,2},{7,3},{8,12},{9,13},{10,... | collective-permute-start | bytes 393224 | tf_op jit(solution)/shard_map/ppermute | solution.py:288
  7.1 7.7 %collective-permute-start.1 = (bf16[256,128]{1,0:T(8,128)(2,1)S(1)}, bf16[256,128]{1,0:T(8,128)(2,1)S(1)}, u32[]{:S(2)}, u32[]{:S(2)}) collective-permute-start(bf16[256,128]{1,0:T(8,128)(2,1)S(1)} %get-tuple-element.18), channel_id=1, source_target_pairs={{8,16},{16,8},{24,32},{32,24},{40,48},{48,40},{9,17},{17,9},{25,33... | collective-permute-start | bytes 196616 | tf_op jit(solution)/shard_map/ppermute | solution.py:297
  7.8 7.4 %collective-permute-start.2 = (bf16[256,128]{1,0:T(8,128)(2,1)S(1)}, bf16[256,128]{1,0:T(8,128)(2,1)S(1)}, u32[]{:S(2)}, u32[]{:S(2)}) collective-permute-start(bf16[256,128]{1,0:T(8,128)(2,1)S(1)} %get-tuple-element.19), channel_id=1, source_target_pairs={{0,8},{8,0},{16,24},{24,16},{32,40},{40,32},{48,56},{56,48},{1,9},... | collective-permute-start | bytes 196616 | tf_op jit(solution)/shard_map/ppermute | solution.py:298
  12.9 0.9 %copy-start.3 = (bf16[1,4,2,32,256]{4,3,2,1,0:T(8,128)(2,1)S(1)}, bf16[1,4,2,32,256]{4,3,2,1,0:T(8,128)(2,1)}, u32[]{:S(2)}) copy-start(bf16[1,4,2,32,256]{4,3,2,1,0:T(8,128)(2,1)} %param.3) | copy-start | bytes 393220
  14.7 2.0 %collective-permute-start.8 = (bf16[3,4,64,128]{3,2,1,0:T(8,128)(2,1)S(1)}, bf16[3,4,64,128]{3,2,1,0:T(8,128)(2,1)S(1)}, u32[]{:S(2)}, u32[]{:S(2)}) collective-permute-start(bf16[3,4,64,128]{3,2,1,0:T(8,128)(2,1)S(1)} %shard_map.53), channel_id=1, source_target_pairs={{0,1},{1,0},{2,3},{3,2},{4,5},{5,4},{6,7},{7,6},{8,9},{9,8},{10,11... | collective-permute-start | bytes 589832 | tf_op jit(solution)/shard_map/ppermute | solution.py:288
  15.2 1.4 %collective-permute-start.3 = (bf16[2,256,128]{2,1,0:T(8,128)(2,1)S(1)}, bf16[2,256,128]{2,1,0:T(8,128)(2,1)S(1)}, u32[]{:S(2)}, u32[]{:S(2)}) collective-permute-start(bf16[2,256,128]{2,1,0:T(8,128)(2,1)S(1)} %shard_map.52.refs_0_.rims_ref), channel_id=1, source_target_pairs={{0,1},{1,0},{2,3},{3,2},{4,5},{5,4},{6,7},{7,6},{8,9},{9,8},{10,11... | collective-permute-start | bytes 393224 | tf_op jit(solution)/shard_map/ppermute | solution.py:288
  15.4 1.3 %collective-permute-start.7 = (bf16[4,64,128]{2,1,0:T(8,128)(2,1)S(1)}, bf16[4,64,128]{2,1,0:T(8,128)(2,1)S(1)}, u32[]{:S(2)}, u32[]{:S(2)}) collective-permute-start(bf16[4,64,128]{2,1,0:T(8,128)(2,1)S(1)} %get-tuple-element.21), channel_id=1, source_target_pairs={{0,1},{1,0},{2,3},{3,2},{4,5},{5,4},{6,7},{7,6},{8,9},{9,8},{10,11... | collective-permute-start | bytes 196616 | tf_op jit(solution)/shard_map/ppermute | solution.py:288
  20.2 0.9 %copy-start.1 = (bf16[64,56,128]{2,1,0:T(8,128)(2,1)}, bf16[64,56,128]{2,1,0:T(8,128)(2,1)S(1)}, u32[]{:S(2)}) copy-start(bf16[64,56,128]{2,1,0:T(8,128)(2,1)S(1)} %get-tuple-element.28) | copy-start | bytes 2752516
  21.1 28.2 %all-to-all-start = ((bf16[64,56,128]{2,1,0:T(8,128)(2,1)}), bf16[64,56,128]{2,1,0:T(8,128)(2,1)S(1)}, u32[]{:S(2)}, u32[]{:S(2)}) async-start(bf16[64,56,128]{2,1,0:T(8,128)(2,1)} %copy-done.1), calls=%async_computation | async-start | bytes 1835008 | tf_op jit(solution)/shard_map/all_to_all | solution.py:316
  31.3 3.0 %copy-start = (bf16[27,256,512]{2,1,0:T(8,128)(2,1)S(1)}, bf16[27,256,512]{2,1,0:T(8,128)(2,1)}, u32[]{:S(2)}) copy-start(bf16[27,256,512]{2,1,0:T(8,128)(2,1)} %weight_ref.1) | copy-start | bytes 21233668
  39.0 0.6 copy-start.4
  49.3 5.4 %copy-start.5 = (bf16[528,128]{1,0:T(8,128)(2,1)S(1)}, bf16[528,128]{1,0:T(8,128)(2,1)}, u32[]{:S(2)}) copy-start(bf16[528,128]{1,0:T(8,128)(2,1)} %copy-done.4) | copy-start | bytes 405508
  51.0 18.5 %all-to-all-start.1 = ((bf16[16,4,56,128]{3,2,1,0:T(8,128)(2,1)}), bf16[16,4,56,128]{3,2,1,0:T(8,128)(2,1)S(1)}, u32[]{:S(2)}, u32[]{:S(2)}) async-start(bf16[16,4,56,128]{3,2,1,0:T(8,128)(2,1)} %shard_map.57), calls=%async_computation.1 | async-start | bytes 1835008 | tf_op jit(solution)/shard_map/all_to_all | solution.py:326
  54.7 5.8 %collective-permute-start.10 = (bf16[528,128]{1,0:T(8,128)(2,1)S(1)}, bf16[528,128]{1,0:T(8,128)(2,1)S(1)}, u32[]{:S(2)}, u32[]{:S(2)}) collective-permute-start(bf16[528,128]{1,0:T(8,128)(2,1)S(1)} %copy-done.5), channel_id=1, source_target_pairs={{0,6},{1,7},{2,0},{3,1},{4,2},{5,3},{6,4},{7,5},{8,14},{9,15},{10,... | collective-permute-start | bytes 405512 | tf_op jit(solution)/shard_map/ppermute | solution.py:288
  55.7 7.3 %collective-permute-start.11 = (bf16[528,128]{1,0:T(8,128)(2,1)S(1)}, bf16[528,128]{1,0:T(8,128)(2,1)S(1)}, u32[]{:S(2)}, u32[]{:S(2)}) collective-permute-start(bf16[528,128]{1,0:T(8,128)(2,1)S(1)} %get-tuple-element.27), channel_id=1, source_target_pairs={{0,4},{1,5},{2,6},{3,7},{4,0},{5,1},{6,2},{7,3},{8,12},{9,13},{10,... | collective-permute-start | bytes 405512 | tf_op jit(solution)/shard_map/ppermute | solution.py:288
  57.4 6.9 %collective-permute-start.9 = (bf16[528,128]{1,0:T(8,128)(2,1)S(1)}, bf16[528,128]{1,0:T(8,128)(2,1)S(1)}, u32[]{:S(2)}, u32[]{:S(2)}) collective-permute-start(bf16[528,128]{1,0:T(8,128)(2,1)S(1)} %get-tuple-element.25), channel_id=1, source_target_pairs={{0,2},{1,3},{2,4},{3,5},{4,6},{5,7},{6,0},{7,1},{8,10},{9,11},{10,... | collective-permute-start | bytes 405512 | tf_op jit(solution)/shard_map/ppermute | solution.py:288
